TPU v7x, 32 devices: a whole 2x2x4 slice. The times are simulated.
32 devices in a mesh: groups: 2 (over x), gy: 16 (over z, y, core).
Axes of the slice: x: 2, y: 2, z: 4, core: 2. Of those that a mesh axis runs over, the one named last changes fastest.
Arguments:
- field: bfloat16 [64, 64, 2048], P(None, ('groups', 'gy')), parts along dimension 1, may hold values from -6 to 6
- cotangent: bfloat16 [64, 64, 2048], P(None, ('groups', 'gy')), parts along dimension 1, may hold values from -6 to 6
- banks: bfloat16 [2, 128, 36864], P(None, 'gy'), may hold values from -0.25 to 0.25
- region_map: int32 [64, 2048], P(('groups', 'gy')), parts along dimension 0, may hold values from 0 to 127, as said below
- tile_regions: int32 [512, 2], P(('groups', 'gy')), parts along dimension 0, may hold values from 0 to 127, as said below
- bank_slot: int32 [256], P('groups'), parts along dimension 0, may hold values from 0 to 127, as said below
Outputs:
- refined: bfloat16 [64, 64, 2048], P(None, ('groups', 'gy')), parts along dimension 1
- input_grad: bfloat16 [64, 64, 2048], P(None, ('groups', 'gy')), parts along dimension 1
- grad_banks: float32 [4, 128, 36864], P('groups', 'gy'), parts along dimension 0
There are 2 independent parts, one for each index of `groups`. A program takes and returns all parts, laid end to end along the dimension named above; an argument that names none is the same for every part. Nothing has to cross between parts.
Inputs may be any that keep to these rules, and one draw needn't show every extreme that they name: `region_map`: the region of every cell is one of the two regions that tile_regions lists for its tile. `tile_regions`: the two regions of a tile differ; the 32 regions listed for the tiles of one group of 2 rows are distinct, at most 2 of them has bank rows in one aligned block of 8 rows of banks, and some block holds exactly 2 of them. `bank_slot`: A permutation.
All inputs are finite; a program needn't handle non-finite values.
Results may differ from a plain program's by a relative error of at most 0.0054.
Values may be sent and summed in bfloat16 or wider, within the bound.
No kernel may reach another device: no remote copies, remote signals or barrier semaphores. Data moves between devices by JAX's collectives and lax.ppermute only.
A program may use at most 128 MiB of HBM per device.

v0:
```python
import functools

import jax
import jax.numpy as jnp
from jax import lax
from jax.experimental import pallas as pl
from jax.experimental.pallas import tpu as pltpu
from jax.sharding import PartitionSpec as P

grad_unscale = 0.03125
F32 = jnp.float32
BF16 = jnp.bfloat16
LANES = 128
VMEM = pl.BlockSpec(memory_space=pltpu.VMEM)
SMEM = pl.BlockSpec(memory_space=pltpu.SMEM)
HBM = pl.BlockSpec(memory_space=pl.ANY)


def params(mib):
    return pltpu.CompilerParams(vmem_limit_bytes=mib * 2**20)


def cost(flops, moved):
    return pl.CostEstimate(flops=flops, bytes_accessed=moved, transcendentals=0)


def swap_halves(tile):
    return pltpu.roll(tile, LANES // 2, 1)


def low_half(tile):
    return lax.broadcasted_iota(jnp.int32, tile.shape, 1) < LANES // 2


def select_kernel(per_dev, rows, requested, banks, out, natural, travel, wire, sems):
    for chunk in range(rows):
        tile = banks[0, :, chunk * LANES : (chunk + 1) * LANES].astype(F32)
        natural[pl.ds(chunk, per_dev, stride=rows), :] = tile

    @pl.loop(0, per_dev)
    def _(row):
        base = row * rows

        def blend(first, second, start, count):
            even = jnp.where(low_half(first), first, swap_halves(second))
            odd = jnp.where(low_half(first), swap_halves(first), second)
            travel[pl.ds(start, count, stride=2), :] = even
            travel[pl.ds(start + 1, count, stride=2), :] = odd

        for pair in range(4):
            blend(
                natural[pl.ds(base + 64 * pair, 32), :],
                natural[pl.ds(base + 64 * pair + 32, 32), :],
                64 * pair,
                32,
            )
        blend(natural[pl.ds(base + 256, 16), :], natural[pl.ds(base + 272, 16), :], 256, 16)
        wire[row] = travel[...].astype(BF16)

    places = out.shape[0]

    def copy(place):
        source = wire.at[jnp.maximum(requested[place], 0)]
        return pltpu.make_async_copy(source, out.at[place], sems.at[place])

    for place in range(places):
        copy(place).start()
    for place in range(places):
        copy(place).wait()


def select(requested, banks, layer):
    layers, per_dev, width = banks.shape
    rows = width // LANES
    places = requested.shape[0]
    return pl.pallas_call(
        functools.partial(select_kernel, per_dev, rows),
        grid=(1,),
        out_shape=jax.ShapeDtypeStruct((places, rows, LANES), BF16),
        in_specs=[SMEM, pl.BlockSpec((1, per_dev, width), lambda step: (layer, 0, 0))],
        out_specs=HBM,
        scratch_shapes=[
            pltpu.VMEM((per_dev * rows, LANES), F32),
            pltpu.VMEM((rows, LANES), F32),
            pltpu.VMEM((per_dev, rows, LANES), BF16),
            pltpu.SemaphoreType.DMA((places,)),
        ],
        compiler_params=params(24),
        cost_estimate=cost(1000000, 2 * (places + per_dev) * width),
        name=f"select_{layer}",
    )(requested, banks)


def total_kernel(per_dev, rows, requested, parts, *rest):
    out, total, natural = rest[-3:]
    total[...] = jnp.zeros_like(total)

    @pl.loop(0, parts.shape[0])
    def _(place):
        row = requested[place]

        @pl.when(row >= 0)
        def _():
            total[pl.ds(pl.multiple_of(row * rows, 8), rows), :] += parts[place].astype(F32)

    @pl.loop(0, per_dev)
    def _(row):
        base = row * rows

        def split(start, count, first, second):
            even = total[pl.ds(base + start, count, stride=2), :] * grad_unscale
            odd = total[pl.ds(base + start + 1, count, stride=2), :] * grad_unscale
            natural[pl.ds(base + first, count), :] = jnp.where(low_half(even), even, swap_halves(odd))
            natural[pl.ds(base + second, count), :] = jnp.where(low_half(even), swap_halves(even), odd)

        for pair in range(4):
            split(64 * pair, 32, 64 * pair, 64 * pair + 32)
        split(256, 16, 256, 272)

    for chunk in range(rows):
        out[0, :, chunk * LANES : (chunk + 1) * LANES] = natural[pl.ds(chunk, per_dev, stride=rows), :]


def total_of(requested, parts, banks, layer, earlier=None):
    layers, per_dev, width = banks.shape
    rows = width // LANES
    places = requested.shape[0]
    args, specs = [requested, parts], [SMEM, pl.BlockSpec(parts.shape, lambda step: (0, 0, 0))]
    if earlier is not None:
        args.append(earlier)
        specs.append(HBM)
    return pl.pallas_call(
        functools.partial(total_kernel, per_dev, rows),
        grid=(1,),
        out_shape=jax.ShapeDtypeStruct((layers, per_dev, width), F32),
        in_specs=specs,
        out_specs=pl.BlockSpec((1, per_dev, width), lambda step: (layer, 0, 0)),
        scratch_shapes=[
            pltpu.VMEM((per_dev * rows, LANES), F32),
            pltpu.VMEM((per_dev * rows, LANES), F32),
        ],
        input_output_aliases={2: 0} if earlier is not None else {},
        compiler_params=params(32),
        cost_estimate=cost(1000000, 2 * places * width + 4 * per_dev * width),
        name=f"total_{layer}",
    )(*args)


def fill_shifts(above, middle, below, shifts):
    tile_rows, channels, columns = middle.shape
    step = 16

    @pl.loop(0, channels // step)
    def _(group):
        start = pl.multiple_of(group * step, step)
        for row in range(tile_rows + 2):
            if row == 0:
                cells = above[pl.ds(start, step), :]
            elif row == tile_rows + 1:
                cells = below[pl.ds(start, step), :]
            else:
                cells = middle[row - 1, pl.ds(start, step), :]
            cells = jnp.maximum(cells.astype(F32), 0.0)
            column = lax.broadcasted_iota(jnp.int32, cells.shape, 1)
            left = jnp.where(column == 0, 0.0, pltpu.roll(cells, 1, 1))
            right = jnp.where(column == columns - 1, 0.0, pltpu.roll(cells, columns - 1, 1))
            shifts[0, row, pl.ds(start, step), :] = left.astype(BF16)
            shifts[1, row, pl.ds(start, step), :] = cells.astype(BF16)
            shifts[2, row, pl.ds(start, step), :] = right.astype(BF16)


def band_slice(band):
    return pl.ds(pl.multiple_of(band * LANES, LANES), LANES)


def unfolded(shifts, band, tile_rows):
    taps = []
    for shift_y in range(3):
        for shift_x in range(3):
            rows = [shifts[shift_x, shift_y + row, :, band_slice(band)] for row in range(tile_rows)]
            taps.append(jnp.concatenate(rows, axis=1))
    return jnp.concatenate(taps, axis=0)


def band_weights(kernels, position, band):
    wide, last = [], []
    for slot in range(2):
        one = kernels.at[position[2 * band + slot]]
        wide.append(jnp.concatenate([one[64 * pair : 64 * pair + 64, :] for pair in range(4)], axis=1))
        tail = one[256:288, :]
        last.extend([tail[:, :64], tail[:, 64:]])
    return jnp.concatenate(wide, axis=0), jnp.concatenate(last, axis=0)


def first_mask(regions, listed, band, channels, tile_rows):
    rows = [regions[row : row + 1, band_slice(band)] for row in range(tile_rows)]
    flat = jnp.concatenate(rows, axis=1)
    return jnp.broadcast_to(flat, (channels, flat.shape[1])) == listed[2 * band]


def masked(upstream, mask):
    wide = upstream.astype(F32)
    first = jnp.where(mask, wide, 0.0).astype(BF16)
    second = jnp.where(mask, 0.0, wide).astype(BF16)
    return jnp.concatenate([first, second], axis=0)


def side_by_side(cells, band, tile_rows):
    return jnp.concatenate([cells[row, :, band_slice(band)] for row in range(tile_rows)], axis=1)


def dot(left, right, left_dim, right_dim):
    return lax.dot_general(
        left, right, (((left_dim,), (right_dim,)), ((), ())), preferred_element_type=F32
    )


def conv_kernel(position, listed, regions, above, middle, below, kernels, out, shifts):
    tile_rows, channels, columns = middle.shape
    fill_shifts(above, middle, below, shifts)

    @pl.loop(0, columns // LANES)
    def _(band):
        cells = unfolded(shifts, band, tile_rows)
        wide, last = band_weights(kernels, position, band)
        both = dot(wide, cells[:512], 1, 0) + dot(last, cells[512:], 1, 0)
        mask = first_mask(regions, listed, band, channels, tile_rows)
        mixed = jnp.where(mask, both[:channels], both[channels:])
        for row in range(tile_rows):
            here = mixed[:, row * LANES : (row + 1) * LANES]
            here = here + middle[row, :, band_slice(band)].astype(F32)
            out[row, :, band_slice(band)] = here.astype(BF16)


def conv(position, listed, regions, above, middle, below, kernels, name):
    tile_rows, channels, columns = middle.shape
    return pl.pallas_call(
        conv_kernel,
        out_shape=jax.ShapeDtypeStruct(middle.shape, BF16),
        in_specs=[SMEM, SMEM] + [VMEM] * 5,
        out_specs=VMEM,
        scratch_shapes=[pltpu.VMEM((3, tile_rows + 2, channels, columns), BF16)],
        compiler_params=params(32),
        cost_estimate=cost(4 * 9 * channels * channels * columns * tile_rows, 5000000),
        name=name,
    )(position, listed, regions, above, middle, below, kernels)


def partial_bands(position, listed, regions, upstream, shifts, out):
    tile_rows, channels, columns = upstream.shape

    @pl.loop(0, columns // LANES)
    def _(band):
        cells = unfolded(shifts, band, tile_rows)
        mask = first_mask(regions, listed, band, channels, tile_rows)
        both = masked(side_by_side(upstream, band, tile_rows), mask)
        sums = dot(both, cells, 1, 1).astype(BF16)
        for slot in range(2):
            mine = sums[channels * slot : channels * (slot + 1)]
            there = out.at[position[2 * band + slot]]
            for pair in range(4):
                there[64 * pair : 64 * pair + 64, :] = mine[:, LANES * pair : LANES * (pair + 1)]
            there[256:288, :] = jnp.concatenate([mine[:32, 512:], mine[32:, 512:]], axis=1)


def partial_kernel(position, listed, regions, upstream, above, middle, below, out, shifts):
    fill_shifts(above, middle, below, shifts)
    partial_bands(position, listed, regions, upstream, shifts, out)


def partial_of(position, listed, regions, upstream, above, middle, below, places):
    tile_rows, channels, columns = middle.shape
    rows = 9 * channels * channels // LANES
    return pl.pallas_call(
        partial_kernel,
        out_shape=jax.ShapeDtypeStruct((places, rows, LANES), BF16),
        in_specs=[SMEM, SMEM] + [VMEM] * 5,
        out_specs=VMEM,
        scratch_shapes=[pltpu.VMEM((3, tile_rows + 2, channels, columns), BF16)],
        compiler_params=params(32),
        cost_estimate=cost(4 * 9 * channels * channels * columns * tile_rows, 5000000),
        name="partial_1",
    )(position, listed, regions, upstream, above, middle, below)


def carried_kernel(
    position, listed, regions, cotangent, hidden, inner, from_above, from_below, above, middle, below,
    carried, out, shifts,
):
    tile_rows, channels, columns = middle.shape
    fill_shifts(above, middle, below, shifts)
    step = 16

    @pl.loop(0, channels // step)
    def _(group):
        here = pl.ds(pl.multiple_of(group * step, step), step)
        for row in range(tile_rows):
            back = inner[row, here, :]
            if row == 0:
                back = back + from_above[here, :].astype(F32)
            if row == tile_rows - 1:
                back = back + from_below[here, :].astype(F32)
            keep = hidden[row, here, :].astype(F32) > 0.0
            value = cotangent[row, here, :].astype(F32) + jnp.where(keep, back, 0.0)
            carried[row, here, :] = value.astype(BF16)

    partial_bands(position, listed, regions, carried, shifts, out)


def carried_of(
    position, listed, regions, cotangent, hidden, inner, from_above, from_below, above, middle, below,
    places,
):
    tile_rows, channels, columns = middle.shape
    rows = 9 * channels * channels // LANES
    return pl.pallas_call(
        carried_kernel,
        out_shape=(
            jax.ShapeDtypeStruct(middle.shape, BF16),
            jax.ShapeDtypeStruct((places, rows, LANES), BF16),
        ),
        in_specs=[SMEM, SMEM] + [VMEM] * 9,
        out_specs=(VMEM, VMEM),
        scratch_shapes=[pltpu.VMEM((3, tile_rows + 2, channels, columns), BF16)],
        compiler_params=params(32),
        cost_estimate=cost(4 * 9 * channels * channels * columns * tile_rows, 7000000),
        name="carried_partial_0",
    )(
        position, listed, regions, cotangent, hidden, inner, from_above, from_below, above, middle,
        below,
    )


def spread_kernel(position, listed, regions, upstream, kernels, inner, edges, total):
    tile_rows, channels, columns = upstream.shape
    total[...] = jnp.zeros_like(total)

    @pl.loop(0, columns // LANES)
    def _(band):
        wide, last = band_weights(kernels, position, band)
        mask = first_mask(regions, listed, band, channels, tile_rows)
        both = masked(side_by_side(upstream, band, tile_rows), mask)
        spread = jnp.concatenate([dot(wide, both, 0, 0), dot(last, both, 0, 0)], axis=0)
        lane = lax.broadcasted_iota(jnp.int32, (channels, LANES), 1)
        for target in range(tile_rows + 2):
            moved = []
            for shift_x in range(3):
                value = None
                for row in range(tile_rows):
                    shift_y = target - 1 - row + 1
                    if 0 <= shift_y <= 2:
                        tap = 3 * shift_y + shift_x
                        piece = spread[
                            channels * tap : channels * (tap + 1), LANES * row : LANES * (row + 1)
                        ]
                        value = piece if value is None else value + piece
                moved.append(value)
            left = pltpu.roll(moved[0], LANES - 1, 1)
            right = pltpu.roll(moved[2], 1, 1)
            centre = (
                moved[1]
                + jnp.where(lane == LANES - 1, 0.0, left)
                + jnp.where(lane == 0, 0.0, right)
            )
            total[target, :, band_slice(band)] += jnp.where(lane == LANES - 1, left, 0.0)
            total[target, :, band_slice(band + 1)] += centre
            total[target, :, band_slice(band + 2)] += jnp.where(lane == 0, right, 0.0)

    for row in range(tile_rows):
        inner[row] = total[row + 1, :, LANES : LANES + columns]
    edges[0] = total[0, :, LANES : LANES + columns].astype(BF16)
    edges[1] = total[tile_rows + 1, :, LANES : LANES + columns].astype(BF16)


def spread_of(position, listed, regions, upstream, kernels, name):
    tile_rows, channels, columns = upstream.shape
    return pl.pallas_call(
        spread_kernel,
        out_shape=(
            jax.ShapeDtypeStruct(upstream.shape, F32),
            jax.ShapeDtypeStruct((2, channels, columns), BF16),
        ),
        in_specs=[SMEM, SMEM] + [VMEM] * 3,
        out_specs=(VMEM, VMEM),
        scratch_shapes=[pltpu.VMEM((tile_rows + 2, channels, columns + 2 * LANES), F32)],
        compiler_params=params(32),
        cost_estimate=cost(4 * 9 * channels * channels * columns * tile_rows, 5000000),
        name=name,
    )(position, listed, regions, upstream, kernels)


def from_neighbours(upper, lower):
    count = lax.axis_size("gy")
    above = lax.ppermute(upper, "gy", [(i, i + 1) for i in range(count - 1)])
    below = lax.ppermute(lower, "gy", [(i + 1, i) for i in range(count - 1)])
    return above, below


def body(field, cotangent, banks, region_map, tile_regions, bank_slot):
    col_bands = tile_regions.shape[0]
    devices = lax.axis_size("gy")
    per_dev = banks.shape[1]
    slots_per = max(1, 2 * col_bands // devices)
    places = devices * slots_per
    listed = tile_regions.reshape(-1)
    bank_row = bank_slot[listed]
    holder = bank_row // per_dev
    local_row = bank_row % per_dev
    order = jnp.arange(2 * col_bands, dtype=jnp.int32)
    earlier = (holder[:, None] == holder[None, :]) & (order[None, :] < order[:, None])
    rank_in = jnp.sum(earlier.astype(jnp.int32), axis=-1)
    position = holder * slots_per + rank_in
    hits = position[None, :] == jnp.arange(places, dtype=jnp.int32)[:, None]
    wanted = jnp.max(jnp.where(hits, local_row[None, :], -1), axis=1).reshape(devices, slots_per)
    requested = lax.all_to_all(wanted, "gy", split_axis=0, concat_axis=0, tiled=True).reshape(-1)

    def exchange(value):
        return lax.all_to_all(value, "gy", split_axis=0, concat_axis=0, tiled=True)

    cells = jnp.transpose(field, (1, 0, 2))
    upstream = jnp.transpose(cotangent, (1, 0, 2))
    last = cells.shape[0] - 1

    kernel_zero = exchange(select(requested, banks, 0))
    kernel_one = exchange(select(requested, banks, 1))
    above, below = from_neighbours(cells[last], cells[0])
    where = (position, listed, region_map)
    hidden = conv(*where, above, cells, below, kernel_zero, "conv_0")
    hidden_above, hidden_below = from_neighbours(hidden[last], hidden[0])
    around = (hidden_above, hidden, hidden_below)
    sent_one = exchange(partial_of(*where, upstream, *around, places))
    inner_one, edges_one = spread_of(*where, upstream, kernel_one, "spread_1")
    from_above, from_below = from_neighbours(edges_one[1], edges_one[0])
    refined = conv(*where, *around, kernel_one, "conv_1")
    carried, partial_zero = carried_of(
        *where, upstream, hidden, inner_one, from_above, from_below, above, cells, below, places
    )
    sent_zero = exchange(partial_zero)
    inner_zero, edges_zero = spread_of(*where, carried, kernel_zero, "spread_0")
    from_above, from_below = from_neighbours(edges_zero[1], edges_zero[0])
    back = inner_zero.at[0].add(from_above.astype(F32)).at[last].add(from_below.astype(F32))
    input_grad = (carried.astype(F32) + jnp.where(cells > 0, back, 0.0)).astype(BF16)
    half = total_of(requested, sent_one, banks, 1)
    grad_banks = total_of(requested, sent_zero, banks, 0, half)
    return (jnp.transpose(refined, (1, 0, 2)), jnp.transpose(input_grad, (1, 0, 2)), grad_banks)


def solution(mesh):
    return jax.shard_map(
        body,
        mesh=mesh,
        in_specs=(
            P(None, ("groups", "gy"), None),
            P(None, ("groups", "gy"), None),
            P(None, "gy", None),
            P(("groups", "gy"), None),
            P(("groups", "gy"), None),
            P("groups"),
        ),
        out_specs=(
            P(None, ("groups", "gy"), None),
            P(None, ("groups", "gy"), None),
            P("groups", "gy", None),
        ),
        check_vma=False,
    )
```

profile of v0, /device:TPU:13, one launch (start us, length us, event | category | flops | bytes accessed | tf_op | source)
XLA Modules:
  0.0 315.4 jit_solution(4906140495135380902)
XLA Ops:
  2.6 10.2 %all_to_all.29 = s32[16,1,2]{2,1,0:T(1,128)S(1)} all-to-all(s32[16,1,2]{2,1,0:T(1,128)S(1)} %bitcast.43), channel_id=1, replica_groups=mesh['groups'=2,'gy'=16] {'gy'}, dimensions={0} | all-to-all | bytes 256 | tf_op jit(solution)/shard_map/all_to_all | solution.py:415
  15.4 5.8 %select_0.1 = bf16[32,288,128]{2,1,0:T(8,128)(2,1)S(1)} custom-call(s32[32]{0:T(128)S(1)} %reshape.166.requested, bf16[2,8,36864]{2,1,0:T(8,128)(2,1)S(1)} %copy-done.6), custom_call_target="tpu_custom_call" | custom-call | flops 1000000 | bytes 2949120 | tf_op jit(solution)/shard_map/select_0/pallas_call | solution.py:76
  22.6 6.4 %all-to-all-start.1 = ((bf16[32,288,128]{2,1,0:T(8,128)(2,1)}), bf16[32,288,128]{2,1,0:T(8,128)(2,1)S(1)}, u32[]{:S(2)}, u32[]{:S(2)}) async-start(bf16[32,288,128]{2,1,0:T(8,128)(2,1)} %copy-done.3), calls=%async_computation.1 | async-start | bytes 4718592 | tf_op jit(solution)/shard_map/all_to_all | solution.py:418
  28.9 5.8 %select_1.1 = bf16[32,288,128]{2,1,0:T(8,128)(2,1)S(1)} custom-call(s32[32]{0:T(128)S(1)} %reshape.166.requested, bf16[2,8,36864]{2,1,0:T(8,128)(2,1)S(1)} %copy-done.7), custom_call_target="tpu_custom_call" | custom-call | flops 1000000 | bytes 2949120 | tf_op jit(solution)/shard_map/select_1/pallas_call | solution.py:76
  34.7 1.4 copy-done.1
  36.2 45.8 %all-to-all-done.1.kernels = bf16[32,288,128]{2,1,0:T(8,128)(2,1)S(1)} async-done(((bf16[32,288,128]{2,1,0:T(8,128)(2,1)}), bf16[32,288,128]{2,1,0:T(8,128)(2,1)S(1)}, u32[]{:S(2)}, u32[]{:S(2)}) %all-to-all-start.1) | async-done | bytes 2359328 | tf_op jit(solution)/shard_map/all_to_all | solution.py:418
  82.0 4.9 %all-to-all-start.2 = ((bf16[32,288,128]{2,1,0:T(8,128)(2,1)}), bf16[32,288,128]{2,1,0:T(8,128)(2,1)}, u32[]{:S(2)}, u32[]{:S(2)}) async-start(bf16[32,288,128]{2,1,0:T(8,128)(2,1)} %copy-done.1), calls=%async_computation.2 | async-start | bytes 4718592 | tf_op jit(solution)/shard_map/all_to_all | solution.py:418
  87.9 3.3 %collective-permute-start = (bf16[64,2048]{1,0:T(8,128)(2,1)}, bf16[64,2048]{1,0:T(8,128)(2,1)S(1)}, u32[]{:S(2)}, u32[]{:S(2)}) collective-permute-start(bf16[64,2048]{1,0:T(8,128)(2,1)} %get-tuple-element.58), channel_id=1, source_target_pairs={{0,1},{1,2},{2,3},{3,4},{4,5},{5,6},{6,7},{7,8},{8,9},{9,10},{10,1... | collective-permute-start | bytes 786440 | tf_op jit(solution)/shard_map/ppermute | solution.py:394
  91.2 1.9 collective-permute-start.1
  93.2 47.9 %collective-permute-done.above = bf16[64,2048]{1,0:T(8,128)(2,1)S(1)} collective-permute-done((bf16[64,2048]{1,0:T(8,128)(2,1)}, bf16[64,2048]{1,0:T(8,128)(2,1)S(1)}, u32[]{:S(2)}, u32[]{:S(2)}) %collective-permute-start) | collective-permute-done | bytes 262176 | tf_op jit(solution)/shard_map/ppermute | solution.py:394
  145.3 5.4 %conv_0.1.middle.hidden = bf16[2,64,2048]{2,1,0:T(8,128)(2,1)S(1)} custom-call(s32[32]{0:T(128)S(1)} %multiply_add_fusion.position, s32[32]{0:T(128)S(1)} %reshape.165.listed, s32[2,2048]{1,0:T(2,128)S(1)} %copy-done.21, bf16[64,2048]{1,0:T(8,128)(2,1)S(1)} %copy-done.16, bf16[2,64,2048]{2,1,0:T(8,128)(2,1)S(1)} %bitcast.37, ...), custom_call_target="tpu_custom_call" | custom-call | flops 603979776 | bytes 5000000 | tf_op jit(solution)/shard_map/conv_0/pallas_call | solution.py:237
  150.8 4.3 %collective-permute-start.2 = (bf16[64,2048]{1,0:T(8,128)(2,1)S(1)}, bf16[64,2048]{1,0:T(8,128)(2,1)S(1)}, u32[]{:S(2)}, u32[]{:S(2)}) collective-permute-start(bf16[64,2048]{1,0:T(8,128)(2,1)S(1)} %get-tuple-element.56), channel_id=1, source_target_pairs={{0,1},{1,2},{2,3},{3,4},{4,5},{5,6},{6,7},{7,8},{8,9},{9,10},{10,1... | collective-permute-start | bytes 786440 | tf_op jit(solution)/shard_map/ppermute | solution.py:394
  155.0 1.9 collective-permute-start.3
  158.3 5.3 %collective-permute-done.3.below = bf16[64,2048]{1,0:T(8,128)(2,1)S(1)} collective-permute-done((bf16[64,2048]{1,0:T(8,128)(2,1)S(1)}, bf16[64,2048]{1,0:T(8,128)(2,1)S(1)}, u32[]{:S(2)}, u32[]{:S(2)}) %collective-permute-start.3) | collective-permute-done | bytes 262176 | tf_op jit(solution)/shard_map/ppermute | solution.py:395
  163.6 6.6 %partial_1.1 = bf16[32,288,128]{2,1,0:T(8,128)(2,1)S(1)} custom-call(s32[32]{0:T(128)S(1)} %multiply_add_fusion.position, s32[32]{0:T(128)S(1)} %reshape.165.listed, s32[2,2048]{1,0:T(2,128)S(1)} %copy-done.21, bf16[2,64,2048]{2,1,0:T(8,128)(2,1)S(1)} %bitcast.39, bf16[64,2048]{1,0:T(8,128)(2,1)S(1)} %collective-permute-done.2.above, ...), custom_call_target="tpu_custom_call" | custom-call | flops 603979776 | bytes 5000000 | tf_op jit(solution)/shard_map/partial_1/pallas_call | solution.py:274
  173.8 4.4 %all-to-all-start.4 = ((bf16[32,288,128]{2,1,0:T(8,128)(2,1)}), bf16[32,288,128]{2,1,0:T(8,128)(2,1)}, u32[]{:S(2)}, u32[]{:S(2)}) async-start(bf16[32,288,128]{2,1,0:T(8,128)(2,1)} %copy-done.2), calls=%async_computation.4 | async-start | bytes 4718592 | tf_op jit(solution)/shard_map/all_to_all | solution.py:418
  179.3 8.2 %spread_1.1 = (f32[2,64,2048]{2,1,0:T(8,128)S(1)}, bf16[2,64,2048]{2,1,0:T(8,128)(2,1)S(1)}) custom-call(s32[32]{0:T(128)S(1)} %multiply_add_fusion.position, s32[32]{0:T(128)S(1)} %reshape.165.listed, s32[2,2048]{1,0:T(2,128)S(1)} %copy-done.21, bf16[2,64,2048]{2,1,0:T(8,128)(2,1)S(1)} %bitcast.40, bf16[32,288,128]{2,1,0:T(8,128)(2,1)} %all-to-all-done.2.kernels), custom_call_target="tpu_custom_call" | custom-call | flops 603979776 | bytes 5000000 | tf_op jit(solution)/shard_map/spread_1/pallas_call | solution.py:377
  187.5 2.9 collective-permute-start.4
  190.4 1.9 collective-permute-start.5
  192.3 39.8 %collective-permute-done.4.from_above = bf16[64,2048]{1,0:T(8,128)(2,1)S(1)} collective-permute-done((bf16[64,2048]{1,0:T(8,128)(2,1)S(1)}, bf16[64,2048]{1,0:T(8,128)(2,1)S(1)}, u32[]{:S(2)}, u32[]{:S(2)}) %collective-permute-start.4) | collective-permute-done | bytes 262176 | tf_op jit(solution)/shard_map/ppermute | solution.py:394
  232.2 1.4 collective-permute-done.5.from_below
  233.6 6.8 %carried_partial_0.1 = (bf16[2,64,2048]{2,1,0:T(8,128)(2,1)S(1)}, bf16[32,288,128]{2,1,0:T(8,128)(2,1)S(1)}) custom-call(s32[32]{0:T(128)S(1)} %multiply_add_fusion.position, s32[32]{0:T(128)S(1)} %reshape.165.listed, s32[2,2048]{1,0:T(2,128)S(1)} %copy-done.21, bf16[2,64,2048]{2,1,0:T(8,128)(2,1)S(1)} %bitcast.41, ...), custom_call_target="tpu_custom_call" | custom-call | flops 603979776 | bytes 7000000 | tf_op jit(solution)/shard_map/carried_partial_0/pallas_call | solution.py:316
  240.5 1.4 copy-done.8
  242.7 4.9 %all-to-all-start.3 = ((bf16[32,288,128]{2,1,0:T(8,128)(2,1)}), bf16[32,288,128]{2,1,0:T(8,128)(2,1)}, u32[]{:S(2)}, u32[]{:S(2)}) async-start(bf16[32,288,128]{2,1,0:T(8,128)(2,1)} %copy-done.8), calls=%async_computation.3 | async-start | bytes 4718592 | tf_op jit(solution)/shard_map/all_to_all | solution.py:418
  247.6 7.0 %spread_0.1 = (f32[2,64,2048]{2,1,0:T(8,128)S(1)}, bf16[2,64,2048]{2,1,0:T(8,128)(2,1)S(1)}) custom-call(s32[32]{0:T(128)S(1)} %multiply_add_fusion.position, s32[32]{0:T(128)S(1)} %reshape.165.listed, s32[2,2048]{1,0:T(2,128)S(1)} %copy-done.21, bf16[2,64,2048]{2,1,0:T(8,128)(2,1)S(1)} %copy-done.10, bf16[32,288,128]{2,1,0:T(8,128)(2,1)S(1)} %all-to-all-done.1.kernels), custom_call_target="tpu_custom_call" | custom-call | flops 603979776 | bytes 5000000 | tf_op jit(solution)/shard_map/spread_0/pallas_call | solution.py:377
  254.6 3.5 %collective-permute-start.6 = (bf16[64,2048]{1,0:T(8,128)(2,1)S(1)}, bf16[64,2048]{1,0:T(8,128)(2,1)S(1)}, u32[]{:S(2)}, u32[]{:S(2)}) collective-permute-start(bf16[64,2048]{1,0:T(8,128)(2,1)S(1)} %get-tuple-element.52), channel_id=1, source_target_pairs={{0,1},{1,2},{2,3},{3,4},{4,5},{5,6},{6,7},{7,8},{8,9},{9,10},{10,1... | collective-permute-start | bytes 786440 | tf_op jit(solution)/shard_map/ppermute | solution.py:394
  258.1 6.5 %conv_1.1 = bf16[2,64,2048]{2,1,0:T(8,128)(2,1)S(1)} custom-call(s32[32]{0:T(128)S(1)} %multiply_add_fusion.position, s32[32]{0:T(128)S(1)} %reshape.165.listed, s32[2,2048]{1,0:T(2,128)S(1)} %copy-done.21, bf16[64,2048]{1,0:T(8,128)(2,1)S(1)} %copy-done.12, bf16[2,64,2048]{2,1,0:T(8,128)(2,1)S(1)} %conv_0.1.middle.hidden, bf16[64,2048]{1,0:T(8,128)(2,1)S(1)} %copy-done.14, ...), custom_call_target="tpu_custom_call" | custom-call | flops 603979776 | bytes 5000000 | tf_op jit(solution)/shard_map/conv_1/pallas_call | solution.py:237
  266.0 1.9 collective-permute-start.7
  267.9 33.8 %collective-permute-done.6 = bf16[64,2048]{1,0:T(8,128)(2,1)S(1)} collective-permute-done((bf16[64,2048]{1,0:T(8,128)(2,1)S(1)}, bf16[64,2048]{1,0:T(8,128)(2,1)S(1)}, u32[]{:S(2)}, u32[]{:S(2)}) %collective-permute-start.6) | collective-permute-done | bytes 262176 | tf_op jit(solution)/shard_map/ppermute | solution.py:394
  301.8 1.5 collective-permute-done.7
  305.2 5.1 %total_1.1.rest_0_ = f32[2,8,36864]{2,1,0:T(8,128)} custom-call(s32[32]{0:T(128)S(1)} %reshape.166.requested, bf16[32,288,128]{2,1,0:T(8,128)(2,1)} %all-to-all-done.4.parts), custom_call_target="tpu_custom_call" | custom-call | flops 1000000 | bytes 3538944 | tf_op jit(solution)/shard_map/total_1/pallas_call | solution.py:132
  310.3 5.1 %total_0.1 = f32[2,8,36864]{2,1,0:T(8,128)} custom-call(s32[32]{0:T(128)S(1)} %reshape.166.requested, bf16[32,288,128]{2,1,0:T(8,128)(2,1)} %all-to-all-done.3.parts, f32[2,8,36864]{2,1,0:T(8,128)} %total_1.1.rest_0_), custom_call_target="tpu_custom_call", output_to_operand_aliasing={{}: (2, {})} | custom-call | flops 1000000 | bytes 3538944 | tf_op jit(solution)/shard_map/total_0/pallas_call | solution.py:132
  (82 shorter events, 21.4 us)
Async XLA Ops:
  1.4 12.6 %copy-start.25 = (s32[16,2]{1,0:T(8,128)}, s32[16,2]{1,0:T(8,128)S(1)}, u32[]{:S(2)}) copy-start(s32[16,2]{1,0:T(8,128)S(1)} %copy.29) | copy-start | bytes 388
  14.1 1.3 copy-start.6
  21.1 1.4 copy-start.3
  22.5 6.4 %copy-start.7 = (bf16[2,8,36864]{2,1,0:T(8,128)(2,1)S(1)}, bf16[2,8,36864]{2,1,0:T(8,128)(2,1)}, u32[]{:S(2)}) copy-start(bf16[2,8,36864]{2,1,0:T(8,128)(2,1)} %banks.3) | copy-start | bytes 3538948
  22.6 59.4 %all-to-all-start.1 = ((bf16[32,288,128]{2,1,0:T(8,128)(2,1)}), bf16[32,288,128]{2,1,0:T(8,128)(2,1)S(1)}, u32[]{:S(2)}, u32[]{:S(2)}) async-start(bf16[32,288,128]{2,1,0:T(8,128)(2,1)} %copy-done.3), calls=%async_computation.1 | async-start | bytes 4718592 | tf_op jit(solution)/shard_map/all_to_all | solution.py:418
  34.7 1.4 copy-start.1
  36.2 50.7 %copy-start.22 = (bf16[64,2,2048]{2,1,0:T(2,128)(2,1)S(1)}, bf16[64,2,2048]{2,1,0:T(2,128)(2,1)}, u32[]{:S(2)}) copy-start(bf16[64,2,2048]{2,1,0:T(2,128)(2,1)} %param.10) | copy-start | bytes 1572868
  36.2 57.0 %copy-start.26 = (s32[16,2]{1,0:T(8,128)S(1)}, s32[16,2]{1,0:T(8,128)}, u32[]{:S(2)}) copy-start(s32[16,2]{1,0:T(8,128)} %copy-done.25) | copy-start | bytes 388
  36.2 107.3 %copy-start.21 = (s32[2,2048]{1,0:T(2,128)S(1)}, s32[2,2048]{1,0:T(2,128)}, u32[]{:S(2)}) copy-start(s32[2,2048]{1,0:T(2,128)} %regions.11) | copy-start | bytes 49156
  82.0 91.9 %all-to-all-start.2 = ((bf16[32,288,128]{2,1,0:T(8,128)(2,1)}), bf16[32,288,128]{2,1,0:T(8,128)(2,1)}, u32[]{:S(2)}, u32[]{:S(2)}) async-start(bf16[32,288,128]{2,1,0:T(8,128)(2,1)} %copy-done.1), calls=%async_computation.2 | async-start | bytes 4718592 | tf_op jit(solution)/shard_map/all_to_all | solution.py:418
  87.9 53.2 %collective-permute-start = (bf16[64,2048]{1,0:T(8,128)(2,1)}, bf16[64,2048]{1,0:T(8,128)(2,1)S(1)}, u32[]{:S(2)}, u32[]{:S(2)}) collective-permute-start(bf16[64,2048]{1,0:T(8,128)(2,1)} %get-tuple-element.58), channel_id=1, source_target_pairs={{0,1},{1,2},{2,3},{3,4},{4,5},{5,6},{6,7},{7,8},{8,9},{9,10},{10,1... | collective-permute-start | bytes 786440 | tf_op jit(solution)/shard_map/ppermute | solution.py:394
  91.2 51.5 %collective-permute-start.1 = (bf16[64,2048]{1,0:T(8,128)(2,1)}, bf16[64,2048]{1,0:T(8,128)(2,1)S(1)}, u32[]{:S(2)}, u32[]{:S(2)}) collective-permute-start(bf16[64,2048]{1,0:T(8,128)(2,1)} %get-tuple-element.57), channel_id=1, source_target_pairs={{1,0},{2,1},{3,2},{4,3},{5,4},{6,5},{7,6},{8,7},{9,8},{10,9},{11,1... | collective-permute-start | bytes 786440 | tf_op jit(solution)/shard_map/ppermute | solution.py:395
  143.4 1.0 copy-start.16
  144.4 0.9 copy-start.19
  145.3 11.6 %copy-start.24 = (bf16[64,2,2048]{2,1,0:T(2,128)(2,1)S(1)}, bf16[64,2,2048]{2,1,0:T(2,128)(2,1)}, u32[]{:S(2)}) copy-start(bf16[64,2,2048]{2,1,0:T(2,128)(2,1)} %param.11) | copy-start | bytes 1572868
  150.8 7.6 %collective-permute-start.2 = (bf16[64,2048]{1,0:T(8,128)(2,1)S(1)}, bf16[64,2048]{1,0:T(8,128)(2,1)S(1)}, u32[]{:S(2)}, u32[]{:S(2)}) collective-permute-start(bf16[64,2048]{1,0:T(8,128)(2,1)S(1)} %get-tuple-element.56), channel_id=1, source_target_pairs={{0,1},{1,2},{2,3},{3,4},{4,5},{5,6},{6,7},{7,8},{8,9},{9,10},{10,1... | collective-permute-start | bytes 786440 | tf_op jit(solution)/shard_map/ppermute | solution.py:394
  155.0 8.6 %collective-permute-start.3 = (bf16[64,2048]{1,0:T(8,128)(2,1)S(1)}, bf16[64,2048]{1,0:T(8,128)(2,1)S(1)}, u32[]{:S(2)}, u32[]{:S(2)}) collective-permute-start(bf16[64,2048]{1,0:T(8,128)(2,1)S(1)} %get-tuple-element.55), channel_id=1, source_target_pairs={{1,0},{2,1},{3,2},{4,3},{5,4},{6,5},{7,6},{8,7},{9,8},{10,9},{11,1... | collective-permute-start | bytes 786440 | tf_op jit(solution)/shard_map/ppermute | solution.py:395
  170.2 1.4 copy-start.2
  173.8 68.9 %all-to-all-start.4 = ((bf16[32,288,128]{2,1,0:T(8,128)(2,1)}), bf16[32,288,128]{2,1,0:T(8,128)(2,1)}, u32[]{:S(2)}, u32[]{:S(2)}) async-start(bf16[32,288,128]{2,1,0:T(8,128)(2,1)} %copy-done.2), calls=%async_computation.4 | async-start | bytes 4718592 | tf_op jit(solution)/shard_map/all_to_all | solution.py:418
  178.2 1.0 copy-start.5
  179.2 54.4 %copy-start.17 = (bf16[64,2048]{1,0:T(8,128)(2,1)S(1)}, bf16[64,2048]{1,0:T(8,128)(2,1)}, u32[]{:S(2)}) copy-start(bf16[64,2048]{1,0:T(8,128)(2,1)} %copy-done.15) | copy-start | bytes 786436
  179.2 54.4 %copy-start.20 = (bf16[64,2048]{1,0:T(8,128)(2,1)S(1)}, bf16[64,2048]{1,0:T(8,128)(2,1)}, u32[]{:S(2)}) copy-start(bf16[64,2048]{1,0:T(8,128)(2,1)} %copy-done.18) | copy-start | bytes 786436
  187.5 44.7 %collective-permute-start.4 = (bf16[64,2048]{1,0:T(8,128)(2,1)S(1)}, bf16[64,2048]{1,0:T(8,128)(2,1)S(1)}, u32[]{:S(2)}, u32[]{:S(2)}) collective-permute-start(bf16[64,2048]{1,0:T(8,128)(2,1)S(1)} %get-tuple-element.54), channel_id=1, source_target_pairs={{0,1},{1,2},{2,3},{3,4},{4,5},{5,6},{6,7},{7,8},{8,9},{9,10},{10,1... | collective-permute-start | bytes 786440 | tf_op jit(solution)/shard_map/ppermute | solution.py:394
  190.4 43.2 %collective-permute-start.5 = (bf16[64,2048]{1,0:T(8,128)(2,1)S(1)}, bf16[64,2048]{1,0:T(8,128)(2,1)S(1)}, u32[]{:S(2)}, u32[]{:S(2)}) collective-permute-start(bf16[64,2048]{1,0:T(8,128)(2,1)S(1)} %get-tuple-element.53), channel_id=1, source_target_pairs={{1,0},{2,1},{3,2},{4,3},{5,4},{6,5},{7,6},{8,7},{9,8},{10,9},{11,1... | collective-permute-start | bytes 786440 | tf_op jit(solution)/shard_map/ppermute | solution.py:395
  240.5 1.5 copy-start.8
  242.7 4.9 %copy-start.10 = (bf16[2,64,2048]{2,1,0:T(8,128)(2,1)S(1)}, bf16[2,64,2048]{2,1,0:T(8,128)(2,1)}, u32[]{:S(2)}) copy-start(bf16[2,64,2048]{2,1,0:T(8,128)(2,1)} %copy-done.9) | copy-start | bytes 1572868
  242.7 67.6 %all-to-all-start.3 = ((bf16[32,288,128]{2,1,0:T(8,128)(2,1)}), bf16[32,288,128]{2,1,0:T(8,128)(2,1)}, u32[]{:S(2)}, u32[]{:S(2)}) async-start(bf16[32,288,128]{2,1,0:T(8,128)(2,1)} %copy-done.8), calls=%async_computation.3 | async-start | bytes 4718592 | tf_op jit(solution)/shard_map/all_to_all | solution.py:418
  247.6 10.5 %copy-start.12 = (bf16[64,2048]{1,0:T(8,128)(2,1)S(1)}, bf16[64,2048]{1,0:T(8,128)(2,1)}, u32[]{:S(2)}) copy-start(bf16[64,2048]{1,0:T(8,128)(2,1)} %copy-done.11) | copy-start | bytes 786436
  247.6 10.5 %copy-start.14 = (bf16[64,2048]{1,0:T(8,128)(2,1)S(1)}, bf16[64,2048]{1,0:T(8,128)(2,1)}, u32[]{:S(2)}) copy-start(bf16[64,2048]{1,0:T(8,128)(2,1)} %copy-done.13) | copy-start | bytes 786436
  254.6 47.1 %collective-permute-start.6 = (bf16[64,2048]{1,0:T(8,128)(2,1)S(1)}, bf16[64,2048]{1,0:T(8,128)(2,1)S(1)}, u32[]{:S(2)}, u32[]{:S(2)}) collective-permute-start(bf16[64,2048]{1,0:T(8,128)(2,1)S(1)} %get-tuple-element.52), channel_id=1, source_target_pairs={{0,1},{1,2},{2,3},{3,4},{4,5},{5,6},{6,7},{7,8},{8,9},{9,10},{10,1... | collective-permute-start | bytes 786440 | tf_op jit(solution)/shard_map/ppermute | solution.py:394
  264.6 38.9 %copy-start.23 = (bf16[64,2,2048]{2,1,0:T(2,128)(2,1)S(1)}, bf16[64,2,2048]{2,1,0:T(2,128)(2,1)}, u32[]{:S(2)}) copy-start(bf16[64,2,2048]{2,1,0:T(2,128)(2,1)} %param.10) | copy-start | bytes 1572868
  266.0 37.4 %collective-permute-start.7 = (bf16[64,2048]{1,0:T(8,128)(2,1)S(1)}, bf16[64,2048]{1,0:T(8,128)(2,1)S(1)}, u32[]{:S(2)}, u32[]{:S(2)}) collective-permute-start(bf16[64,2048]{1,0:T(8,128)(2,1)S(1)} %get-tuple-element.51), channel_id=1, source_target_pairs={{1,0},{2,1},{3,2},{4,3},{5,4},{6,5},{7,6},{8,7},{9,8},{10,9},{11,1... | collective-permute-start | bytes 786440 | tf_op jit(solution)/shard_map/ppermute | solution.py:395
  (7 other events, 5.3 us)
where the time goes:
time: 316 us; the launch traced here: 315 us
  waiting for transfers between devices  178 us (56%)
  Pallas kernels  62.2 us (20%)
  starting transfers between devices  42.2 us (13%)
  local copies, waits for them, and re-layouts  20.6 us (7%)
  blocking collectives  10.2 us (3%)
    ppermute x4, waiting for transfers between devices, from_neighbours(): above = lax.ppermute(upper, 'gy', [(i, i + 1) for i in range(count - 1)])  123 us
    all_to_all x4, waiting for transfers between devices, exchange(): return lax.all_to_all(value, 'gy', split_axis=0, concat_axis=0, tiled=True)  45.8 us
    all_to_all x4, starting transfers between devices, exchange(): return lax.all_to_all(value, 'gy', split_axis=0, concat_axis=0, tiled=True)  20.5 us
    unnamed x59, local copies, waits for them, and re-layouts  18.1 us
    pallas_call x2, Pallas kernels, spread_of(): pl.pallas_call(spread_kernel, out_shape=(jax.ShapeDtypeStruct(upstream.sh...  15.1 us
    ppermute x4, starting transfers between devices, from_neighbours(): above = lax.ppermute(upper, 'gy', [(i, i + 1) for i in range(count - 1)])  14 us
    pallas_call x2, Pallas kernels, conv(): pl.pallas_call(conv_kernel, out_shape=jax.ShapeDtypeStruct(middle.shape,...  11.8 us
    pallas_call x2, Pallas kernels, select(): pl.pallas_call(functools.partial(select_kernel, per_dev, rows), grid=(1,)...  11.5 us
  transfers between devices with their start and end apart: 12, of which 9 were waited for; matrix products, arithmetic and copies ran while one was open for 1% of the time, Pallas kernels for 16%

commit v1 on v0

--- a/solution.py
+++ b/solution.py
@@ -396,6 +396,10 @@
     return above, below
 
 
+def after(first, value):
+    return lax.optimization_barrier((*first, value))
+
+
 def body(field, cotangent, banks, region_map, tile_regions, bank_slot):
     col_bands = tile_regions.shape[0]
     devices = lax.axis_size("gy")
@@ -421,27 +425,30 @@
     upstream = jnp.transpose(cotangent, (1, 0, 2))
     last = cells.shape[0] - 1
 
-    kernel_zero = exchange(select(requested, banks, 0))
-    kernel_one = exchange(select(requested, banks, 1))
-    above, below = from_neighbours(cells[last], cells[0])
     where = (position, listed, region_map)
+    above, below, requested = after(from_neighbours(cells[last], cells[0]), requested)
+    wire_one = select(requested, banks, 1)
+    wire_one, requested_then = after((wire_one,), requested)
+    kernel_one = exchange(wire_one)
+    kernel_zero = exchange(select(requested_then, banks, 0))
+    inner_one, edges_one = spread_of(*where, upstream, kernel_one, "spread_1")
+    from_above, from_below = from_neighbours(edges_one[1], edges_one[0])
     hidden = conv(*where, above, cells, below, kernel_zero, "conv_0")
     hidden_above, hidden_below = from_neighbours(hidden[last], hidden[0])
-    around = (hidden_above, hidden, hidden_below)
-    sent_one = exchange(partial_of(*where, upstream, *around, places))
-    inner_one, edges_one = spread_of(*where, upstream, kernel_one, "spread_1")
-    from_above, from_below = from_neighbours(edges_one[1], edges_one[0])
-    refined = conv(*where, *around, kernel_one, "conv_1")
     carried, partial_zero = carried_of(
         *where, upstream, hidden, inner_one, from_above, from_below, above, cells, below, places
     )
+    hidden_above, hidden_below, partial_zero = after((hidden_above, hidden_below), partial_zero)
+    around = (hidden_above, hidden, hidden_below)
     sent_zero = exchange(partial_zero)
     inner_zero, edges_zero = spread_of(*where, carried, kernel_zero, "spread_0")
     from_above, from_below = from_neighbours(edges_zero[1], edges_zero[0])
+    sent_one = exchange(partial_of(*where, upstream, *around, places))
+    refined = conv(*where, *around, kernel_one, "conv_1")
     back = inner_zero.at[0].add(from_above.astype(F32)).at[last].add(from_below.astype(F32))
     input_grad = (carried.astype(F32) + jnp.where(cells > 0, back, 0.0)).astype(BF16)
-    half = total_of(requested, sent_one, banks, 1)
-    grad_banks = total_of(requested, sent_zero, banks, 0, half)
+    half = total_of(requested, sent_zero, banks, 0)
+    grad_banks = total_of(requested, sent_one, banks, 1, half)
     return (jnp.transpose(refined, (1, 0, 2)), jnp.transpose(input_grad, (1, 0, 2)), grad_banks)
 
 

time: 316 us -> 303 us (0.959)
  waiting for transfers between devices: 178 us -> 160 us
    ppermute x4, waiting for transfers between devices: 123 us -> 33.9 us  [from_neighbours(): above = lax.ppermute(upper, 'gy', [(i, i + 1) for i in range(count - 1)])]
    all_to_all x4, waiting for transfers between devices: 45.8 us -> 124 us  [exchange(): return lax.all_to_all(value, 'gy', split_axis=0, concat_axis=0, tiled=True)]
    ppermute x4, waiting for transfers between devices: 9.2 us -> 1.56 us  [from_neighbours(): below = lax.ppermute(lower, 'gy', [(i + 1, i) for i in range(count - 1)])]
  transfers between devices with their start and end apart: 12 -> 12, of which waited for: 9 -> 5; matrix products, arithmetic and copies ran while one was open for 1% -> 2% of each run, Pallas kernels for 16% -> 17%
where the time goes in v1:
time: 303 us; the launch traced here: 302 us
  waiting for transfers between devices  160 us (53%)
  Pallas kernels  62.8 us (21%)
  starting transfers between devices  45.2 us (15%)
  local copies, waits for them, and re-layouts  23.2 us (8%)
  blocking collectives  8.58 us (3%)
    all_to_all x4, waiting for transfers between devices, exchange(): return lax.all_to_all(value, 'gy', split_axis=0, concat_axis=0, tiled=True)  124 us
    ppermute x4, waiting for transfers between devices, from_neighbours(): above = lax.ppermute(upper, 'gy', [(i, i + 1) for i in range(count - 1)])  33.9 us
    unnamed x59, local copies, waits for them, and re-layouts  20.7 us
    all_to_all x4, starting transfers between devices, exchange(): return lax.all_to_all(value, 'gy', split_axis=0, concat_axis=0, tiled=True)  20.5 us
    ppermute x4, starting transfers between devices, from_neighbours(): above = lax.ppermute(upper, 'gy', [(i, i + 1) for i in range(count - 1)])  15.7 us
    pallas_call x2, Pallas kernels, spread_of(): pl.pallas_call(spread_kernel, out_shape=(jax.ShapeDtypeStruct(upstream.sh...  15.1 us
    pallas_call x2, Pallas kernels, conv(): pl.pallas_call(conv_kernel, out_shape=jax.ShapeDtypeStruct(middle.shape,...  11.9 us
    pallas_call x2, Pallas kernels, select(): pl.pallas_call(functools.partial(select_kernel, per_dev, rows), grid=(1,)...  11.5 us
  transfers between devices with their start and end apart: 12, of which 5 were waited for; matrix products, arithmetic and copies ran while one was open for 2% of the time, Pallas kernels for 17%

profile of v1, /device:TPU:13, one launch (start us, length us, event | category | flops | bytes accessed | tf_op | source)
XLA Modules:
  0.0 302.1 jit_solution(7823559846942736945)
XLA Ops:
  2.0 2.6 collective-permute-start.1
  4.6 3.9 %collective-permute-start = (bf16[64,2048]{1,0:T(8,128)(2,1)S(1)}, bf16[64,2048]{1,0:T(8,128)(2,1)S(1)}, u32[]{:S(2)}, u32[]{:S(2)}) collective-permute-start(bf16[64,2048]{1,0:T(8,128)(2,1)S(1)} %get-tuple-element.74), channel_id=1, source_target_pairs={{0,1},{1,2},{2,3},{3,4},{4,5},{5,6},{6,7},{7,8},{8,9},{9,10},{10,1... | collective-permute-start | bytes 786440 | tf_op jit(solution)/shard_map/ppermute | solution.py:394
  10.5 8.6 %all_to_all.29 = s32[16,1,2]{2,1,0:T(1,128)S(1)} all-to-all(s32[16,1,2]{2,1,0:T(1,128)S(1)} %bitcast.43), channel_id=1, replica_groups=mesh['groups'=2,'gy'=16] {'gy'}, dimensions={0} | all-to-all | bytes 256 | tf_op jit(solution)/shard_map/all_to_all | solution.py:419
  20.4 5.8 %select_1.1 = bf16[32,288,128]{2,1,0:T(8,128)(2,1)S(1)} custom-call(s32[32]{0:T(128)S(1)} %reshape.166.requested, bf16[2,8,36864]{2,1,0:T(8,128)(2,1)S(1)} %copy-done.7), custom_call_target="tpu_custom_call" | custom-call | flops 1000000 | bytes 2949120 | tf_op jit(solution)/shard_map/select_1/pallas_call | solution.py:76
  26.2 1.4 copy-done.3
  27.6 6.2 %all-to-all-start.2 = ((bf16[32,288,128]{2,1,0:T(8,128)(2,1)}), bf16[32,288,128]{2,1,0:T(8,128)(2,1)S(1)}, u32[]{:S(2)}, u32[]{:S(2)}) async-start(bf16[32,288,128]{2,1,0:T(8,128)(2,1)} %copy-done.3), calls=%async_computation.2 | async-start | bytes 4718592 | tf_op jit(solution)/shard_map/all_to_all | solution.py:422
  35.1 5.8 %select_0.1 = bf16[32,288,128]{2,1,0:T(8,128)(2,1)S(1)} custom-call(s32[32]{0:T(128)S(1)} %reshape.166.requested, bf16[2,8,36864]{2,1,0:T(8,128)(2,1)S(1)} %copy-done.8), custom_call_target="tpu_custom_call" | custom-call | flops 1000000 | bytes 2949120 | tf_op jit(solution)/shard_map/select_0/pallas_call | solution.py:76
  40.9 1.4 copy-done.2
  42.3 44.6 %all-to-all-done.2.kernels = bf16[32,288,128]{2,1,0:T(8,128)(2,1)S(1)} async-done(((bf16[32,288,128]{2,1,0:T(8,128)(2,1)}), bf16[32,288,128]{2,1,0:T(8,128)(2,1)S(1)}, u32[]{:S(2)}, u32[]{:S(2)}) %all-to-all-start.2) | async-done | bytes 2359328 | tf_op jit(solution)/shard_map/all_to_all | solution.py:422
  86.9 4.9 %all-to-all-start.1 = ((bf16[32,288,128]{2,1,0:T(8,128)(2,1)}), bf16[32,288,128]{2,1,0:T(8,128)(2,1)}, u32[]{:S(2)}, u32[]{:S(2)}) async-start(bf16[32,288,128]{2,1,0:T(8,128)(2,1)} %copy-done.2), calls=%async_computation.1 | async-start | bytes 4718592 | tf_op jit(solution)/shard_map/all_to_all | solution.py:422
  92.1 7.0 %spread_1.1 = (f32[2,64,2048]{2,1,0:T(8,128)S(1)}, bf16[2,64,2048]{2,1,0:T(8,128)(2,1)S(1)}) custom-call(s32[32]{0:T(128)S(1)} %multiply_add_fusion.position, s32[32]{0:T(128)S(1)} %reshape.165.listed, s32[2,2048]{1,0:T(2,128)S(1)} %copy-done.24, bf16[2,64,2048]{2,1,0:T(8,128)(2,1)S(1)} %bitcast.39, bf16[32,288,128]{2,1,0:T(8,128)(2,1)S(1)} %all-to-all-done.2.kernels), custom_call_target="tpu_custom_call" | custom-call | flops 603979776 | bytes 5000000 | tf_op jit(solution)/shard_map/spread_1/pallas_call | solution.py:377
  101.6 2.3 collective-permute-start.5
  103.9 4.2 %collective-permute-start.4 = (bf16[64,2048]{1,0:T(8,128)(2,1)}, bf16[64,2048]{1,0:T(8,128)(2,1)}, u32[]{:S(2)}, u32[]{:S(2)}) collective-permute-start(bf16[64,2048]{1,0:T(8,128)(2,1)} %get-tuple-element.70), channel_id=1, source_target_pairs={{0,1},{1,2},{2,3},{3,4},{4,5},{5,6},{6,7},{7,8},{8,9},{9,10},{10,1... | collective-permute-start | bytes 786440 | tf_op jit(solution)/shard_map/ppermute | solution.py:394
  108.1 36.9 %all-to-all-done.1.kernels = bf16[32,288,128]{2,1,0:T(8,128)(2,1)} async-done(((bf16[32,288,128]{2,1,0:T(8,128)(2,1)}), bf16[32,288,128]{2,1,0:T(8,128)(2,1)}, u32[]{:S(2)}, u32[]{:S(2)}) %all-to-all-start.1) | async-done | bytes 2359328 | tf_op jit(solution)/shard_map/all_to_all | solution.py:422
  146.9 6.6 %conv_0.1.hidden.middle = bf16[2,64,2048]{2,1,0:T(8,128)(2,1)S(1)} custom-call(s32[32]{0:T(128)S(1)} %multiply_add_fusion.position, s32[32]{0:T(128)S(1)} %reshape.165.listed, s32[2,2048]{1,0:T(2,128)S(1)} %copy-done.24, bf16[64,2048]{1,0:T(8,128)(2,1)S(1)} %copy-done.23, bf16[2,64,2048]{2,1,0:T(8,128)(2,1)S(1)} %bitcast.37, ...), custom_call_target="tpu_custom_call" | custom-call | flops 603979776 | bytes 5000000 | tf_op jit(solution)/shard_map/conv_0/pallas_call | solution.py:237
  153.5 2.1 collective-permute-start.3
  155.6 4.3 %collective-permute-start.2 = (bf16[64,2048]{1,0:T(8,128)(2,1)S(1)}, bf16[64,2048]{1,0:T(8,128)(2,1)S(1)}, u32[]{:S(2)}, u32[]{:S(2)}) collective-permute-start(bf16[64,2048]{1,0:T(8,128)(2,1)S(1)} %get-tuple-element.72), channel_id=1, source_target_pairs={{0,1},{1,2},{2,3},{3,4},{4,5},{5,6},{6,7},{7,8},{8,9},{9,10},{10,1... | collective-permute-start | bytes 786440 | tf_op jit(solution)/shard_map/ppermute | solution.py:394
  161.0 7.4 %carried_partial_0.1 = (bf16[2,64,2048]{2,1,0:T(8,128)(2,1)S(1)}, bf16[32,288,128]{2,1,0:T(8,128)(2,1)S(1)}) custom-call(s32[32]{0:T(128)S(1)} %multiply_add_fusion.position, s32[32]{0:T(128)S(1)} %reshape.165.listed, s32[2,2048]{1,0:T(2,128)S(1)} %copy-done.24, bf16[2,64,2048]{2,1,0:T(8,128)(2,1)S(1)} %bitcast.40, ...), custom_call_target="tpu_custom_call" | custom-call | flops 603979776 | bytes 7000000 | tf_op jit(solution)/shard_map/carried_partial_0/pallas_call | solution.py:316
  168.4 1.4 copy-done.9
  172.0 4.5 %all-to-all-start.4 = ((bf16[32,288,128]{2,1,0:T(8,128)(2,1)}), bf16[32,288,128]{2,1,0:T(8,128)(2,1)}, u32[]{:S(2)}, u32[]{:S(2)}) async-start(bf16[32,288,128]{2,1,0:T(8,128)(2,1)} %copy-done.9), calls=%async_computation.4 | async-start | bytes 4718592 | tf_op jit(solution)/shard_map/all_to_all | solution.py:422
  178.4 6.6 %partial_1.1 = bf16[32,288,128]{2,1,0:T(8,128)(2,1)S(1)} custom-call(s32[32]{0:T(128)S(1)} %multiply_add_fusion.position, s32[32]{0:T(128)S(1)} %reshape.165.listed, s32[2,2048]{1,0:T(2,128)S(1)} %copy-done.24, bf16[2,64,2048]{2,1,0:T(8,128)(2,1)S(1)} %bitcast.41, bf16[64,2048]{1,0:T(8,128)(2,1)S(1)} %copy-done.16, ...), custom_call_target="tpu_custom_call" | custom-call | flops 603979776 | bytes 5000000 | tf_op jit(solution)/shard_map/partial_1/pallas_call | solution.py:274
  185.0 1.4 copy-done.1
  186.5 42.8 %all-to-all-done.4.parts = bf16[32,288,128]{2,1,0:T(8,128)(2,1)} async-done(((bf16[32,288,128]{2,1,0:T(8,128)(2,1)}), bf16[32,288,128]{2,1,0:T(8,128)(2,1)}, u32[]{:S(2)}, u32[]{:S(2)}) %all-to-all-start.4) | async-done | bytes 2359328 | tf_op jit(solution)/shard_map/all_to_all | solution.py:422
  229.3 4.9 %all-to-all-start.3 = ((bf16[32,288,128]{2,1,0:T(8,128)(2,1)}), bf16[32,288,128]{2,1,0:T(8,128)(2,1)}, u32[]{:S(2)}, u32[]{:S(2)}) async-start(bf16[32,288,128]{2,1,0:T(8,128)(2,1)} %copy-done.1), calls=%async_computation.3 | async-start | bytes 4718592 | tf_op jit(solution)/shard_map/all_to_all | solution.py:422
  234.2 8.2 %spread_0.1 = (f32[2,64,2048]{2,1,0:T(8,128)S(1)}, bf16[2,64,2048]{2,1,0:T(8,128)(2,1)S(1)}) custom-call(s32[32]{0:T(128)S(1)} %multiply_add_fusion.position, s32[32]{0:T(128)S(1)} %reshape.165.listed, s32[2,2048]{1,0:T(2,128)S(1)} %copy-done.24, bf16[2,64,2048]{2,1,0:T(8,128)(2,1)S(1)} %copy-done.11, bf16[32,288,128]{2,1,0:T(8,128)(2,1)} %all-to-all-done.1.kernels), custom_call_target="tpu_custom_call" | custom-call | flops 603979776 | bytes 5000000 | tf_op jit(solution)/shard_map/spread_0/pallas_call | solution.py:377
  242.4 3.3 %collective-permute-start.6 = (bf16[64,2048]{1,0:T(8,128)(2,1)S(1)}, bf16[64,2048]{1,0:T(8,128)(2,1)S(1)}, u32[]{:S(2)}, u32[]{:S(2)}) collective-permute-start(bf16[64,2048]{1,0:T(8,128)(2,1)S(1)} %get-tuple-element.68), channel_id=1, source_target_pairs={{0,1},{1,2},{2,3},{3,4},{4,5},{5,6},{6,7},{7,8},{8,9},{9,10},{10,1... | collective-permute-start | bytes 786440 | tf_op jit(solution)/shard_map/ppermute | solution.py:394
  245.8 1.9 collective-permute-start.7
  247.7 5.4 %conv_1.1 = bf16[2,64,2048]{2,1,0:T(8,128)(2,1)S(1)} custom-call(s32[32]{0:T(128)S(1)} %multiply_add_fusion.position, s32[32]{0:T(128)S(1)} %reshape.165.listed, s32[2,2048]{1,0:T(2,128)S(1)} %copy-done.24, bf16[64,2048]{1,0:T(8,128)(2,1)S(1)} %copy-done.17, bf16[2,64,2048]{2,1,0:T(8,128)(2,1)S(1)} %conv_0.1.hidden.middle, bf16[64,2048]{1,0:T(8,128)(2,1)S(1)} %copy-done.14, ...), custom_call_target="tpu_custom_call" | custom-call | flops 603979776 | bytes 5000000 | tf_op jit(solution)/shard_map/conv_1/pallas_call | solution.py:237
  254.4 33.9 %collective-permute-done.6 = bf16[64,2048]{1,0:T(8,128)(2,1)S(1)} collective-permute-done((bf16[64,2048]{1,0:T(8,128)(2,1)S(1)}, bf16[64,2048]{1,0:T(8,128)(2,1)S(1)}, u32[]{:S(2)}, u32[]{:S(2)}) %collective-permute-start.6) | collective-permute-done | bytes 262176 | tf_op jit(solution)/shard_map/ppermute | solution.py:394
  288.4 1.6 collective-permute-done.7
  291.8 5.1 %total_0.1.rest_0_ = f32[2,8,36864]{2,1,0:T(8,128)} custom-call(s32[32]{0:T(128)S(1)} %reshape.166.requested, bf16[32,288,128]{2,1,0:T(8,128)(2,1)} %all-to-all-done.4.parts), custom_call_target="tpu_custom_call" | custom-call | flops 1000000 | bytes 3538944 | tf_op jit(solution)/shard_map/total_0/pallas_call | solution.py:132
  296.9 5.1 %total_1.1 = f32[2,8,36864]{2,1,0:T(8,128)} custom-call(s32[32]{0:T(128)S(1)} %reshape.166.requested, bf16[32,288,128]{2,1,0:T(8,128)(2,1)} %all-to-all-done.3.parts, f32[2,8,36864]{2,1,0:T(8,128)} %total_0.1.rest_0_), custom_call_target="tpu_custom_call", output_to_operand_aliasing={{}: (2, {})} | custom-call | flops 1000000 | bytes 3538944 | tf_op jit(solution)/shard_map/total_1/pallas_call | solution.py:132
  (82 shorter events, 19.1 us)
Async XLA Ops:
  0.6 8.7 %copy-start = (s32[128]{0:T(128)S(1)}, s32[128]{0:T(128)}, u32[]{:S(2)}) copy-start(s32[128]{0:T(128)} %param.15) | copy-start | bytes 1540
  0.6 19.7 %copy-start.7 = (bf16[2,8,36864]{2,1,0:T(8,128)(2,1)S(1)}, bf16[2,8,36864]{2,1,0:T(8,128)(2,1)}, u32[]{:S(2)}) copy-start(bf16[2,8,36864]{2,1,0:T(8,128)(2,1)} %banks.3) | copy-start | bytes 3538948
  2.0 18.3 %collective-permute-start.1 = (bf16[64,2048]{1,0:T(8,128)(2,1)S(1)}, bf16[64,2048]{1,0:T(8,128)(2,1)S(1)}, u32[]{:S(2)}, u32[]{:S(2)}) collective-permute-start(bf16[64,2048]{1,0:T(8,128)(2,1)S(1)} %get-tuple-element.73), channel_id=1, source_target_pairs={{1,0},{2,1},{3,2},{4,3},{5,4},{6,5},{7,6},{8,7},{9,8},{10,9},{11,1... | collective-permute-start | bytes 786440 | tf_op jit(solution)/shard_map/ppermute | solution.py:395
  4.6 15.8 %collective-permute-start = (bf16[64,2048]{1,0:T(8,128)(2,1)S(1)}, bf16[64,2048]{1,0:T(8,128)(2,1)S(1)}, u32[]{:S(2)}, u32[]{:S(2)}) collective-permute-start(bf16[64,2048]{1,0:T(8,128)(2,1)S(1)} %get-tuple-element.74), channel_id=1, source_target_pairs={{0,1},{1,2},{2,3},{3,4},{4,5},{5,6},{6,7},{7,8},{8,9},{9,10},{10,1... | collective-permute-start | bytes 786440 | tf_op jit(solution)/shard_map/ppermute | solution.py:394
  20.3 7.2 %copy-start.20 = (bf16[64,2048]{1,0:T(8,128)(2,1)}, bf16[64,2048]{1,0:T(8,128)(2,1)S(1)}, u32[]{:S(2)}) copy-start(bf16[64,2048]{1,0:T(8,128)(2,1)S(1)} %collective-permute-done.1.below) | copy-start | bytes 786436
  20.4 7.2 %copy-start.22 = (bf16[64,2048]{1,0:T(8,128)(2,1)}, bf16[64,2048]{1,0:T(8,128)(2,1)S(1)}, u32[]{:S(2)}) copy-start(bf16[64,2048]{1,0:T(8,128)(2,1)S(1)} %collective-permute-done.above) | copy-start | bytes 786436
  26.2 1.4 copy-start.3
  27.6 59.3 %all-to-all-start.2 = ((bf16[32,288,128]{2,1,0:T(8,128)(2,1)}), bf16[32,288,128]{2,1,0:T(8,128)(2,1)S(1)}, u32[]{:S(2)}, u32[]{:S(2)}) async-start(bf16[32,288,128]{2,1,0:T(8,128)(2,1)} %copy-done.3), calls=%async_computation.2 | async-start | bytes 4718592 | tf_op jit(solution)/shard_map/all_to_all | solution.py:422
  33.8 1.3 copy-start.8
  40.9 1.4 copy-start.2
  42.3 49.6 %copy-start.26 = (bf16[64,2,2048]{2,1,0:T(2,128)(2,1)S(1)}, bf16[64,2,2048]{2,1,0:T(2,128)(2,1)}, u32[]{:S(2)}) copy-start(bf16[64,2,2048]{2,1,0:T(2,128)(2,1)} %param.11) | copy-start | bytes 1572868
  42.3 49.7 %copy-start.24 = (s32[2,2048]{1,0:T(2,128)S(1)}, s32[2,2048]{1,0:T(2,128)}, u32[]{:S(2)}) copy-start(s32[2,2048]{1,0:T(2,128)} %regions.11) | copy-start | bytes 49156
  86.9 58.1 %all-to-all-start.1 = ((bf16[32,288,128]{2,1,0:T(8,128)(2,1)}), bf16[32,288,128]{2,1,0:T(8,128)(2,1)}, u32[]{:S(2)}, u32[]{:S(2)}) async-start(bf16[32,288,128]{2,1,0:T(8,128)(2,1)} %copy-done.2), calls=%async_computation.1 | async-start | bytes 4718592 | tf_op jit(solution)/shard_map/all_to_all | solution.py:422
  99.8 1.0 copy-start.18
  101.6 58.3 %collective-permute-start.5 = (bf16[64,2048]{1,0:T(8,128)(2,1)}, bf16[64,2048]{1,0:T(8,128)(2,1)}, u32[]{:S(2)}, u32[]{:S(2)}) collective-permute-start(bf16[64,2048]{1,0:T(8,128)(2,1)} %get-tuple-element.69), channel_id=1, source_target_pairs={{1,0},{2,1},{3,2},{4,3},{5,4},{6,5},{7,6},{8,7},{9,8},{10,9},{11,1... | collective-permute-start | bytes 786440 | tf_op jit(solution)/shard_map/ppermute | solution.py:395
  103.9 56.1 %collective-permute-start.4 = (bf16[64,2048]{1,0:T(8,128)(2,1)}, bf16[64,2048]{1,0:T(8,128)(2,1)}, u32[]{:S(2)}, u32[]{:S(2)}) collective-permute-start(bf16[64,2048]{1,0:T(8,128)(2,1)} %get-tuple-element.70), channel_id=1, source_target_pairs={{0,1},{1,2},{2,3},{3,4},{4,5},{5,6},{6,7},{7,8},{8,9},{9,10},{10,1... | collective-permute-start | bytes 786440 | tf_op jit(solution)/shard_map/ppermute | solution.py:394
  146.9 13.1 %copy-start.19 = (f32[2,64,2048]{2,1,0:T(8,128)S(1)}, f32[2,64,2048]{2,1,0:T(8,128)}, u32[]{:S(2)}) copy-start(f32[2,64,2048]{2,1,0:T(8,128)} %copy-done.18) | copy-start | bytes 3145732
  153.5 17.1 %collective-permute-start.3 = (bf16[64,2048]{1,0:T(8,128)(2,1)S(1)}, bf16[64,2048]{1,0:T(8,128)(2,1)S(1)}, u32[]{:S(2)}, u32[]{:S(2)}) collective-permute-start(bf16[64,2048]{1,0:T(8,128)(2,1)S(1)} %get-tuple-element.71), channel_id=1, source_target_pairs={{1,0},{2,1},{3,2},{4,3},{5,4},{6,5},{7,6},{8,7},{9,8},{10,9},{11,1... | collective-permute-start | bytes 786440 | tf_op jit(solution)/shard_map/ppermute | solution.py:395
  155.6 15.7 %collective-permute-start.2 = (bf16[64,2048]{1,0:T(8,128)(2,1)S(1)}, bf16[64,2048]{1,0:T(8,128)(2,1)S(1)}, u32[]{:S(2)}, u32[]{:S(2)}) collective-permute-start(bf16[64,2048]{1,0:T(8,128)(2,1)S(1)} %get-tuple-element.72), channel_id=1, source_target_pairs={{0,1},{1,2},{2,3},{3,4},{4,5},{5,6},{6,7},{7,8},{8,9},{9,10},{10,1... | collective-permute-start | bytes 786440 | tf_op jit(solution)/shard_map/ppermute | solution.py:394
  160.0 1.0 copy-start.5
  168.4 1.4 copy-start.9
  172.0 4.5 %copy-start.6 = (bf16[64,2,2048]{2,0,1:T(8,128)(2,1)S(1)}, bf16[64,2,2048]{2,0,1:T(8,128)(2,1)}, u32[]{:S(2)}) copy-start(bf16[64,2,2048]{2,0,1:T(8,128)(2,1)} %copy-done.4) | copy-start | bytes 1572868
  172.0 57.2 %all-to-all-start.4 = ((bf16[32,288,128]{2,1,0:T(8,128)(2,1)}), bf16[32,288,128]{2,1,0:T(8,128)(2,1)}, u32[]{:S(2)}, u32[]{:S(2)}) async-start(bf16[32,288,128]{2,1,0:T(8,128)(2,1)} %copy-done.9), calls=%async_computation.4 | async-start | bytes 4718592 | tf_op jit(solution)/shard_map/all_to_all | solution.py:422
  176.5 1.0 copy-start.13
  185.0 1.5 copy-start.1
  186.5 47.7 %copy-start.11 = (bf16[2,64,2048]{2,1,0:T(8,128)(2,1)S(1)}, bf16[2,64,2048]{2,1,0:T(8,128)(2,1)}, u32[]{:S(2)}) copy-start(bf16[2,64,2048]{2,1,0:T(8,128)(2,1)} %copy-done.10) | copy-start | bytes 1572868
  229.3 67.6 %all-to-all-start.3 = ((bf16[32,288,128]{2,1,0:T(8,128)(2,1)}), bf16[32,288,128]{2,1,0:T(8,128)(2,1)}, u32[]{:S(2)}, u32[]{:S(2)}) async-start(bf16[32,288,128]{2,1,0:T(8,128)(2,1)} %copy-done.1), calls=%async_computation.3 | async-start | bytes 4718592 | tf_op jit(solution)/shard_map/all_to_all | solution.py:422
  234.2 13.5 %copy-start.14 = (bf16[64,2048]{1,0:T(8,128)(2,1)S(1)}, bf16[64,2048]{1,0:T(8,128)(2,1)}, u32[]{:S(2)}) copy-start(bf16[64,2048]{1,0:T(8,128)(2,1)} %copy-done.12) | copy-start | bytes 786436
  234.2 13.5 %copy-start.17 = (bf16[64,2048]{1,0:T(8,128)(2,1)S(1)}, bf16[64,2048]{1,0:T(8,128)(2,1)}, u32[]{:S(2)}) copy-start(bf16[64,2048]{1,0:T(8,128)(2,1)} %copy-done.15) | copy-start | bytes 786436
  242.4 45.9 %collective-permute-start.6 = (bf16[64,2048]{1,0:T(8,128)(2,1)S(1)}, bf16[64,2048]{1,0:T(8,128)(2,1)S(1)}, u32[]{:S(2)}, u32[]{:S(2)}) collective-permute-start(bf16[64,2048]{1,0:T(8,128)(2,1)S(1)} %get-tuple-element.68), channel_id=1, source_target_pairs={{0,1},{1,2},{2,3},{3,4},{4,5},{5,6},{6,7},{7,8},{8,9},{9,10},{10,1... | collective-permute-start | bytes 786440 | tf_op jit(solution)/shard_map/ppermute | solution.py:394
  245.8 44.2 %collective-permute-start.7 = (bf16[64,2048]{1,0:T(8,128)(2,1)S(1)}, bf16[64,2048]{1,0:T(8,128)(2,1)S(1)}, u32[]{:S(2)}, u32[]{:S(2)}) collective-permute-start(bf16[64,2048]{1,0:T(8,128)(2,1)S(1)} %get-tuple-element.67), channel_id=1, source_target_pairs={{1,0},{2,1},{3,2},{4,3},{5,4},{6,5},{7,6},{8,7},{9,8},{10,9},{11,1... | collective-permute-start | bytes 786440 | tf_op jit(solution)/shard_map/ppermute | solution.py:395
  253.1 37.0 %copy-start.25 = (bf16[64,2,2048]{2,1,0:T(2,128)(2,1)S(1)}, bf16[64,2,2048]{2,1,0:T(2,128)(2,1)}, u32[]{:S(2)}) copy-start(bf16[64,2,2048]{2,1,0:T(2,128)(2,1)} %param.10) | copy-start | bytes 1572868
  (7 other events, 5.9 us)

commit v2 on v1

--- a/solution.py
+++ b/solution.py
@@ -5,6 +5,7 @@
 from jax import lax
 from jax.experimental import pallas as pl
 from jax.experimental.pallas import tpu as pltpu
+from jax.sharding import Mesh
 from jax.sharding import PartitionSpec as P
 
 grad_unscale = 0.03125
@@ -15,6 +16,28 @@
 SMEM = pl.BlockSpec(memory_space=pltpu.SMEM)
 HBM = pl.BlockSpec(memory_space=pl.ANY)
 
+NEAR = 4
+
+
+def pairs_of(parts):
+    return 4 // parts
+
+
+def tail_of(parts):
+    return 32 // parts
+
+
+def part_rows(parts):
+    return 64 * pairs_of(parts) + tail_of(parts)
+
+
+def pair_start(pair, parts):
+    return pair // pairs_of(parts) * part_rows(parts) + 64 * (pair % pairs_of(parts))
+
+
+def tail_start(part, parts):
+    return part * part_rows(parts) + 64 * pairs_of(parts)
+
 
 def params(mib):
     return pltpu.CompilerParams(vmem_limit_bytes=mib * 2**20)
@@ -32,66 +55,81 @@
     return lax.broadcasted_iota(jnp.int32, tile.shape, 1) < LANES // 2
 
 
-def select_kernel(per_dev, rows, requested, banks, out, natural, travel, wire, sems):
-    for chunk in range(rows):
-        tile = banks[0, :, chunk * LANES : (chunk + 1) * LANES].astype(F32)
-        natural[pl.ds(chunk, per_dev, stride=rows), :] = tile
-
-    @pl.loop(0, per_dev)
-    def _(row):
-        base = row * rows
-
-        def blend(first, second, start, count):
-            even = jnp.where(low_half(first), first, swap_halves(second))
-            odd = jnp.where(low_half(first), swap_halves(first), second)
-            travel[pl.ds(start, count, stride=2), :] = even
-            travel[pl.ds(start + 1, count, stride=2), :] = odd
-
-        for pair in range(4):
-            blend(
-                natural[pl.ds(base + 64 * pair, 32), :],
-                natural[pl.ds(base + 64 * pair + 32, 32), :],
-                64 * pair,
-                32,
-            )
-        blend(natural[pl.ds(base + 256, 16), :], natural[pl.ds(base + 272, 16), :], 256, 16)
-        wire[row] = travel[...].astype(BF16)
-
-    places = out.shape[0]
-
-    def copy(place):
-        source = wire.at[jnp.maximum(requested[place], 0)]
-        return pltpu.make_async_copy(source, out.at[place], sems.at[place])
-
-    for place in range(places):
-        copy(place).start()
-    for place in range(places):
-        copy(place).wait()
-
-
-def select(requested, banks, layer):
+def wire_kernel(parts, per_dev, rows, own_part, banks, out, natural, travel):
+    for part in range(parts):
+
+        @pl.when(own_part[0] == part)
+        def _(part=part):
+            pairs = range(part * pairs_of(parts), (part + 1) * pairs_of(parts))
+            half = tail_of(parts) // 2
+            for chunk in [*range(64 * pairs[0], 64 * pairs[-1] + 64), *range(256, rows)]:
+                tile = banks[0, :, chunk * LANES : (chunk + 1) * LANES].astype(F32)
+                natural[pl.ds(chunk, per_dev, stride=rows), :] = tile
+
+            @pl.loop(0, per_dev)
+            def _(row):
+                base = row * rows
+
+                def blend(first, second, start, count):
+                    first = natural[pl.ds(base + first, count), :]
+                    second = natural[pl.ds(base + second, count), :]
+                    even = jnp.where(low_half(first), first, swap_halves(second))
+                    odd = jnp.where(low_half(first), swap_halves(first), second)
+                    travel[pl.ds(start, count, stride=2), :] = even
+                    travel[pl.ds(start + 1, count, stride=2), :] = odd
+
+                for order, pair in enumerate(pairs):
+                    blend(64 * pair, 64 * pair + 32, 64 * order, 32)
+                blend(256 + part * half, 272 + part * half, 64 * len(pairs), half)
+                out[row] = travel[...].astype(BF16)
+
+
+def wire(own_part, banks, layer, parts):
     layers, per_dev, width = banks.shape
     rows = width // LANES
-    places = requested.shape[0]
-    return pl.pallas_call(
-        functools.partial(select_kernel, per_dev, rows),
+    return pl.pallas_call(
+        functools.partial(wire_kernel, parts, per_dev, rows),
         grid=(1,),
-        out_shape=jax.ShapeDtypeStruct((places, rows, LANES), BF16),
+        out_shape=jax.ShapeDtypeStruct((per_dev, part_rows(parts), LANES), BF16),
         in_specs=[SMEM, pl.BlockSpec((1, per_dev, width), lambda step: (layer, 0, 0))],
-        out_specs=HBM,
+        out_specs=pl.BlockSpec((per_dev, part_rows(parts), LANES), lambda step: (0, 0, 0)),
         scratch_shapes=[
             pltpu.VMEM((per_dev * rows, LANES), F32),
-            pltpu.VMEM((rows, LANES), F32),
-            pltpu.VMEM((per_dev, rows, LANES), BF16),
-            pltpu.SemaphoreType.DMA((places,)),
+            pltpu.VMEM((part_rows(parts), LANES), F32),
         ],
         compiler_params=params(24),
-        cost_estimate=cost(1000000, 2 * (places + per_dev) * width),
-        name=f"select_{layer}",
-    )(requested, banks)
-
-
-def total_kernel(per_dev, rows, requested, parts, *rest):
+        cost_estimate=cost(10**11, 4 * per_dev * width),
+        name=f"wire_{layer}",
+    )(own_part, banks)
+
+
+def pack_kernel(step_of, row_of, *refs):
+    buffers, out = refs[:-1], refs[-1]
+
+    @pl.loop(0, out.shape[0])
+    def _(place):
+        for step, buffer in enumerate(buffers):
+
+            @pl.when(step_of[place] == step)
+            def _(buffer=buffer):
+                out[place] = buffer[row_of[place]]
+
+
+def pack(step_of, row_of, buffers, name):
+    places = step_of.shape[0]
+    shape = buffers[0].shape[1:]
+    return pl.pallas_call(
+        pack_kernel,
+        out_shape=jax.ShapeDtypeStruct((places, *shape), BF16),
+        in_specs=[SMEM, SMEM] + [VMEM] * len(buffers),
+        out_specs=VMEM,
+        compiler_params=params(32),
+        cost_estimate=cost(10**11, 4 * places * shape[0] * shape[1]),
+        name=name,
+    )(step_of, row_of, *buffers)
+
+
+def total_kernel(groups, per_dev, rows, requested, parts, *rest):
     out, total, natural = rest[-3:]
     total[...] = jnp.zeros_like(total)
 
@@ -114,14 +152,16 @@
             natural[pl.ds(base + second, count), :] = jnp.where(low_half(even), swap_halves(even), odd)
 
         for pair in range(4):
-            split(64 * pair, 32, 64 * pair, 64 * pair + 32)
-        split(256, 16, 256, 272)
+            split(pair_start(pair, groups), 32, 64 * pair, 64 * pair + 32)
+        half = tail_of(groups) // 2
+        for part in range(groups):
+            split(tail_start(part, groups), half, 256 + part * half, 272 + part * half)
 
     for chunk in range(rows):
         out[0, :, chunk * LANES : (chunk + 1) * LANES] = natural[pl.ds(chunk, per_dev, stride=rows), :]
 
 
-def total_of(requested, parts, banks, layer, earlier=None):
+def total_of(requested, parts, banks, layer, groups, earlier=None):
     layers, per_dev, width = banks.shape
     rows = width // LANES
     places = requested.shape[0]
@@ -130,7 +170,7 @@
         args.append(earlier)
         specs.append(HBM)
     return pl.pallas_call(
-        functools.partial(total_kernel, per_dev, rows),
+        functools.partial(total_kernel, groups, per_dev, rows),
         grid=(1,),
         out_shape=jax.ShapeDtypeStruct((layers, per_dev, width), F32),
         in_specs=specs,
@@ -182,13 +222,16 @@
     return jnp.concatenate(taps, axis=0)
 
 
-def band_weights(kernels, position, band):
+def band_weights(kernels, place_of, band):
+    parts = kernels.shape[0]
+    tail = 64 * pairs_of(parts)
     wide, last = [], []
     for slot in range(2):
-        one = kernels.at[position[2 * band + slot]]
-        wide.append(jnp.concatenate([one[64 * pair : 64 * pair + 64, :] for pair in range(4)], axis=1))
-        tail = one[256:288, :]
-        last.extend([tail[:, :64], tail[:, 64:]])
+        ones = [kernels.at[part, place_of[2 * band + slot]] for part in range(parts)]
+        blocks = [one[start : start + 64, :] for one in ones for start in range(0, tail, 64)]
+        wide.append(jnp.concatenate(blocks, axis=1))
+        rest = jnp.concatenate([one[tail : tail + tail_of(parts), :] for one in ones], axis=0)
+        last.extend([rest[:, :64], rest[:, 64:]])
     return jnp.concatenate(wide, axis=0), jnp.concatenate(last, axis=0)
 
 
@@ -219,7 +262,7 @@
     tile_rows, channels, columns = middle.shape
     fill_shifts(above, middle, below, shifts)
 
-    @pl.loop(0, columns // LANES)
+    @pl.loop(0, columns // LANES, unroll=2)
     def _(band):
         cells = unfolded(shifts, band, tile_rows)
         wide, last = band_weights(kernels, position, band)
@@ -246,10 +289,10 @@
     )(position, listed, regions, above, middle, below, kernels)
 
 
-def partial_bands(position, listed, regions, upstream, shifts, out):
+def partial_bands(groups, position, listed, regions, upstream, shifts, out):
     tile_rows, channels, columns = upstream.shape
 
-    @pl.loop(0, columns // LANES)
+    @pl.loop(0, columns // LANES, unroll=2)
     def _(band):
         cells = unfolded(shifts, band, tile_rows)
         mask = first_mask(regions, listed, band, channels, tile_rows)
@@ -259,20 +302,25 @@
             mine = sums[channels * slot : channels * (slot + 1)]
             there = out.at[position[2 * band + slot]]
             for pair in range(4):
-                there[64 * pair : 64 * pair + 64, :] = mine[:, LANES * pair : LANES * (pair + 1)]
-            there[256:288, :] = jnp.concatenate([mine[:32, 512:], mine[32:, 512:]], axis=1)
-
-
-def partial_kernel(position, listed, regions, upstream, above, middle, below, out, shifts):
+                start = pair_start(pair, groups)
+                there[start : start + 64, :] = mine[:, LANES * pair : LANES * (pair + 1)]
+            rest = jnp.concatenate([mine[:32, 512:], mine[32:, 512:]], axis=1)
+            size = tail_of(groups)
+            for part in range(groups):
+                start = tail_start(part, groups)
+                there[start : start + size, :] = rest[size * part : size * (part + 1)]
+
+
+def partial_kernel(groups, position, listed, regions, upstream, above, middle, below, out, shifts):
     fill_shifts(above, middle, below, shifts)
-    partial_bands(position, listed, regions, upstream, shifts, out)
-
-
-def partial_of(position, listed, regions, upstream, above, middle, below, places):
+    partial_bands(groups, position, listed, regions, upstream, shifts, out)
+
+
+def partial_of(position, listed, regions, upstream, above, middle, below, places, groups):
     tile_rows, channels, columns = middle.shape
     rows = 9 * channels * channels // LANES
     return pl.pallas_call(
-        partial_kernel,
+        functools.partial(partial_kernel, groups),
         out_shape=jax.ShapeDtypeStruct((places, rows, LANES), BF16),
         in_specs=[SMEM, SMEM] + [VMEM] * 5,
         out_specs=VMEM,
@@ -284,7 +332,7 @@
 
 
 def carried_kernel(
-    position, listed, regions, cotangent, hidden, inner, from_above, from_below, above, middle, below,
+    groups, position, listed, regions, cotangent, hidden, inner, from_above, from_below, above, middle, below,
     carried, out, shifts,
 ):
     tile_rows, channels, columns = middle.shape
@@ -304,17 +352,17 @@
             value = cotangent[row, here, :].astype(F32) + jnp.where(keep, back, 0.0)
             carried[row, here, :] = value.astype(BF16)
 
-    partial_bands(position, listed, regions, carried, shifts, out)
+    partial_bands(groups, position, listed, regions, carried, shifts, out)
 
 
 def carried_of(
     position, listed, regions, cotangent, hidden, inner, from_above, from_below, above, middle, below,
-    places,
+    places, groups,
 ):
     tile_rows, channels, columns = middle.shape
     rows = 9 * channels * channels // LANES
     return pl.pallas_call(
-        carried_kernel,
+        functools.partial(carried_kernel, groups),
         out_shape=(
             jax.ShapeDtypeStruct(middle.shape, BF16),
             jax.ShapeDtypeStruct((places, rows, LANES), BF16),
@@ -335,7 +383,7 @@
     tile_rows, channels, columns = upstream.shape
     total[...] = jnp.zeros_like(total)
 
-    @pl.loop(0, columns // LANES)
+    @pl.loop(0, columns // LANES, unroll=2)
     def _(band):
         wide, last = band_weights(kernels, position, band)
         mask = first_mask(regions, listed, band, channels, tile_rows)
@@ -389,85 +437,126 @@
     )(position, listed, regions, upstream, kernels)
 
 
+GY = ("far", "near")
+PLANE = ("groups", "near")
+ALL = ("groups", "far", "near")
+
+
 def from_neighbours(upper, lower):
-    count = lax.axis_size("gy")
-    above = lax.ppermute(upper, "gy", [(i, i + 1) for i in range(count - 1)])
-    below = lax.ppermute(lower, "gy", [(i + 1, i) for i in range(count - 1)])
+    count = lax.axis_size(GY)
+    above = lax.ppermute(upper, GY, [(i, i + 1) for i in range(count - 1)])
+    below = lax.ppermute(lower, GY, [(i + 1, i) for i in range(count - 1)])
     return above, below
+
+
+def exchange(value, axes):
+    return lax.all_to_all(value, axes, split_axis=0, concat_axis=0, tiled=True)
 
 
 def after(first, value):
     return lax.optimization_barrier((*first, value))
 
 
+def places_for(owner, owners, per_owner, content):
+    order = jnp.arange(owner.shape[0], dtype=jnp.int32)
+    earlier = (owner[:, None] == owner[None, :]) & (order[None, :] < order[:, None])
+    position = owner * per_owner + jnp.sum(earlier.astype(jnp.int32), axis=-1)
+    hits = position[None, :] == jnp.arange(owners * per_owner, dtype=jnp.int32)[:, None]
+    wanted = jnp.max(jnp.where(hits, content[None, :], -1), axis=1)
+    return position, wanted.reshape(owners, per_owner)
+
+
 def body(field, cotangent, banks, region_map, tile_regions, bank_slot):
     col_bands = tile_regions.shape[0]
-    devices = lax.axis_size("gy")
+    groups, far, near = (lax.axis_size(axis) for axis in ALL)
+    devices = far * near
     per_dev = banks.shape[1]
     slots_per = max(1, 2 * col_bands // devices)
     places = devices * slots_per
+    most = min(far * slots_per, 2 * col_bands)
     listed = tile_regions.reshape(-1)
     bank_row = bank_slot[listed]
     holder = bank_row // per_dev
     local_row = bank_row % per_dev
-    order = jnp.arange(2 * col_bands, dtype=jnp.int32)
-    earlier = (holder[:, None] == holder[None, :]) & (order[None, :] < order[:, None])
-    rank_in = jnp.sum(earlier.astype(jnp.int32), axis=-1)
-    position = holder * slots_per + rank_in
-    hits = position[None, :] == jnp.arange(places, dtype=jnp.int32)[:, None]
-    wanted = jnp.max(jnp.where(hits, local_row[None, :], -1), axis=1).reshape(devices, slots_per)
-    requested = lax.all_to_all(wanted, "gy", split_axis=0, concat_axis=0, tiled=True).reshape(-1)
-
-    def exchange(value):
-        return lax.all_to_all(value, "gy", split_axis=0, concat_axis=0, tiled=True)
+    position, wanted = places_for(holder, devices, slots_per, local_row)
+    source, asking = places_for(holder % near, near, most, holder // near * per_dev + local_row)
+    my_group, my_far = lax.axis_index("groups"), lax.axis_index("far")
 
     cells = jnp.transpose(field, (1, 0, 2))
     upstream = jnp.transpose(cotangent, (1, 0, 2))
     last = cells.shape[0] - 1
-
     where = (position, listed, region_map)
-    above, below, requested = after(from_neighbours(cells[last], cells[0]), requested)
-    wire_one = select(requested, banks, 1)
-    wire_one, requested_then = after((wire_one,), requested)
-    kernel_one = exchange(wire_one)
-    kernel_zero = exchange(select(requested_then, banks, 0))
-    inner_one, edges_one = spread_of(*where, upstream, kernel_one, "spread_1")
+    fetch = (source, listed, region_map)
+
+    own_part = my_group.astype(jnp.int32).reshape(1)
+    wire_one = wire(own_part, banks, 1, groups)
+    turns = [[(k, (k + step) % far) for k in range(far)] for step in range(1, far)]
+    bank_one = [wire_one] + [lax.ppermute(wire_one, "far", turn) for turn in turns]
+    above, below = from_neighbours(cells[last], cells[0])
+    *bank_one, above, below, own_part = after((*bank_one, above, below), own_part)
+    wire_zero = wire(own_part, banks, 0, groups)
+    bank_zero = [wire_zero] + [lax.ppermute(wire_zero, "far", turn) for turn in turns]
+    message = jnp.concatenate(
+        [
+            jnp.broadcast_to(wanted.reshape(1, far, near, slots_per), (groups, far, near, slots_per)),
+            jnp.broadcast_to(asking.reshape(1, 1, near, most), (groups, far, near, most)),
+        ],
+        axis=-1,
+    )
+    message = exchange(message.reshape(groups * devices, slots_per + most), ALL)
+    message = message.reshape(groups, far, near, slots_per + most)
+    requested = lax.dynamic_index_in_dim(message, my_group, 0, False)[:, :, :slots_per].reshape(-1)
+    asked = lax.dynamic_index_in_dim(message, my_far, 1, False)[:, :, slots_per:].reshape(-1)
+    step_of = jnp.where(asked < 0, 0, (my_far - asked // per_dev + far) % far).astype(jnp.int32)
+    row_of = jnp.where(asked < 0, 0, asked % per_dev)
+
+    def fetched(buffers, name):
+        arrived = exchange(pack(step_of, row_of, buffers, name), PLANE)
+        return arrived.reshape(groups, near * most, *arrived.shape[1:])
+
+    kernel_one = fetched(bank_one, "pack_1")
+    kernel_zero = fetched(bank_zero, "pack_0")
+    inner_one, edges_one = spread_of(*fetch, upstream, kernel_one, "spread_1")
     from_above, from_below = from_neighbours(edges_one[1], edges_one[0])
-    hidden = conv(*where, above, cells, below, kernel_zero, "conv_0")
+    hidden = conv(*fetch, above, cells, below, kernel_zero, "conv_0")
     hidden_above, hidden_below = from_neighbours(hidden[last], hidden[0])
     carried, partial_zero = carried_of(
-        *where, upstream, hidden, inner_one, from_above, from_below, above, cells, below, places
+        *where, upstream, hidden, inner_one, from_above, from_below, above, cells, below, places, groups
     )
     hidden_above, hidden_below, partial_zero = after((hidden_above, hidden_below), partial_zero)
     around = (hidden_above, hidden, hidden_below)
-    sent_zero = exchange(partial_zero)
-    inner_zero, edges_zero = spread_of(*where, carried, kernel_zero, "spread_0")
+    sent_zero = exchange(partial_zero, GY)
+    inner_zero, edges_zero = spread_of(*fetch, carried, kernel_zero, "spread_0")
     from_above, from_below = from_neighbours(edges_zero[1], edges_zero[0])
-    sent_one = exchange(partial_of(*where, upstream, *around, places))
-    refined = conv(*where, *around, kernel_one, "conv_1")
+    partial_one = partial_of(*where, upstream, *around, places, groups)
+    from_above, from_below, partial_one = after((from_above, from_below), partial_one)
+    sent_one = exchange(partial_one, GY)
+    refined = conv(*fetch, *around, kernel_one, "conv_1")
     back = inner_zero.at[0].add(from_above.astype(F32)).at[last].add(from_below.astype(F32))
     input_grad = (carried.astype(F32) + jnp.where(cells > 0, back, 0.0)).astype(BF16)
-    half = total_of(requested, sent_zero, banks, 0)
-    grad_banks = total_of(requested, sent_one, banks, 1, half)
+    half = total_of(requested, sent_zero, banks, 0, groups)
+    grad_banks = total_of(requested, sent_one, banks, 1, groups, half)
     return (jnp.transpose(refined, (1, 0, 2)), jnp.transpose(input_grad, (1, 0, 2)), grad_banks)
 
 
 def solution(mesh):
+    groups, devices = mesh.shape["groups"], mesh.shape["gy"]
+    cut = Mesh(mesh.devices.reshape(groups, devices // NEAR, NEAR), ALL)
     return jax.shard_map(
         body,
-        mesh=mesh,
+        mesh=cut,
         in_specs=(
-            P(None, ("groups", "gy"), None),
-            P(None, ("groups", "gy"), None),
-            P(None, "gy", None),
-            P(("groups", "gy"), None),
-            P(("groups", "gy"), None),
+            P(None, ALL, None),
+            P(None, ALL, None),
+            P(None, GY, None),
+            P(ALL, None),
+            P(ALL, None),
             P("groups"),
         ),
         out_specs=(
-            P(None, ("groups", "gy"), None),
-            P(None, ("groups", "gy"), None),
-            P("groups", "gy", None),
+            P(None, ALL, None),
+            P(None, ALL, None),
+            P("groups", GY, None),
         ),
         check_vma=False,
     )

time: 303 us -> 260 us (0.86)
  waiting for transfers between devices: 160 us -> 120 us
  starting transfers between devices: 45.2 us -> 61.2 us
  Pallas kernels: 62.8 us -> 49.7 us
  blocking collectives: 8.58 us -> 0 us
    all_to_all x4 -> x5, waiting for transfers between devices: 124 us -> 68.2 us  [exchange(): return lax.all_to_all(value, axes, split_axis=0, concat_axis=0, tiled=True)]
    ppermute x8 -> x14, waiting for transfers between devices: 35.4 us -> 52 us  [the longest x4 39.1 us: from_neighbours(): below = lax.ppermute(lower, GY, [(i + 1, i) for i in range(count - 1)])]
    ppermute x8 -> x14, starting transfers between devices: 24.6 us -> 34.9 us  [the longest x4 15.2 us: from_neighbours(): above = lax.ppermute(upper, GY, [(i, i + 1) for i in range(count - 1)])]
    all_to_all x1 -> x0, blocking collectives: 8.58 us -> none  [body(): lax.all_to_all(wanted, 'gy', split_axis=0, concat_axis=0, tiled=True)]
    pallas_call x6 -> x8, Pallas kernels: 35.7 us -> 29.8 us  [the longest x2 10.2 us: total_of(): pl.pallas_call(functools.partial(total_kernel, groups, per_dev, rows), gr...]
    all_to_all x4 -> x5, starting transfers between devices: 20.5 us -> 26.3 us  [exchange(): return lax.all_to_all(value, axes, split_axis=0, concat_axis=0, tiled=True)]
    pallas_call x2, Pallas kernels: 15.1 us -> 10.6 us  [spread_of(): pl.pallas_call(spread_kernel, out_shape=(jax.ShapeDtypeStruct(upstream.sh...]
    unnamed x59 -> x85, local copies, waits for them, and re-layouts: 20.7 us -> 20.3 us
  transfers between devices with their start and end apart: 12 -> 19, of which waited for: 5 -> 9; matrix products, arithmetic and copies ran while one was open for 2% -> 4% of each run, Pallas kernels for 17% -> 16%
where the time goes in v2:
time: 260 us; the launch traced here: 259 us
  waiting for transfers between devices  120 us (46%)
  starting transfers between devices  61.2 us (24%)
  Pallas kernels  49.7 us (19%)
  local copies, waits for them, and re-layouts  22.6 us (9%)
  other arithmetic  3.71 us (1%)
    all_to_all x5, waiting for transfers between devices, exchange(): return lax.all_to_all(value, axes, split_axis=0, concat_axis=0, tiled=True)  68.2 us
    ppermute x4, waiting for transfers between devices, from_neighbours(): below = lax.ppermute(lower, GY, [(i + 1, i) for i in range(count - 1)])  39.1 us
    all_to_all x5, starting transfers between devices, exchange(): return lax.all_to_all(value, axes, split_axis=0, concat_axis=0, tiled=True)  26.3 us
    unnamed x85, local copies, waits for them, and re-layouts  20.3 us
    ppermute x4, starting transfers between devices, from_neighbours(): above = lax.ppermute(upper, GY, [(i, i + 1) for i in range(count - 1)])  15.2 us
    ppermute x3, waiting for transfers between devices, body(): lax.ppermute(wire_zero, 'far', turn)  12.3 us
    pallas_call x2, Pallas kernels, spread_of(): pl.pallas_call(spread_kernel, out_shape=(jax.ShapeDtypeStruct(upstream.sh...  10.6 us
    ppermute x4, starting transfers between devices, from_neighbours(): below = lax.ppermute(lower, GY, [(i + 1, i) for i in range(count - 1)])  10.6 us
  transfers between devices with their start and end apart: 19, of which 9 were waited for; matrix products, arithmetic and copies ran while one was open for 4% of the time, Pallas kernels for 16%

profile of v2, /device:TPU:13, one launch (start us, length us, event | category | flops | bytes accessed | tf_op | source)
XLA Modules:
  0.0 258.7 jit_solution(13942279739316083148)
XLA Ops:
  3.4 2.3 collective-permute-start.1
  5.7 2.2 collective-permute-start
  10.8 5.4 %all-to-all-start = ((s32[32,1,10]{2,1,0:T(1,128)}), s32[32,1,10]{2,1,0:T(1,128)S(1)}, u32[]{:S(2)}, u32[]{:S(2)}) async-start(s32[32,1,10]{2,1,0:T(1,128)} %bitcast.5), calls=%async_computation | async-start | bytes 32768 | tf_op jit(solution)/shard_map/all_to_all | solution.py:453
  17.2 2.3 collective-permute-start.4
  19.5 4.2 %collective-permute-start.3 = (bf16[64,2048]{1,0:T(8,128)(2,1)S(1)}, bf16[64,2048]{1,0:T(8,128)(2,1)S(1)}, u32[]{:S(2)}, u32[]{:S(2)}) collective-permute-start(bf16[64,2048]{1,0:T(8,128)(2,1)S(1)} %get-tuple-element.87), channel_id=1, source_target_pairs={{0,1},{1,2},{2,3},{3,4},{4,5},{5,6},{6,7},{7,8},{8,9},{9,10},{10,1... | collective-permute-start | bytes 786440 | tf_op jit(solution)/shard_map/ppermute | solution.py:447
  23.7 8.4 %all-to-all-done = s32[32,1,10]{2,1,0:T(1,128)S(1)} async-done(((s32[32,1,10]{2,1,0:T(1,128)}), s32[32,1,10]{2,1,0:T(1,128)S(1)}, u32[]{:S(2)}, u32[]{:S(2)}) %all-to-all-start) | async-done | bytes 1312 | tf_op jit(solution)/shard_map/all_to_all | solution.py:453
  40.2 3.3 %pack_1.1 = bf16[64,144,128]{2,1,0:T(8,128)(2,1)S(1)} custom-call(s32[64]{0:T(128)S(1)} %get-tuple-element.89.step_of, s32[64]{0:T(128)S(1)} %get-tuple-element.88.row_of, bf16[8,144,128]{2,1,0:T(8,128)(2,1)S(1)} %wire_1.1.refs_0_, bf16[8,144,128]{2,1,0:T(8,128)(2,1)S(1)} %collective-permute-done.refs_1_, ...), custom_call_target="tpu_custom_call" | custom-call | flops 99999997952 | bytes 4718592 | tf_op jit(solution)/shard_map/pack_1/pallas_call | solution.py:121
  44.9 6.1 %all-to-all-start.2 = ((bf16[64,144,128]{2,1,0:T(8,128)(2,1)}), bf16[64,144,128]{2,1,0:T(8,128)(2,1)S(1)}, u32[]{:S(2)}, u32[]{:S(2)}) async-start(bf16[64,144,128]{2,1,0:T(8,128)(2,1)} %copy-done.11), calls=%async_computation.2 | async-start | bytes 4718592 | tf_op jit(solution)/shard_map/all_to_all | solution.py:453
  51.1 6.0 %collective-permute-done.6.refs_2_ = bf16[8,144,128]{2,1,0:T(8,128)(2,1)} collective-permute-done((bf16[8,144,128]{2,1,0:T(8,128)(2,1)S(1)}, bf16[8,144,128]{2,1,0:T(8,128)(2,1)}, u32[]{:S(2)}, u32[]{:S(2)}) %collective-permute-start.6) | collective-permute-done | bytes 294944 | tf_op jit(solution)/shard_map/ppermute | solution.py:498
  57.1 6.3 %collective-permute-done.5.refs_1_ = bf16[8,144,128]{2,1,0:T(8,128)(2,1)} collective-permute-done((bf16[8,144,128]{2,1,0:T(8,128)(2,1)S(1)}, bf16[8,144,128]{2,1,0:T(8,128)(2,1)}, u32[]{:S(2)}, u32[]{:S(2)}) %collective-permute-start.5) | collective-permute-done | bytes 294944 | tf_op jit(solution)/shard_map/ppermute | solution.py:498
  63.4 3.8 %pack_0.1 = bf16[64,144,128]{2,1,0:T(8,128)(2,1)S(1)} custom-call(s32[64]{0:T(128)S(1)} %get-tuple-element.89.step_of, s32[64]{0:T(128)S(1)} %get-tuple-element.88.row_of, bf16[8,144,128]{2,1,0:T(8,128)(2,1)S(1)} %wire_0.1.refs_0_, bf16[8,144,128]{2,1,0:T(8,128)(2,1)} %collective-permute-done.5.refs_1_, bf16[8,144,128]{2,1,0:T(8,128)(2,1)} %collective-permute-done.6.refs_2_, ...), custom_call_target="tpu_custom_call" | custom-call | flops 99999997952 | bytes 4718592 | tf_op jit(solution)/shard_map/pack_0/pallas_call | solution.py:121
  68.6 9.9 %all-to-all-done.2 = bf16[64,144,128]{2,1,0:T(8,128)(2,1)S(1)} async-done(((bf16[64,144,128]{2,1,0:T(8,128)(2,1)}), bf16[64,144,128]{2,1,0:T(8,128)(2,1)S(1)}, u32[]{:S(2)}, u32[]{:S(2)}) %all-to-all-start.2) | async-done | bytes 2359328 | tf_op jit(solution)/shard_map/all_to_all | solution.py:453
  78.5 5.3 %all-to-all-start.1 = ((bf16[64,144,128]{2,1,0:T(8,128)(2,1)}), bf16[64,144,128]{2,1,0:T(8,128)(2,1)}, u32[]{:S(2)}, u32[]{:S(2)}) async-start(bf16[64,144,128]{2,1,0:T(8,128)(2,1)} %copy-done.10), calls=%async_computation.1 | async-start | bytes 4718592 | tf_op jit(solution)/shard_map/all_to_all | solution.py:453
  85.3 4.7 %spread_1.1 = (f32[2,64,2048]{2,1,0:T(8,128)S(1)}, bf16[2,64,2048]{2,1,0:T(8,128)(2,1)S(1)}) custom-call(s32[32]{0:T(128)S(1)} %copy-done.28, s32[32]{0:T(128)S(1)} %reshape.233.listed, s32[2,2048]{1,0:T(2,128)S(1)} %copy-done.26, bf16[2,64,2048]{2,1,0:T(8,128)(2,1)S(1)} %bitcast.50, bf16[2,32,144,128]{3,2,1,0:T(8,128)(2,1)S(1)} %bitcast.45), custom_call_target="tpu_custom_call" | custom-call | flops 603979776 | bytes 5000000 | tf_op jit(solution)/shard_map/spread_1/pallas_call | solution.py:425
  92.6 2.3 collective-permute-start.11
  94.9 4.2 %collective-permute-start.10 = (bf16[64,2048]{1,0:T(8,128)(2,1)}, bf16[64,2048]{1,0:T(8,128)(2,1)}, u32[]{:S(2)}, u32[]{:S(2)}) collective-permute-start(bf16[64,2048]{1,0:T(8,128)(2,1)} %get-tuple-element.83), channel_id=1, source_target_pairs={{0,1},{1,2},{2,3},{3,4},{4,5},{5,6},{6,7},{7,8},{8,9},{9,10},{10,1... | collective-permute-start | bytes 786440 | tf_op jit(solution)/shard_map/ppermute | solution.py:447
  99.1 13.2 %all-to-all-done.1 = bf16[64,144,128]{2,1,0:T(8,128)(2,1)} async-done(((bf16[64,144,128]{2,1,0:T(8,128)(2,1)}), bf16[64,144,128]{2,1,0:T(8,128)(2,1)}, u32[]{:S(2)}, u32[]{:S(2)}) %all-to-all-start.1) | async-done | bytes 2359328 | tf_op jit(solution)/shard_map/all_to_all | solution.py:453
  114.2 5.3 %conv_0.1.hidden.middle = bf16[2,64,2048]{2,1,0:T(8,128)(2,1)S(1)} custom-call(s32[32]{0:T(128)S(1)} %copy-done.28, s32[32]{0:T(128)S(1)} %reshape.233.listed, s32[2,2048]{1,0:T(2,128)S(1)} %copy-done.26, bf16[64,2048]{1,0:T(8,128)(2,1)S(1)} %copy-done.25, bf16[2,64,2048]{2,1,0:T(8,128)(2,1)S(1)} %bitcast.48, bf16[64,2048]{1,0:T(8,128)(2,1)S(1)} %copy-done.23, ...), custom_call_target="tpu_custom_call" | custom-call | flops 603979776 | bytes 5000000 | tf_op jit(solution)/shard_map/conv_0/pallas_call | solution.py:280
  119.5 3.8 %collective-permute-start.9 = (bf16[64,2048]{1,0:T(8,128)(2,1)S(1)}, bf16[64,2048]{1,0:T(8,128)(2,1)S(1)}, u32[]{:S(2)}, u32[]{:S(2)}) collective-permute-start(bf16[64,2048]{1,0:T(8,128)(2,1)S(1)} %get-tuple-element.84), channel_id=1, source_target_pairs={{1,0},{2,1},{3,2},{4,3},{5,4},{6,5},{7,6},{8,7},{9,8},{10,9},{11,1... | collective-permute-start | bytes 786440 | tf_op jit(solution)/shard_map/ppermute | solution.py:448
  123.4 2.6 %collective-permute-start.8 = (bf16[64,2048]{1,0:T(8,128)(2,1)S(1)}, bf16[64,2048]{1,0:T(8,128)(2,1)S(1)}, u32[]{:S(2)}, u32[]{:S(2)}) collective-permute-start(bf16[64,2048]{1,0:T(8,128)(2,1)S(1)} %get-tuple-element.85), channel_id=1, source_target_pairs={{0,1},{1,2},{2,3},{3,4},{4,5},{5,6},{6,7},{7,8},{8,9},{9,10},{10,1... | collective-permute-start | bytes 786440 | tf_op jit(solution)/shard_map/ppermute | solution.py:447
  126.1 5.5 %carried_partial_0.1 = (bf16[2,64,2048]{2,1,0:T(8,128)(2,1)S(1)}, bf16[32,288,128]{2,1,0:T(8,128)(2,1)S(1)}) custom-call(s32[32]{0:T(128)S(1)} %copy-done.30, s32[32]{0:T(128)S(1)} %reshape.233.listed, s32[2,2048]{1,0:T(2,128)S(1)} %copy-done.26, bf16[2,64,2048]{2,1,0:T(8,128)(2,1)S(1)} %bitcast.51, bf16[2,64,2048]{2,1,0:T(8,128)(2,1)S(1)} %conv_0.1.hidden.middle, ...), custom_call_target="tpu_custom_call" | custom-call | flops 603979776 | bytes 7000000 | tf_op jit(solution)/shard_map/carried_partial_0/pallas_call | solution.py:364
  135.2 4.9 %all-to-all-start.4 = ((bf16[32,288,128]{2,1,0:T(8,128)(2,1)}), bf16[32,288,128]{2,1,0:T(8,128)(2,1)}, u32[]{:S(2)}, u32[]{:S(2)}) async-start(bf16[32,288,128]{2,1,0:T(8,128)(2,1)} %copy-done.9), calls=%async_computation.4 | async-start | bytes 4718592 | tf_op jit(solution)/shard_map/all_to_all | solution.py:453
  140.1 5.9 %spread_0.1 = (f32[2,64,2048]{2,1,0:T(8,128)S(1)}, bf16[2,64,2048]{2,1,0:T(8,128)(2,1)S(1)}) custom-call(s32[32]{0:T(128)S(1)} %copy-done.28, s32[32]{0:T(128)S(1)} %reshape.233.listed, s32[2,2048]{1,0:T(2,128)S(1)} %copy-done.26, bf16[2,64,2048]{2,1,0:T(8,128)(2,1)S(1)} %copy-done.13, bf16[2,32,144,128]{3,2,1,0:T(8,128)(2,1)} %bitcast.8.kernels), custom_call_target="tpu_custom_call" | custom-call | flops 603979776 | bytes 5000000 | tf_op jit(solution)/shard_map/spread_0/pallas_call | solution.py:425
  146.1 2.3 collective-permute-start.13
  148.3 4.2 %collective-permute-start.12 = (bf16[64,2048]{1,0:T(8,128)(2,1)S(1)}, bf16[64,2048]{1,0:T(8,128)(2,1)}, u32[]{:S(2)}, u32[]{:S(2)}) collective-permute-start(bf16[64,2048]{1,0:T(8,128)(2,1)S(1)} %get-tuple-element.81), channel_id=1, source_target_pairs={{0,1},{1,2},{2,3},{3,4},{4,5},{5,6},{6,7},{7,8},{8,9},{9,10},{10,1... | collective-permute-start | bytes 786440 | tf_op jit(solution)/shard_map/ppermute | solution.py:447
  152.6 4.7 %partial_1.1 = bf16[32,288,128]{2,1,0:T(8,128)(2,1)S(1)} custom-call(s32[32]{0:T(128)S(1)} %copy-done.30, s32[32]{0:T(128)S(1)} %reshape.233.listed, s32[2,2048]{1,0:T(2,128)S(1)} %copy-done.26, bf16[2,64,2048]{2,1,0:T(8,128)(2,1)S(1)} %bitcast.52, bf16[64,2048]{1,0:T(8,128)(2,1)S(1)} %copy-done.18, bf16[2,64,2048]{2,1,0:T(8,128)(2,1)S(1)} %conv_0.1.hidden.middle, ...), custom_call_target="tpu_custom_call" | custom-call | flops 603979776 | bytes 5000000 | tf_op jit(solution)/shard_map/partial_1/pallas_call | solution.py:322
  158.6 37.3 %collective-permute-done.13 = bf16[64,2048]{1,0:T(8,128)(2,1)} collective-permute-done((bf16[64,2048]{1,0:T(8,128)(2,1)S(1)}, bf16[64,2048]{1,0:T(8,128)(2,1)}, u32[]{:S(2)}, u32[]{:S(2)}) %collective-permute-start.13) | collective-permute-done | bytes 262176 | tf_op jit(solution)/shard_map/ppermute | solution.py:448
  196.0 4.5 %all-to-all-start.3 = ((bf16[32,288,128]{2,1,0:T(8,128)(2,1)}), bf16[32,288,128]{2,1,0:T(8,128)(2,1)}, u32[]{:S(2)}, u32[]{:S(2)}) async-start(bf16[32,288,128]{2,1,0:T(8,128)(2,1)} %copy-done.1), calls=%async_computation.3 | async-start | bytes 4718592 | tf_op jit(solution)/shard_map/all_to_all | solution.py:453
  202.6 4.0 %conv_1.1 = bf16[2,64,2048]{2,1,0:T(8,128)(2,1)S(1)} custom-call(s32[32]{0:T(128)S(1)} %copy-done.28, s32[32]{0:T(128)S(1)} %reshape.233.listed, s32[2,2048]{1,0:T(2,128)S(1)} %copy-done.26, bf16[64,2048]{1,0:T(8,128)(2,1)S(1)} %copy-done.19, bf16[2,64,2048]{2,1,0:T(8,128)(2,1)S(1)} %conv_0.1.hidden.middle, bf16[64,2048]{1,0:T(8,128)(2,1)S(1)} %copy-done.16, ...), custom_call_target="tpu_custom_call" | custom-call | flops 603979776 | bytes 5000000 | tf_op jit(solution)/shard_map/conv_1/pallas_call | solution.py:280
  211.7 5.1 %total_0.1.rest_0_ = f32[2,8,36864]{2,1,0:T(8,128)} custom-call(s32[32]{0:T(128)S(1)} %reshape.241.requested, bf16[32,288,128]{2,1,0:T(8,128)(2,1)} %all-to-all-done.4.parts), custom_call_target="tpu_custom_call" | custom-call | flops 1000000 | bytes 3538944 | tf_op jit(solution)/shard_map/total_0/pallas_call | solution.py:172
  216.9 36.7 %all-to-all-done.3.parts = bf16[32,288,128]{2,1,0:T(8,128)(2,1)} async-done(((bf16[32,288,128]{2,1,0:T(8,128)(2,1)}), bf16[32,288,128]{2,1,0:T(8,128)(2,1)}, u32[]{:S(2)}, u32[]{:S(2)}) %all-to-all-start.3) | async-done | bytes 2359328 | tf_op jit(solution)/shard_map/all_to_all | solution.py:453
  253.6 5.1 %total_1.1 = f32[2,8,36864]{2,1,0:T(8,128)} custom-call(s32[32]{0:T(128)S(1)} %reshape.241.requested, bf16[32,288,128]{2,1,0:T(8,128)(2,1)} %all-to-all-done.3.parts, f32[2,8,36864]{2,1,0:T(8,128)} %total_0.1.rest_0_), custom_call_target="tpu_custom_call", output_to_operand_aliasing={{}: (2, {})} | custom-call | flops 1000000 | bytes 3538944 | tf_op jit(solution)/shard_map/total_1/pallas_call | solution.py:172
  (132 shorter events, 35.6 us)
Async XLA Ops:
  1.9 14.3 %copy-start.33 = (bf16[64,2,2048]{2,1,0:T(2,128)(2,1)S(1)}, bf16[64,2,2048]{2,1,0:T(2,128)(2,1)}, u32[]{:S(2)}) copy-start(bf16[64,2,2048]{2,1,0:T(2,128)(2,1)} %param.10) | copy-start | bytes 1572868
  3.1 31.6 %copy-start.32 = (bf16[2,8,36864]{2,1,0:T(8,128)(2,1)S(1)}, bf16[2,8,36864]{2,1,0:T(8,128)(2,1)}, u32[]{:S(2)}) copy-start(bf16[2,8,36864]{2,1,0:T(8,128)(2,1)} %banks.3) | copy-start | bytes 3538948
  3.1 31.5 %collective-permute-start.2 = (bf16[8,144,128]{2,1,0:T(8,128)(2,1)S(1)}, bf16[8,144,128]{2,1,0:T(8,128)(2,1)S(1)}, u32[]{:S(2)}, u32[]{:S(2)}) collective-permute-start(bf16[8,144,128]{2,1,0:T(8,128)(2,1)S(1)} %wire_1.1.refs_0_), channel_id=1, source_target_pairs={{0,12},{4,0},{8,4},{12,8},{1,13},{5,1},{9,5},{13,9},{2,14},{6,2},{... | collective-permute-start | bytes 884744 | tf_op jit(solution)/shard_map/ppermute | solution.py:494
  3.4 31.3 %collective-permute-start.1 = (bf16[8,144,128]{2,1,0:T(8,128)(2,1)S(1)}, bf16[8,144,128]{2,1,0:T(8,128)(2,1)S(1)}, u32[]{:S(2)}, u32[]{:S(2)}) collective-permute-start(bf16[8,144,128]{2,1,0:T(8,128)(2,1)S(1)} %wire_1.1.refs_0_), channel_id=1, source_target_pairs={{0,8},{4,12},{8,0},{12,4},{1,9},{5,13},{9,1},{13,5},{2,10},{6,14},... | collective-permute-start | bytes 884744 | tf_op jit(solution)/shard_map/ppermute | solution.py:494
  5.7 29.0 %collective-permute-start = (bf16[8,144,128]{2,1,0:T(8,128)(2,1)S(1)}, bf16[8,144,128]{2,1,0:T(8,128)(2,1)S(1)}, u32[]{:S(2)}, u32[]{:S(2)}) collective-permute-start(bf16[8,144,128]{2,1,0:T(8,128)(2,1)S(1)} %wire_1.1.refs_0_), channel_id=1, source_target_pairs={{0,4},{4,8},{8,12},{12,0},{1,5},{5,9},{9,13},{13,1},{2,6},{6,10},{... | collective-permute-start | bytes 884744 | tf_op jit(solution)/shard_map/ppermute | solution.py:494
  7.9 27.9 %copy-start.35 = (s32[16,2]{1,0:T(8,128)}, s32[16,2]{1,0:T(8,128)S(1)}, u32[]{:S(2)}) copy-start(s32[16,2]{1,0:T(8,128)S(1)} %copy.28) | copy-start | bytes 388
  10.8 21.3 %all-to-all-start = ((s32[32,1,10]{2,1,0:T(1,128)}), s32[32,1,10]{2,1,0:T(1,128)S(1)}, u32[]{:S(2)}, u32[]{:S(2)}) async-start(s32[32,1,10]{2,1,0:T(1,128)} %bitcast.5), calls=%async_computation | async-start | bytes 32768 | tf_op jit(solution)/shard_map/all_to_all | solution.py:453
  17.2 16.8 %collective-permute-start.4 = (bf16[64,2048]{1,0:T(8,128)(2,1)S(1)}, bf16[64,2048]{1,0:T(8,128)(2,1)S(1)}, u32[]{:S(2)}, u32[]{:S(2)}) collective-permute-start(bf16[64,2048]{1,0:T(8,128)(2,1)S(1)} %get-tuple-element.86), channel_id=1, source_target_pairs={{1,0},{2,1},{3,2},{4,3},{5,4},{6,5},{7,6},{8,7},{9,8},{10,9},{11,1... | collective-permute-start | bytes 786440 | tf_op jit(solution)/shard_map/ppermute | solution.py:448
  19.5 15.2 %collective-permute-start.3 = (bf16[64,2048]{1,0:T(8,128)(2,1)S(1)}, bf16[64,2048]{1,0:T(8,128)(2,1)S(1)}, u32[]{:S(2)}, u32[]{:S(2)}) collective-permute-start(bf16[64,2048]{1,0:T(8,128)(2,1)S(1)} %get-tuple-element.87), channel_id=1, source_target_pairs={{0,1},{1,2},{2,3},{3,4},{4,5},{5,6},{6,7},{7,8},{8,9},{9,10},{10,1... | collective-permute-start | bytes 786440 | tf_op jit(solution)/shard_map/ppermute | solution.py:447
  35.9 15.2 %collective-permute-start.7 = (bf16[8,144,128]{2,1,0:T(8,128)(2,1)S(1)}, bf16[8,144,128]{2,1,0:T(8,128)(2,1)S(1)}, u32[]{:S(2)}, u32[]{:S(2)}) collective-permute-start(bf16[8,144,128]{2,1,0:T(8,128)(2,1)S(1)} %wire_0.1.refs_0_), channel_id=1, source_target_pairs={{0,12},{4,0},{8,4},{12,8},{1,13},{5,1},{9,5},{13,9},{2,14},{6,2},{... | collective-permute-start | bytes 884744 | tf_op jit(solution)/shard_map/ppermute | solution.py:498
  36.3 20.8 %collective-permute-start.6 = (bf16[8,144,128]{2,1,0:T(8,128)(2,1)S(1)}, bf16[8,144,128]{2,1,0:T(8,128)(2,1)}, u32[]{:S(2)}, u32[]{:S(2)}) collective-permute-start(bf16[8,144,128]{2,1,0:T(8,128)(2,1)S(1)} %wire_0.1.refs_0_), channel_id=1, source_target_pairs={{0,8},{4,12},{8,0},{12,4},{1,9},{5,13},{9,1},{13,5},{2,10},{6,14},... | collective-permute-start | bytes 884744 | tf_op jit(solution)/shard_map/ppermute | solution.py:498
  38.3 25.2 %collective-permute-start.5 = (bf16[8,144,128]{2,1,0:T(8,128)(2,1)S(1)}, bf16[8,144,128]{2,1,0:T(8,128)(2,1)}, u32[]{:S(2)}, u32[]{:S(2)}) collective-permute-start(bf16[8,144,128]{2,1,0:T(8,128)(2,1)S(1)} %wire_0.1.refs_0_), channel_id=1, source_target_pairs={{0,4},{4,8},{8,12},{12,0},{1,5},{5,9},{9,13},{13,1},{2,6},{6,10},{... | collective-permute-start | bytes 884744 | tf_op jit(solution)/shard_map/ppermute | solution.py:498
  44.9 33.6 %all-to-all-start.2 = ((bf16[64,144,128]{2,1,0:T(8,128)(2,1)}), bf16[64,144,128]{2,1,0:T(8,128)(2,1)S(1)}, u32[]{:S(2)}, u32[]{:S(2)}) async-start(bf16[64,144,128]{2,1,0:T(8,128)(2,1)} %copy-done.11), calls=%async_computation.2 | async-start | bytes 4718592 | tf_op jit(solution)/shard_map/all_to_all | solution.py:453
  68.6 15.3 %copy-start.36 = (s32[16,2]{1,0:T(8,128)S(1)}, s32[16,2]{1,0:T(8,128)}, u32[]{:S(2)}) copy-start(s32[16,2]{1,0:T(8,128)} %copy-done.35) | copy-start | bytes 388
  68.6 16.6 %copy-start.26 = (s32[2,2048]{1,0:T(2,128)S(1)}, s32[2,2048]{1,0:T(2,128)}, u32[]{:S(2)}) copy-start(s32[2,2048]{1,0:T(2,128)} %regions.11) | copy-start | bytes 49156
  68.6 16.6 %copy-start.28 = (s32[32]{0:T(128)S(1)}, s32[32]{0:T(128)}, u32[]{:S(2)}) copy-start(s32[32]{0:T(128)} %copy-done.27) | copy-start | bytes 388
  78.5 33.8 %all-to-all-start.1 = ((bf16[64,144,128]{2,1,0:T(8,128)(2,1)}), bf16[64,144,128]{2,1,0:T(8,128)(2,1)}, u32[]{:S(2)}, u32[]{:S(2)}) async-start(bf16[64,144,128]{2,1,0:T(8,128)(2,1)} %copy-done.10), calls=%async_computation.1 | async-start | bytes 4718592 | tf_op jit(solution)/shard_map/all_to_all | solution.py:453
  84.0 28.3 %copy-start.3 = (bf16[64,2,2048]{2,0,1:T(8,128)(2,1)S(1)}, bf16[64,2,2048]{2,0,1:T(8,128)(2,1)}, u32[]{:S(2)}) copy-start(bf16[64,2,2048]{2,0,1:T(8,128)(2,1)} %copy-done.2) | copy-start | bytes 1572868
  92.6 33.4 %collective-permute-start.11 = (bf16[64,2048]{1,0:T(8,128)(2,1)}, bf16[64,2048]{1,0:T(8,128)(2,1)}, u32[]{:S(2)}, u32[]{:S(2)}) collective-permute-start(bf16[64,2048]{1,0:T(8,128)(2,1)} %get-tuple-element.82), channel_id=1, source_target_pairs={{1,0},{2,1},{3,2},{4,3},{5,4},{6,5},{7,6},{8,7},{9,8},{10,9},{11,1... | collective-permute-start | bytes 786440 | tf_op jit(solution)/shard_map/ppermute | solution.py:448
  94.9 31.1 %collective-permute-start.10 = (bf16[64,2048]{1,0:T(8,128)(2,1)}, bf16[64,2048]{1,0:T(8,128)(2,1)}, u32[]{:S(2)}, u32[]{:S(2)}) collective-permute-start(bf16[64,2048]{1,0:T(8,128)(2,1)} %get-tuple-element.83), channel_id=1, source_target_pairs={{0,1},{1,2},{2,3},{3,4},{4,5},{5,6},{6,7},{7,8},{8,9},{9,10},{10,1... | collective-permute-start | bytes 786440 | tf_op jit(solution)/shard_map/ppermute | solution.py:447
  114.2 11.8 %copy-start.21 = (f32[2,64,2048]{2,1,0:T(8,128)S(1)}, f32[2,64,2048]{2,1,0:T(8,128)}, u32[]{:S(2)}) copy-start(f32[2,64,2048]{2,1,0:T(8,128)} %copy-done.20) | copy-start | bytes 3145732
  114.2 11.8 %copy-start.30 = (s32[32]{0:T(128)S(1)}, s32[32]{0:T(128)}, u32[]{:S(2)}) copy-start(s32[32]{0:T(128)} %copy-done.29) | copy-start | bytes 388
  119.5 14.2 %collective-permute-start.9 = (bf16[64,2048]{1,0:T(8,128)(2,1)S(1)}, bf16[64,2048]{1,0:T(8,128)(2,1)S(1)}, u32[]{:S(2)}, u32[]{:S(2)}) collective-permute-start(bf16[64,2048]{1,0:T(8,128)(2,1)S(1)} %get-tuple-element.84), channel_id=1, source_target_pairs={{1,0},{2,1},{3,2},{4,3},{5,4},{6,5},{7,6},{8,7},{9,8},{10,9},{11,1... | collective-permute-start | bytes 786440 | tf_op jit(solution)/shard_map/ppermute | solution.py:448
  123.4 11.1 %collective-permute-start.8 = (bf16[64,2048]{1,0:T(8,128)(2,1)S(1)}, bf16[64,2048]{1,0:T(8,128)(2,1)S(1)}, u32[]{:S(2)}, u32[]{:S(2)}) collective-permute-start(bf16[64,2048]{1,0:T(8,128)(2,1)S(1)} %get-tuple-element.85), channel_id=1, source_target_pairs={{0,1},{1,2},{2,3},{3,4},{4,5},{5,6},{6,7},{7,8},{8,9},{9,10},{10,1... | collective-permute-start | bytes 786440 | tf_op jit(solution)/shard_map/ppermute | solution.py:447
  135.2 60.8 %all-to-all-start.4 = ((bf16[32,288,128]{2,1,0:T(8,128)(2,1)}), bf16[32,288,128]{2,1,0:T(8,128)(2,1)}, u32[]{:S(2)}, u32[]{:S(2)}) async-start(bf16[32,288,128]{2,1,0:T(8,128)(2,1)} %copy-done.9), calls=%async_computation.4 | async-start | bytes 4718592 | tf_op jit(solution)/shard_map/all_to_all | solution.py:453
  140.0 12.5 %copy-start.6 = (bf16[64,2,2048]{2,0,1:T(8,128)(2,1)S(1)}, bf16[64,2,2048]{2,0,1:T(8,128)(2,1)}, u32[]{:S(2)}) copy-start(bf16[64,2,2048]{2,0,1:T(8,128)(2,1)} %copy-done.4) | copy-start | bytes 1572868
  140.0 12.5 %copy-start.15 = (bf16[64,2048]{1,0:T(8,128)(2,1)S(1)}, bf16[64,2048]{1,0:T(8,128)(2,1)}, u32[]{:S(2)}) copy-start(bf16[64,2048]{1,0:T(8,128)(2,1)} %copy-done.14) | copy-start | bytes 786436
  140.0 12.5 %copy-start.18 = (bf16[64,2048]{1,0:T(8,128)(2,1)S(1)}, bf16[64,2048]{1,0:T(8,128)(2,1)}, u32[]{:S(2)}) copy-start(bf16[64,2048]{1,0:T(8,128)(2,1)} %copy-done.17) | copy-start | bytes 786436
  146.1 49.9 %collective-permute-start.13 = (bf16[64,2048]{1,0:T(8,128)(2,1)S(1)}, bf16[64,2048]{1,0:T(8,128)(2,1)}, u32[]{:S(2)}, u32[]{:S(2)}) collective-permute-start(bf16[64,2048]{1,0:T(8,128)(2,1)S(1)} %get-tuple-element.80), channel_id=1, source_target_pairs={{1,0},{2,1},{3,2},{4,3},{5,4},{6,5},{7,6},{8,7},{9,8},{10,9},{11,1... | collective-permute-start | bytes 786440 | tf_op jit(solution)/shard_map/ppermute | solution.py:448
  148.3 47.6 %collective-permute-start.12 = (bf16[64,2048]{1,0:T(8,128)(2,1)S(1)}, bf16[64,2048]{1,0:T(8,128)(2,1)}, u32[]{:S(2)}, u32[]{:S(2)}) collective-permute-start(bf16[64,2048]{1,0:T(8,128)(2,1)S(1)} %get-tuple-element.81), channel_id=1, source_target_pairs={{0,1},{1,2},{2,3},{3,4},{4,5},{5,6},{6,7},{7,8},{8,9},{9,10},{10,1... | collective-permute-start | bytes 786440 | tf_op jit(solution)/shard_map/ppermute | solution.py:447
  158.6 41.9 %copy-start.38 = (s32[32,1,10]{2,1,0:T(1,128)S(1)}, s32[32,1,10]{2,1,0:T(1,128)}, u32[]{:S(2)}) copy-start(s32[32,1,10]{2,1,0:T(1,128)} %copy-done.37) | copy-start | bytes 3844
  196.0 57.6 %all-to-all-start.3 = ((bf16[32,288,128]{2,1,0:T(8,128)(2,1)}), bf16[32,288,128]{2,1,0:T(8,128)(2,1)}, u32[]{:S(2)}, u32[]{:S(2)}) async-start(bf16[32,288,128]{2,1,0:T(8,128)(2,1)} %copy-done.1), calls=%async_computation.3 | async-start | bytes 4718592 | tf_op jit(solution)/shard_map/all_to_all | solution.py:453
  (27 other events, 65.1 us)

commit v3 on v2

--- a/solution.py
+++ b/solution.py
@@ -55,7 +55,8 @@
     return lax.broadcasted_iota(jnp.int32, tile.shape, 1) < LANES // 2
 
 
-def wire_kernel(parts, per_dev, rows, own_part, banks, out, natural, travel):
+def wire_kernel(parts, per_dev, rows, own_part, banks, *rest):
+    outs, (natural, travel) = rest[:-2], rest[-2:]
     for part in range(parts):
 
         @pl.when(own_part[0] == part)
@@ -81,67 +82,66 @@
                 for order, pair in enumerate(pairs):
                     blend(64 * pair, 64 * pair + 32, 64 * order, 32)
                 blend(256 + part * half, 272 + part * half, 64 * len(pairs), half)
-                out[row] = travel[...].astype(BF16)
-
-
-def wire(own_part, banks, layer, parts):
+                start = 0
+                for out in outs:
+                    out[row] = travel[start : start + out.shape[1], :].astype(BF16)
+                    start += out.shape[1]
+
+
+def wire(own_part, banks, layer, parts, sizes):
     layers, per_dev, width = banks.shape
     rows = width // LANES
     return pl.pallas_call(
         functools.partial(wire_kernel, parts, per_dev, rows),
         grid=(1,),
-        out_shape=jax.ShapeDtypeStruct((per_dev, part_rows(parts), LANES), BF16),
+        out_shape=[jax.ShapeDtypeStruct((per_dev, size, LANES), BF16) for size in sizes],
         in_specs=[SMEM, pl.BlockSpec((1, per_dev, width), lambda step: (layer, 0, 0))],
-        out_specs=pl.BlockSpec((per_dev, part_rows(parts), LANES), lambda step: (0, 0, 0)),
+        out_specs=[pl.BlockSpec((per_dev, size, LANES), lambda step: (0, 0, 0)) for size in sizes],
         scratch_shapes=[
             pltpu.VMEM((per_dev * rows, LANES), F32),
             pltpu.VMEM((part_rows(parts), LANES), F32),
         ],
         compiler_params=params(24),
-        cost_estimate=cost(10**11, 4 * per_dev * width),
+        cost_estimate=cost(10**6, 4 * per_dev * width),
         name=f"wire_{layer}",
     )(own_part, banks)
 
 
-def pack_kernel(step_of, row_of, *refs):
+def pack_kernel(rows, *refs):
     buffers, out = refs[:-1], refs[-1]
-
-    @pl.loop(0, out.shape[0])
-    def _(place):
-        for step, buffer in enumerate(buffers):
-
-            @pl.when(step_of[place] == step)
-            def _(buffer=buffer):
-                out[place] = buffer[row_of[place]]
-
-
-def pack(step_of, row_of, buffers, name):
-    places = step_of.shape[0]
+    inner = rows.shape[1]
+    slots = inner // len(buffers)
+
+    @pl.loop(0, rows.shape[0])
+    def _(target):
+        for entry in range(inner):
+            out[target * inner + entry] = buffers[entry // slots][rows[target, entry]]
+
+
+def pack(rows, buffers, name):
+    targets, inner = rows.shape
     shape = buffers[0].shape[1:]
     return pl.pallas_call(
         pack_kernel,
-        out_shape=jax.ShapeDtypeStruct((places, *shape), BF16),
-        in_specs=[SMEM, SMEM] + [VMEM] * len(buffers),
+        out_shape=jax.ShapeDtypeStruct((targets * inner, *shape), BF16),
+        in_specs=[SMEM] + [VMEM] * len(buffers),
         out_specs=VMEM,
         compiler_params=params(32),
-        cost_estimate=cost(10**11, 4 * places * shape[0] * shape[1]),
+        cost_estimate=cost(10**11, 4 * targets * inner * shape[0] * shape[1]),
         name=name,
-    )(step_of, row_of, *buffers)
+    )(rows, *buffers)
 
 
 def total_kernel(groups, per_dev, rows, requested, parts, *rest):
     out, total, natural = rest[-3:]
     total[...] = jnp.zeros_like(total)
 
-    @pl.loop(0, parts.shape[0])
+    @pl.loop(0, parts.shape[0], unroll=4)
     def _(place):
-        row = requested[place]
-
-        @pl.when(row >= 0)
-        def _():
-            total[pl.ds(pl.multiple_of(row * rows, 8), rows), :] += parts[place].astype(F32)
-
-    @pl.loop(0, per_dev)
+        row = jnp.where(requested[place] < 0, per_dev, requested[place])
+        total[pl.ds(pl.multiple_of(row * rows, 8), rows), :] += parts[place].astype(F32)
+
+    @pl.loop(0, per_dev, unroll=2)
     def _(row):
         base = row * rows
 
@@ -176,7 +176,7 @@
         in_specs=specs,
         out_specs=pl.BlockSpec((1, per_dev, width), lambda step: (layer, 0, 0)),
         scratch_shapes=[
-            pltpu.VMEM((per_dev * rows, LANES), F32),
+            pltpu.VMEM(((per_dev + 1) * rows, LANES), F32),
             pltpu.VMEM((per_dev * rows, LANES), F32),
         ],
         input_output_aliases={2: 0} if earlier is not None else {},
@@ -209,6 +209,19 @@
             shifts[2, row, pl.ds(start, step), :] = right.astype(BF16)
 
 
+def shift(above, middle, below, name):
+    tile_rows, channels, columns = middle.shape
+    return pl.pallas_call(
+        fill_shifts,
+        out_shape=jax.ShapeDtypeStruct((3, tile_rows + 2, channels, columns), BF16),
+        in_specs=[VMEM] * 3,
+        out_specs=VMEM,
+        compiler_params=params(32),
+        cost_estimate=cost(10**7, 8 * tile_rows * channels * columns),
+        name=name,
+    )(above, middle, below)
+
+
 def band_slice(band):
     return pl.ds(pl.multiple_of(band * LANES, LANES), LANES)
 
@@ -222,15 +235,21 @@
     return jnp.concatenate(taps, axis=0)
 
 
-def band_weights(kernels, place_of, band):
-    parts = kernels.shape[0]
-    tail = 64 * pairs_of(parts)
+def band_weights(pieces, groups, place_of, band):
+    def rows_of(part, place, start, count):
+        for piece in pieces:
+            if start < piece.shape[2]:
+                return piece.at[part, place][start : start + count, :]
+            start -= piece.shape[2]
+
     wide, last = [], []
+    tail = 64 * pairs_of(groups)
     for slot in range(2):
-        ones = [kernels.at[part, place_of[2 * band + slot]] for part in range(parts)]
-        blocks = [one[start : start + 64, :] for one in ones for start in range(0, tail, 64)]
+        place = place_of[2 * band + slot]
+        blocks = [rows_of(part, place, start, 64) for part in range(groups) for start in range(0, tail, 64)]
         wide.append(jnp.concatenate(blocks, axis=1))
-        rest = jnp.concatenate([one[tail : tail + tail_of(parts), :] for one in ones], axis=0)
+        rest = [rows_of(part, place, tail, tail_of(groups)) for part in range(groups)]
+        rest = jnp.concatenate(rest, axis=0)
         last.extend([rest[:, :64], rest[:, 64:]])
     return jnp.concatenate(wide, axis=0), jnp.concatenate(last, axis=0)
 
@@ -258,14 +277,14 @@
     )
 
 
-def conv_kernel(position, listed, regions, above, middle, below, kernels, out, shifts):
+def conv_kernel(position, listed, regions, middle, shifts, *rest):
+    pieces, out = rest[:-1], rest[-1]
     tile_rows, channels, columns = middle.shape
-    fill_shifts(above, middle, below, shifts)
-
-    @pl.loop(0, columns // LANES, unroll=2)
+
+    @pl.loop(0, columns // LANES, unroll=4)
     def _(band):
         cells = unfolded(shifts, band, tile_rows)
-        wide, last = band_weights(kernels, position, band)
+        wide, last = band_weights(pieces, pieces[0].shape[0], position, band)
         both = dot(wide, cells[:512], 1, 0) + dot(last, cells[512:], 1, 0)
         mask = first_mask(regions, listed, band, channels, tile_rows)
         mixed = jnp.where(mask, both[:channels], both[channels:])
@@ -275,45 +294,49 @@
             out[row, :, band_slice(band)] = here.astype(BF16)
 
 
-def conv(position, listed, regions, above, middle, below, kernels, name):
+def conv(position, listed, regions, middle, shifts, kernels, name, room=32):
     tile_rows, channels, columns = middle.shape
     return pl.pallas_call(
         conv_kernel,
         out_shape=jax.ShapeDtypeStruct(middle.shape, BF16),
-        in_specs=[SMEM, SMEM] + [VMEM] * 5,
+        in_specs=[SMEM, SMEM] + [VMEM] * (3 + len(kernels)),
         out_specs=VMEM,
-        scratch_shapes=[pltpu.VMEM((3, tile_rows + 2, channels, columns), BF16)],
-        compiler_params=params(32),
+        compiler_params=params(room),
         cost_estimate=cost(4 * 9 * channels * channels * columns * tile_rows, 5000000),
         name=name,
-    )(position, listed, regions, above, middle, below, kernels)
-
-
-def partial_bands(groups, position, listed, regions, upstream, shifts, out):
+    )(position, listed, regions, middle, shifts, *kernels)
+
+
+def store_rows(out, band, cells):
+    for row in range(out.shape[0]):
+        out[row, :, band_slice(band)] = cells[:, row * LANES : (row + 1) * LANES]
+
+
+def store_partial(groups, position, band, upstream, cells, mask, out):
+    channels = upstream.shape[0]
+    sums = dot(masked(upstream, mask), cells, 1, 1).astype(BF16)
+    for slot in range(2):
+        mine = sums[channels * slot : channels * (slot + 1)]
+        there = out.at[position[2 * band + slot]]
+        for pair in range(4):
+            start = pair_start(pair, groups)
+            there[start : start + 64, :] = mine[:, LANES * pair : LANES * (pair + 1)]
+        rest = jnp.concatenate([mine[:32, 512:], mine[32:, 512:]], axis=1)
+        size = tail_of(groups)
+        for part in range(groups):
+            start = tail_start(part, groups)
+            there[start : start + size, :] = rest[size * part : size * (part + 1)]
+
+
+def partial_kernel(groups, position, listed, regions, upstream, above, middle, below, out, shifts):
     tile_rows, channels, columns = upstream.shape
-
-    @pl.loop(0, columns // LANES, unroll=2)
+    fill_shifts(above, middle, below, shifts)
+
+    @pl.loop(0, columns // LANES, unroll=4)
     def _(band):
         cells = unfolded(shifts, band, tile_rows)
         mask = first_mask(regions, listed, band, channels, tile_rows)
-        both = masked(side_by_side(upstream, band, tile_rows), mask)
-        sums = dot(both, cells, 1, 1).astype(BF16)
-        for slot in range(2):
-            mine = sums[channels * slot : channels * (slot + 1)]
-            there = out.at[position[2 * band + slot]]
-            for pair in range(4):
-                start = pair_start(pair, groups)
-                there[start : start + 64, :] = mine[:, LANES * pair : LANES * (pair + 1)]
-            rest = jnp.concatenate([mine[:32, 512:], mine[32:, 512:]], axis=1)
-            size = tail_of(groups)
-            for part in range(groups):
-                start = tail_start(part, groups)
-                there[start : start + size, :] = rest[size * part : size * (part + 1)]
-
-
-def partial_kernel(groups, position, listed, regions, upstream, above, middle, below, out, shifts):
-    fill_shifts(above, middle, below, shifts)
-    partial_bands(groups, position, listed, regions, upstream, shifts, out)
+        store_partial(groups, position, band, side_by_side(upstream, band, tile_rows), cells, mask, out)
 
 
 def partial_of(position, listed, regions, upstream, above, middle, below, places, groups):
@@ -321,71 +344,69 @@
     rows = 9 * channels * channels // LANES
     return pl.pallas_call(
         functools.partial(partial_kernel, groups),
-        out_shape=jax.ShapeDtypeStruct((places, rows, LANES), BF16),
+        out_shape=(
+            jax.ShapeDtypeStruct((places, rows, LANES), BF16),
+            jax.ShapeDtypeStruct((3, tile_rows + 2, channels, columns), BF16),
+        ),
         in_specs=[SMEM, SMEM] + [VMEM] * 5,
-        out_specs=VMEM,
-        scratch_shapes=[pltpu.VMEM((3, tile_rows + 2, channels, columns), BF16)],
-        compiler_params=params(32),
-        cost_estimate=cost(4 * 9 * channels * channels * columns * tile_rows, 5000000),
+        out_specs=(VMEM, VMEM),
+        compiler_params=params(56),
+        cost_estimate=cost(4 * 9 * channels * channels * columns * tile_rows, 8000000),
         name="partial_1",
     )(position, listed, regions, upstream, above, middle, below)
 
 
 def carried_kernel(
-    groups, position, listed, regions, cotangent, hidden, inner, from_above, from_below, above, middle, below,
-    carried, out, shifts,
+    groups, position, listed, regions, cotangent, hidden, inner, from_above, from_below, shifts, carried, out
 ):
-    tile_rows, channels, columns = middle.shape
-    fill_shifts(above, middle, below, shifts)
-    step = 16
-
-    @pl.loop(0, channels // step)
-    def _(group):
-        here = pl.ds(pl.multiple_of(group * step, step), step)
+    tile_rows, channels, columns = hidden.shape
+
+    @pl.loop(0, columns // LANES, unroll=4)
+    def _(band):
+        cells = unfolded(shifts, band, tile_rows)
+        mask = first_mask(regions, listed, band, channels, tile_rows)
+        back = []
         for row in range(tile_rows):
-            back = inner[row, here, :]
+            value = inner[row, :, band_slice(band)]
             if row == 0:
-                back = back + from_above[here, :].astype(F32)
+                value = value + from_above[:, band_slice(band)].astype(F32)
             if row == tile_rows - 1:
-                back = back + from_below[here, :].astype(F32)
-            keep = hidden[row, here, :].astype(F32) > 0.0
-            value = cotangent[row, here, :].astype(F32) + jnp.where(keep, back, 0.0)
-            carried[row, here, :] = value.astype(BF16)
-
-    partial_bands(groups, position, listed, regions, carried, shifts, out)
+                value = value + from_below[:, band_slice(band)].astype(F32)
+            back.append(value)
+        keep = side_by_side(hidden, band, tile_rows).astype(F32) > 0.0
+        back = jnp.where(keep, jnp.concatenate(back, axis=1), 0.0)
+        upstream = (side_by_side(cotangent, band, tile_rows).astype(F32) + back).astype(BF16)
+        store_rows(carried, band, upstream)
+        store_partial(groups, position, band, upstream, cells, mask, out)
 
 
 def carried_of(
-    position, listed, regions, cotangent, hidden, inner, from_above, from_below, above, middle, below,
-    places, groups,
+    position, listed, regions, cotangent, hidden, inner, from_above, from_below, shifts, places, groups
 ):
-    tile_rows, channels, columns = middle.shape
+    tile_rows, channels, columns = hidden.shape
     rows = 9 * channels * channels // LANES
     return pl.pallas_call(
         functools.partial(carried_kernel, groups),
         out_shape=(
-            jax.ShapeDtypeStruct(middle.shape, BF16),
+            jax.ShapeDtypeStruct(hidden.shape, BF16),
             jax.ShapeDtypeStruct((places, rows, LANES), BF16),
         ),
-        in_specs=[SMEM, SMEM] + [VMEM] * 9,
+        in_specs=[SMEM, SMEM] + [VMEM] * 7,
         out_specs=(VMEM, VMEM),
-        scratch_shapes=[pltpu.VMEM((3, tile_rows + 2, channels, columns), BF16)],
         compiler_params=params(32),
         cost_estimate=cost(4 * 9 * channels * channels * columns * tile_rows, 7000000),
         name="carried_partial_0",
-    )(
-        position, listed, regions, cotangent, hidden, inner, from_above, from_below, above, middle,
-        below,
-    )
-
-
-def spread_kernel(position, listed, regions, upstream, kernels, inner, edges, total):
+    )(position, listed, regions, cotangent, hidden, inner, from_above, from_below, shifts)
+
+
+def spread_kernel(position, listed, regions, upstream, *rest):
+    pieces, (inner, edges, total) = rest[:-3], rest[-3:]
     tile_rows, channels, columns = upstream.shape
     total[...] = jnp.zeros_like(total)
 
-    @pl.loop(0, columns // LANES, unroll=2)
+    @pl.loop(0, columns // LANES, unroll=4)
     def _(band):
-        wide, last = band_weights(kernels, position, band)
+        wide, last = band_weights(pieces, pieces[0].shape[0], position, band)
         mask = first_mask(regions, listed, band, channels, tile_rows)
         both = masked(side_by_side(upstream, band, tile_rows), mask)
         spread = jnp.concatenate([dot(wide, both, 0, 0), dot(last, both, 0, 0)], axis=0)
@@ -420,7 +441,7 @@
     edges[1] = total[tile_rows + 1, :, LANES : LANES + columns].astype(BF16)
 
 
-def spread_of(position, listed, regions, upstream, kernels, name):
+def spread_of(position, listed, regions, upstream, kernels, name, room=32):
     tile_rows, channels, columns = upstream.shape
     return pl.pallas_call(
         spread_kernel,
@@ -428,13 +449,13 @@
             jax.ShapeDtypeStruct(upstream.shape, F32),
             jax.ShapeDtypeStruct((2, channels, columns), BF16),
         ),
-        in_specs=[SMEM, SMEM] + [VMEM] * 3,
+        in_specs=[SMEM, SMEM] + [VMEM] * (2 + len(kernels)),
         out_specs=(VMEM, VMEM),
         scratch_shapes=[pltpu.VMEM((tile_rows + 2, channels, columns + 2 * LANES), F32)],
-        compiler_params=params(32),
+        compiler_params=params(room),
         cost_estimate=cost(4 * 9 * channels * channels * columns * tile_rows, 5000000),
         name=name,
-    )(position, listed, regions, upstream, kernels)
+    )(position, listed, regions, upstream, *kernels)
 
 
 GY = ("far", "near")
@@ -473,65 +494,72 @@
     per_dev = banks.shape[1]
     slots_per = max(1, 2 * col_bands // devices)
     places = devices * slots_per
-    most = min(far * slots_per, 2 * col_bands)
     listed = tile_regions.reshape(-1)
     bank_row = bank_slot[listed]
     holder = bank_row // per_dev
     local_row = bank_row % per_dev
     position, wanted = places_for(holder, devices, slots_per, local_row)
-    source, asking = places_for(holder % near, near, most, holder // near * per_dev + local_row)
     my_group, my_far = lax.axis_index("groups"), lax.axis_index("far")
 
     cells = jnp.transpose(field, (1, 0, 2))
     upstream = jnp.transpose(cotangent, (1, 0, 2))
     last = cells.shape[0] - 1
     where = (position, listed, region_map)
-    fetch = (source, listed, region_map)
-
+
+    message = jnp.transpose(wanted.reshape(far, near, slots_per), (1, 0, 2))
+    message = jnp.broadcast_to(message[None, None], (groups, far, near, far, slots_per))
     own_part = my_group.astype(jnp.int32).reshape(1)
-    wire_one = wire(own_part, banks, 1, groups)
-    turns = [[(k, (k + step) % far) for k in range(far)] for step in range(1, far)]
-    bank_one = [wire_one] + [lax.ppermute(wire_one, "far", turn) for turn in turns]
+    message = exchange(message.reshape(groups * devices, far * slots_per), ALL)
+    message = message.reshape(groups, far, near, far, slots_per)
+    mine = lax.dynamic_index_in_dim(message, my_group, 0, False)
+    requested = lax.dynamic_index_in_dim(mine, my_far, 2, False).reshape(-1)
+    asked = lax.dynamic_index_in_dim(message, my_far, 1, False).reshape(groups * near, far, slots_per)
+    steps = jnp.arange(far, dtype=jnp.int32)
+    asked = jnp.maximum(jnp.take(asked, (my_far - steps) % far, axis=1), 0)
+    asked = asked.reshape(groups * near, far * slots_per)
+
+    step = (my_far - holder // near) % far
+    place = (holder % near * far + step) * slots_per + position % slots_per
+    fetch = (place.astype(jnp.int32), listed, region_map)
+
     above, below = from_neighbours(cells[last], cells[0])
-    *bank_one, above, below, own_part = after((*bank_one, above, below), own_part)
-    wire_zero = wire(own_part, banks, 0, groups)
-    bank_zero = [wire_zero] + [lax.ppermute(wire_zero, "far", turn) for turn in turns]
-    message = jnp.concatenate(
-        [
-            jnp.broadcast_to(wanted.reshape(1, far, near, slots_per), (groups, far, near, slots_per)),
-            jnp.broadcast_to(asking.reshape(1, 1, near, most), (groups, far, near, most)),
-        ],
-        axis=-1,
-    )
-    message = exchange(message.reshape(groups * devices, slots_per + most), ALL)
-    message = message.reshape(groups, far, near, slots_per + most)
-    requested = lax.dynamic_index_in_dim(message, my_group, 0, False)[:, :, :slots_per].reshape(-1)
-    asked = lax.dynamic_index_in_dim(message, my_far, 1, False)[:, :, slots_per:].reshape(-1)
-    step_of = jnp.where(asked < 0, 0, (my_far - asked // per_dev + far) % far).astype(jnp.int32)
-    row_of = jnp.where(asked < 0, 0, asked % per_dev)
+    turns = [[(k, (k + turn) % far) for k in range(far)] for turn in range(1, far)]
+    whole = part_rows(groups)
+    wire_a, wire_b = wire(own_part, banks, 1, groups, (64, whole - 64))
+    (wire_zero,) = wire(own_part, banks, 0, groups, (whole,))
+
+    def gathered(mine):
+        return [mine] + [lax.ppermute(mine, "far", turn) for turn in turns]
 
     def fetched(buffers, name):
-        arrived = exchange(pack(step_of, row_of, buffers, name), PLANE)
-        return arrived.reshape(groups, near * most, *arrived.shape[1:])
-
-    kernel_one = fetched(bank_one, "pack_1")
-    kernel_zero = fetched(bank_zero, "pack_0")
-    inner_one, edges_one = spread_of(*fetch, upstream, kernel_one, "spread_1")
+        arrived = exchange(pack(asked, buffers, name), PLANE)
+        return arrived.reshape(groups, near * far * slots_per, *arrived.shape[1:])
+
+    bank_a = gathered(wire_a)
+    *bank_a, wire_b = after(bank_a, wire_b)
+    bank_b = gathered(wire_b)
+    *bank_b, above, below, wire_zero = after((*bank_b, above, below), wire_zero)
+    bank_zero = gathered(wire_zero)
+    kernel_one = [fetched(bank_a, "pack_1a"), fetched(bank_b, "pack_1b")]
+    kernel_zero = [fetched(bank_zero, "pack_0")]
+    shifts = shift(above, cells, below, "shift_0")
+    shifts, upstream_one = after((shifts,), upstream)
+    inner_one, edges_one = spread_of(*fetch, upstream_one, kernel_one, "spread_1")
     from_above, from_below = from_neighbours(edges_one[1], edges_one[0])
-    hidden = conv(*fetch, above, cells, below, kernel_zero, "conv_0")
+    hidden = conv(*fetch, cells, shifts, kernel_zero, "conv_0")
     hidden_above, hidden_below = from_neighbours(hidden[last], hidden[0])
     carried, partial_zero = carried_of(
-        *where, upstream, hidden, inner_one, from_above, from_below, above, cells, below, places, groups
+        *where, upstream, hidden, inner_one, from_above, from_below, shifts, places, groups
     )
     hidden_above, hidden_below, partial_zero = after((hidden_above, hidden_below), partial_zero)
     around = (hidden_above, hidden, hidden_below)
     sent_zero = exchange(partial_zero, GY)
-    inner_zero, edges_zero = spread_of(*fetch, carried, kernel_zero, "spread_0")
+    inner_zero, edges_zero = spread_of(*fetch, carried, kernel_zero, "spread_0", 56)
     from_above, from_below = from_neighbours(edges_zero[1], edges_zero[0])
-    partial_one = partial_of(*where, upstream, *around, places, groups)
+    partial_one, shifts_one = partial_of(*where, upstream, *around, places, groups)
     from_above, from_below, partial_one = after((from_above, from_below), partial_one)
     sent_one = exchange(partial_one, GY)
-    refined = conv(*fetch, *around, kernel_one, "conv_1")
+    refined = conv(*fetch, hidden, shifts_one, kernel_one, "conv_1", 56)
     back = inner_zero.at[0].add(from_above.astype(F32)).at[last].add(from_below.astype(F32))
     input_grad = (carried.astype(F32) + jnp.where(cells > 0, back, 0.0)).astype(BF16)
     half = total_of(requested, sent_zero, banks, 0, groups)

time: 260 us -> 252 us (0.969)
  waiting for transfers between devices: 120 us -> 105 us
  local copies, waits for them, and re-layouts: 22.6 us -> 30.8 us
  starting transfers between devices: 61.2 us -> 68.9 us
  Pallas kernels: 49.7 us -> 43.4 us
  other arithmetic: 3.71 us -> 0.96 us
    all_to_all x5 -> x6, waiting for transfers between devices: 68.2 us -> 51.6 us  [exchange(): return lax.all_to_all(value, axes, split_axis=0, concat_axis=0, tiled=True)]
    ppermute x6 -> x9, waiting for transfers between devices: 12.3 us -> 18.3 us  [gathered(): return [mine] + [lax.ppermute(mine, 'far', turn) for turn in turns]]
    all_to_all x5 -> x6, starting transfers between devices: 26.3 us -> 30.3 us  [exchange(): return lax.all_to_all(value, axes, split_axis=0, concat_axis=0, tiled=True)]
    unnamed x85 -> x89, local copies, waits for them, and re-layouts: 20.3 us -> 24.2 us
    ppermute x4, waiting for transfers between devices: 39.1 us -> 35.4 us  [from_neighbours(): below = lax.ppermute(lower, GY, [(i + 1, i) for i in range(count - 1)])]
    pallas_call x2, Pallas kernels: 10.2 us -> 6.74 us  [total_of(): pl.pallas_call(functools.partial(total_kernel, groups, per_dev, rows), gr...]
    ppermute x6 -> x9, starting transfers between devices: 9.06 us -> 10.8 us  [gathered(): return [mine] + [lax.ppermute(mine, 'far', turn) for turn in turns]]
    pallas_call x3 -> x5, Pallas kernels: 11.7 us -> 11.8 us  [the longest x1 6.63 us: partial_of(): pl.pallas_call(functools.partial(partial_kernel, groups), out_shape=(jax....]
  transfers between devices with their start and end apart: 19 -> 23, of which waited for: 9 -> 9; matrix products, arithmetic and copies ran while one was open for 4% -> 5% of each run, Pallas kernels for 16% -> 16%
where the time goes in v3:
time: 252 us; the launch traced here: 251 us
  waiting for transfers between devices  105 us (42%)
  starting transfers between devices  68.9 us (27%)
  Pallas kernels  43.4 us (17%)
  local copies, waits for them, and re-layouts  30.8 us (12%)
    all_to_all x6, waiting for transfers between devices, exchange(): return lax.all_to_all(value, axes, split_axis=0, concat_axis=0, tiled=True)  51.6 us
    ppermute x4, waiting for transfers between devices, from_neighbours(): below = lax.ppermute(lower, GY, [(i + 1, i) for i in range(count - 1)])  35.4 us
    all_to_all x6, starting transfers between devices, exchange(): return lax.all_to_all(value, axes, split_axis=0, concat_axis=0, tiled=True)  30.3 us
    unnamed x89, local copies, waits for them, and re-layouts  24.2 us
    ppermute x9, waiting for transfers between devices, gathered(): return [mine] + [lax.ppermute(mine, 'far', turn) for turn in turns]  18.3 us
    ppermute x4, starting transfers between devices, from_neighbours(): above = lax.ppermute(upper, GY, [(i, i + 1) for i in range(count - 1)])  17.2 us
    ppermute x9, starting transfers between devices, gathered(): return [mine] + [lax.ppermute(mine, 'far', turn) for turn in turns]  10.8 us
    ppermute x4, starting transfers between devices, from_neighbours(): below = lax.ppermute(lower, GY, [(i + 1, i) for i in range(count - 1)])  10.6 us
  transfers between devices with their start and end apart: 23, of which 9 were waited for; matrix products, arithmetic and copies ran while one was open for 5% of the time, Pallas kernels for 16%

profile of v3, /device:TPU:13, one launch (start us, length us, event | category | flops | bytes accessed | tf_op | source)
XLA Modules:
  0.0 250.7 jit_solution(2643404324799761480)
XLA Ops:
  3.3 2.3 collective-permute-start.1
  5.6 2.2 collective-permute-start
  10.8 5.4 %all-to-all-start = ((s32[32,1,8]{2,1,0:T(1,128)}), s32[32,1,8]{2,1,0:T(1,128)S(1)}, u32[]{:S(2)}, u32[]{:S(2)}) async-start(s32[32,1,8]{2,1,0:T(1,128)} %copy.44), calls=%async_computation | async-start | bytes 32768 | tf_op jit(solution)/shard_map/all_to_all | solution.py:474
  19.1 2.3 collective-permute-start.7
  21.3 4.2 %collective-permute-start.6 = (bf16[64,2048]{1,0:T(8,128)(2,1)}, bf16[64,2048]{1,0:T(8,128)(2,1)S(1)}, u32[]{:S(2)}, u32[]{:S(2)}) collective-permute-start(bf16[64,2048]{1,0:T(8,128)(2,1)} %get-tuple-element.106), channel_id=1, source_target_pairs={{0,1},{1,2},{2,3},{3,4},{4,5},{5,6},{6,7},{7,8},{8,9},{9,10},{10,1... | collective-permute-start | bytes 786440 | tf_op jit(solution)/shard_map/ppermute | solution.py:468
  32.6 5.5 %all-to-all-start.2 = ((bf16[64,64,128]{2,1,0:T(8,128)(2,1)}), bf16[64,64,128]{2,1,0:T(8,128)(2,1)S(1)}, u32[]{:S(2)}, u32[]{:S(2)}) async-start(bf16[64,64,128]{2,1,0:T(8,128)(2,1)} %pack_1a.1), calls=%async_computation.2 | async-start | bytes 2097152 | tf_op jit(solution)/shard_map/all_to_all | solution.py:474
  40.6 2.8 %collective-permute-done.3.refs_1_ = bf16[8,80,128]{2,1,0:T(8,128)(2,1)S(1)} collective-permute-done((bf16[8,80,128]{2,1,0:T(8,128)(2,1)S(1)}, bf16[8,80,128]{2,1,0:T(8,128)(2,1)S(1)}, u32[]{:S(2)}, u32[]{:S(2)}) %collective-permute-start.3) | collective-permute-done | bytes 163872 | tf_op jit(solution)/shard_map/ppermute | solution.py:532
  44.0 2.5 collective-permute-start.10
  52.7 5.5 %all-to-all-start.3 = ((bf16[64,80,128]{2,1,0:T(8,128)(2,1)}), bf16[64,80,128]{2,1,0:T(8,128)(2,1)S(1)}, u32[]{:S(2)}, u32[]{:S(2)}) async-start(bf16[64,80,128]{2,1,0:T(8,128)(2,1)} %pack_1b.1), calls=%async_computation.3 | async-start | bytes 2621440 | tf_op jit(solution)/shard_map/all_to_all | solution.py:474
  58.2 7.5 %collective-permute-done.9.refs_2_ = bf16[8,144,128]{2,1,0:T(8,128)(2,1)S(1)} collective-permute-done((bf16[8,144,128]{2,1,0:T(8,128)(2,1)S(1)}, bf16[8,144,128]{2,1,0:T(8,128)(2,1)S(1)}, u32[]{:S(2)}, u32[]{:S(2)}) %collective-permute-start.9) | collective-permute-done | bytes 294944 | tf_op jit(solution)/shard_map/ppermute | solution.py:532
  65.7 6.3 %collective-permute-done.8.refs_1_ = bf16[8,144,128]{2,1,0:T(8,128)(2,1)S(1)} collective-permute-done((bf16[8,144,128]{2,1,0:T(8,128)(2,1)S(1)}, bf16[8,144,128]{2,1,0:T(8,128)(2,1)S(1)}, u32[]{:S(2)}, u32[]{:S(2)}) %collective-permute-start.8) | collective-permute-done | bytes 294944 | tf_op jit(solution)/shard_map/ppermute | solution.py:532
  74.4 5.3 %all-to-all-start.1 = ((bf16[64,144,128]{2,1,0:T(8,128)(2,1)}), bf16[64,144,128]{2,1,0:T(8,128)(2,1)}, u32[]{:S(2)}, u32[]{:S(2)}) async-start(bf16[64,144,128]{2,1,0:T(8,128)(2,1)} %copy-done.16), calls=%async_computation.1 | async-start | bytes 4718592 | tf_op jit(solution)/shard_map/all_to_all | solution.py:474
  83.8 3.8 %spread_1.1 = (f32[2,64,2048]{2,1,0:T(8,128)S(1)}, bf16[2,64,2048]{2,1,0:T(8,128)(2,1)S(1)}) custom-call(s32[32]{0:T(128)S(1)} %get-tuple-element.108.position, s32[32]{0:T(128)S(1)} %reshape.245.listed, s32[2,2048]{1,0:T(2,128)S(1)} %copy-done.21, bf16[2,64,2048]{2,1,0:T(8,128)(2,1)S(1)} %bitcast.60, bf16[2,32,64,128]{3,2,1,0:T(8,128)(2,1)S(1)} %bitcast.56, ...), custom_call_target="tpu_custom_call" | custom-call | flops 603979776 | bytes 5000000 | tf_op jit(solution)/shard_map/spread_1/pallas_call | solution.py:446
  89.4 2.3 collective-permute-start.14
  91.7 4.2 %collective-permute-start.13 = (bf16[64,2048]{1,0:T(8,128)(2,1)}, bf16[64,2048]{1,0:T(8,128)(2,1)}, u32[]{:S(2)}, u32[]{:S(2)}) collective-permute-start(bf16[64,2048]{1,0:T(8,128)(2,1)} %get-tuple-element.102), channel_id=1, source_target_pairs={{0,1},{1,2},{2,3},{3,4},{4,5},{5,6},{6,7},{7,8},{8,9},{9,10},{10,1... | collective-permute-start | bytes 786440 | tf_op jit(solution)/shard_map/ppermute | solution.py:468
  95.9 12.3 %all-to-all-done.1 = bf16[64,144,128]{2,1,0:T(8,128)(2,1)} async-done(((bf16[64,144,128]{2,1,0:T(8,128)(2,1)}), bf16[64,144,128]{2,1,0:T(8,128)(2,1)}, u32[]{:S(2)}, u32[]{:S(2)}) %all-to-all-start.1) | async-done | bytes 2359328 | tf_op jit(solution)/shard_map/all_to_all | solution.py:474
  109.2 3.5 %conv_0.1.hidden.middle = bf16[2,64,2048]{2,1,0:T(8,128)(2,1)S(1)} custom-call(s32[32]{0:T(128)S(1)} %get-tuple-element.108.position, s32[32]{0:T(128)S(1)} %reshape.245.listed, s32[2,2048]{1,0:T(2,128)S(1)} %copy-done.21, bf16[2,64,2048]{2,1,0:T(8,128)(2,1)S(1)} %bitcast.59, bf16[3,4,64,2048]{3,2,1,0:T(8,128)(2,1)S(1)} %shift_0.1.shifts, ...), custom_call_target="tpu_custom_call" | custom-call | flops 603979776 | bytes 5000000 | tf_op jit(solution)/shard_map/conv_0/pallas_call | solution.py:299
  112.8 3.8 %collective-permute-start.12 = (bf16[64,2048]{1,0:T(8,128)(2,1)S(1)}, bf16[64,2048]{1,0:T(8,128)(2,1)S(1)}, u32[]{:S(2)}, u32[]{:S(2)}) collective-permute-start(bf16[64,2048]{1,0:T(8,128)(2,1)S(1)} %get-tuple-element.103), channel_id=1, source_target_pairs={{1,0},{2,1},{3,2},{4,3},{5,4},{6,5},{7,6},{8,7},{9,8},{10,9},{11,1... | collective-permute-start | bytes 786440 | tf_op jit(solution)/shard_map/ppermute | solution.py:469
  116.6 4.6 %collective-permute-start.11 = (bf16[64,2048]{1,0:T(8,128)(2,1)S(1)}, bf16[64,2048]{1,0:T(8,128)(2,1)S(1)}, u32[]{:S(2)}, u32[]{:S(2)}) collective-permute-start(bf16[64,2048]{1,0:T(8,128)(2,1)S(1)} %get-tuple-element.104), channel_id=1, source_target_pairs={{0,1},{1,2},{2,3},{3,4},{4,5},{5,6},{6,7},{7,8},{8,9},{9,10},{10,1... | collective-permute-start | bytes 786440 | tf_op jit(solution)/shard_map/ppermute | solution.py:468
  121.3 3.6 %carried_partial_0.1 = (bf16[2,64,2048]{2,1,0:T(8,128)(2,1)S(1)}, bf16[32,288,128]{2,1,0:T(8,128)(2,1)S(1)}) custom-call(s32[32]{0:T(128)S(1)} %copy-done.29, s32[32]{0:T(128)S(1)} %reshape.245.listed, s32[2,2048]{1,0:T(2,128)S(1)} %copy-done.21, bf16[2,64,2048]{2,1,0:T(8,128)(2,1)S(1)} %bitcast.62, bf16[2,64,2048]{2,1,0:T(8,128)(2,1)S(1)} %conv_0.1.hidden.middle, ...), custom_call_target="tpu_custom_call" | custom-call | flops 603979776 | bytes 7000000 | tf_op jit(solution)/shard_map/carried_partial_0/pallas_call | solution.py:388
  128.5 4.1 %all-to-all-start.5 = ((bf16[32,288,128]{2,1,0:T(8,128)(2,1)}), bf16[32,288,128]{2,1,0:T(8,128)(2,1)S(1)}, u32[]{:S(2)}, u32[]{:S(2)}) async-start(bf16[32,288,128]{2,1,0:T(8,128)(2,1)} %copy-done.15), calls=%async_computation.5 | async-start | bytes 4718592 | tf_op jit(solution)/shard_map/all_to_all | solution.py:474
  132.6 6.2 %spread_0.1 = (f32[2,64,2048]{2,1,0:T(8,128)}, bf16[2,64,2048]{2,1,0:T(8,128)(2,1)}) custom-call(s32[32]{0:T(128)} %copy-done.27, s32[32]{0:T(128)} %copy-done.26, s32[2,2048]{1,0:T(2,128)} %regions.11, bf16[2,64,2048]{2,1,0:T(8,128)(2,1)} %copy-done.17, bf16[2,32,144,128]{3,2,1,0:T(8,128)(2,1)} %bitcast.10.rest_0_), custom_call_target="tpu_custom_call" | custom-call | flops 603979776 | bytes 5000000 | tf_op jit(solution)/shard_map/spread_0/pallas_call | solution.py:446
  139.9 2.3 collective-permute-start.16
  142.2 4.2 %collective-permute-start.15 = (bf16[64,2048]{1,0:T(8,128)(2,1)S(1)}, bf16[64,2048]{1,0:T(8,128)(2,1)S(1)}, u32[]{:S(2)}, u32[]{:S(2)}) collective-permute-start(bf16[64,2048]{1,0:T(8,128)(2,1)S(1)} %get-tuple-element.100), channel_id=1, source_target_pairs={{0,1},{1,2},{2,3},{3,4},{4,5},{5,6},{6,7},{7,8},{8,9},{9,10},{10,1... | collective-permute-start | bytes 786440 | tf_op jit(solution)/shard_map/ppermute | solution.py:468
  146.4 6.6 %partial_1.1 = (bf16[32,288,128]{2,1,0:T(8,128)(2,1)}, bf16[3,4,64,2048]{3,2,1,0:T(8,128)(2,1)}) custom-call(s32[32]{0:T(128)} %copy-done.28, s32[32]{0:T(128)} %copy-done.26, s32[2,2048]{1,0:T(2,128)} %regions.11, bf16[2,64,2048]{2,1,0:T(8,128)(2,1)} %bitcast.61, bf16[64,2048]{1,0:T(8,128)(2,1)} %copy-done.41, bf16[2,64,2048]{2,1,0:T(8,128)(2,1)} %copy-done.7, ...), custom_call_target="tpu_custom_call" | custom-call | flops 603979776 | bytes 8000000 | tf_op jit(solution)/shard_map/partial_1/pallas_call | solution.py:345
  153.0 35.4 %collective-permute-done.16 = bf16[64,2048]{1,0:T(8,128)(2,1)S(1)} collective-permute-done((bf16[64,2048]{1,0:T(8,128)(2,1)S(1)}, bf16[64,2048]{1,0:T(8,128)(2,1)S(1)}, u32[]{:S(2)}, u32[]{:S(2)}) %collective-permute-start.16) | collective-permute-done | bytes 262176 | tf_op jit(solution)/shard_map/ppermute | solution.py:469
  189.8 4.5 %all-to-all-start.4 = ((bf16[32,288,128]{2,1,0:T(8,128)(2,1)}), bf16[32,288,128]{2,1,0:T(8,128)(2,1)S(1)}, u32[]{:S(2)}, u32[]{:S(2)}) async-start(bf16[32,288,128]{2,1,0:T(8,128)(2,1)} %get-tuple-element.85), calls=%async_computation.4 | async-start | bytes 4718592 | tf_op jit(solution)/shard_map/all_to_all | solution.py:474
  195.2 5.4 %conv_1.1 = bf16[2,64,2048]{2,1,0:T(8,128)(2,1)} custom-call(s32[32]{0:T(128)} %copy-done.27, s32[32]{0:T(128)} %copy-done.26, s32[2,2048]{1,0:T(2,128)} %regions.11, bf16[2,64,2048]{2,1,0:T(8,128)(2,1)} %copy-done.7, bf16[3,4,64,2048]{3,2,1,0:T(8,128)(2,1)} %get-tuple-element.78.shifts, bf16[2,32,64,128]{3,2,1,0:T(8,128)(2,1)} %bitcast.55, ...), custom_call_target="tpu_custom_call" | custom-call | flops 603979776 | bytes 5000000 | tf_op jit(solution)/shard_map/conv_1/pallas_call | solution.py:299
  200.6 2.5 copy.48
  205.0 3.4 %total_0.1.rest_0_ = f32[2,8,36864]{2,1,0:T(8,128)} custom-call(s32[32]{0:T(128)S(1)} %reshape.254.requested, bf16[32,288,128]{2,1,0:T(8,128)(2,1)S(1)} %copy-done.4), custom_call_target="tpu_custom_call" | custom-call | flops 1000000 | bytes 3538944 | tf_op jit(solution)/shard_map/total_0/pallas_call | solution.py:172
  208.4 38.9 %all-to-all-done.4.parts = bf16[32,288,128]{2,1,0:T(8,128)(2,1)S(1)} async-done(((bf16[32,288,128]{2,1,0:T(8,128)(2,1)}), bf16[32,288,128]{2,1,0:T(8,128)(2,1)S(1)}, u32[]{:S(2)}, u32[]{:S(2)}) %all-to-all-start.4) | async-done | bytes 2359328 | tf_op jit(solution)/shard_map/all_to_all | solution.py:474
  247.3 3.4 %total_1.1 = f32[2,8,36864]{2,1,0:T(8,128)} custom-call(s32[32]{0:T(128)S(1)} %reshape.254.requested, bf16[32,288,128]{2,1,0:T(8,128)(2,1)S(1)} %all-to-all-done.4.parts, f32[2,8,36864]{2,1,0:T(8,128)} %total_0.1.rest_0_), custom_call_target="tpu_custom_call", output_to_operand_aliasing={{}: (2, {})} | custom-call | flops 1000000 | bytes 3538944 | tf_op jit(solution)/shard_map/total_1/pallas_call | solution.py:172
  (153 shorter events, 42.8 us)
Async XLA Ops:
  1.9 23.8 %copy-start.12 = (bf16[2,8,36864]{2,1,0:T(8,128)(2,1)S(1)}, bf16[2,8,36864]{2,1,0:T(8,128)(2,1)}, u32[]{:S(2)}) copy-start(bf16[2,8,36864]{2,1,0:T(8,128)(2,1)} %banks.3) | copy-start | bytes 3538948
  3.1 25.4 %collective-permute-start.2 = (bf16[8,64,128]{2,1,0:T(8,128)(2,1)S(1)}, bf16[8,64,128]{2,1,0:T(8,128)(2,1)S(1)}, u32[]{:S(2)}, u32[]{:S(2)}) collective-permute-start(bf16[8,64,128]{2,1,0:T(8,128)(2,1)S(1)} %get-tuple-element.65.refs_0_), channel_id=1, source_target_pairs={{0,12},{4,0},{8,4},{12,8},{1,13},{5,1},{9,5},{13,9},{2,14},{6,2},{... | collective-permute-start | bytes 393224 | tf_op jit(solution)/shard_map/ppermute | solution.py:532
  3.3 25.2 %collective-permute-start.1 = (bf16[8,64,128]{2,1,0:T(8,128)(2,1)S(1)}, bf16[8,64,128]{2,1,0:T(8,128)(2,1)S(1)}, u32[]{:S(2)}, u32[]{:S(2)}) collective-permute-start(bf16[8,64,128]{2,1,0:T(8,128)(2,1)S(1)} %get-tuple-element.65.refs_0_), channel_id=1, source_target_pairs={{0,8},{4,12},{8,0},{12,4},{1,9},{5,13},{9,1},{13,5},{2,10},{6,14},... | collective-permute-start | bytes 393224 | tf_op jit(solution)/shard_map/ppermute | solution.py:532
  5.6 22.9 %collective-permute-start = (bf16[8,64,128]{2,1,0:T(8,128)(2,1)S(1)}, bf16[8,64,128]{2,1,0:T(8,128)(2,1)S(1)}, u32[]{:S(2)}, u32[]{:S(2)}) collective-permute-start(bf16[8,64,128]{2,1,0:T(8,128)(2,1)S(1)} %get-tuple-element.65.refs_0_), channel_id=1, source_target_pairs={{0,4},{4,8},{8,12},{12,0},{1,5},{5,9},{9,13},{13,1},{2,6},{6,10},{... | collective-permute-start | bytes 393224 | tf_op jit(solution)/shard_map/ppermute | solution.py:532
  9.7 23.0 %copy-start.28 = (s32[32]{0:T(128)}, s32[32]{0:T(128)S(1)}, u32[]{:S(2)}) copy-start(s32[32]{0:T(128)S(1)} %get-tuple-element.107.position) | copy-start | bytes 388
  9.7 98.5 %copy-start.27 = (s32[32]{0:T(128)}, s32[32]{0:T(128)S(1)}, u32[]{:S(2)}) copy-start(s32[32]{0:T(128)S(1)} %get-tuple-element.108.position) | copy-start | bytes 388
  10.8 16.2 %all-to-all-start = ((s32[32,1,8]{2,1,0:T(1,128)}), s32[32,1,8]{2,1,0:T(1,128)S(1)}, u32[]{:S(2)}, u32[]{:S(2)}) async-start(s32[32,1,8]{2,1,0:T(1,128)} %copy.44), calls=%async_computation | async-start | bytes 32768 | tf_op jit(solution)/shard_map/all_to_all | solution.py:474
  19.1 19.1 %collective-permute-start.7 = (bf16[64,2048]{1,0:T(8,128)(2,1)}, bf16[64,2048]{1,0:T(8,128)(2,1)S(1)}, u32[]{:S(2)}, u32[]{:S(2)}) collective-permute-start(bf16[64,2048]{1,0:T(8,128)(2,1)} %get-tuple-element.105), channel_id=1, source_target_pairs={{1,0},{2,1},{3,2},{4,3},{5,4},{6,5},{7,6},{8,7},{9,8},{10,9},{11,1... | collective-permute-start | bytes 786440 | tf_op jit(solution)/shard_map/ppermute | solution.py:469
  21.3 16.8 %collective-permute-start.6 = (bf16[64,2048]{1,0:T(8,128)(2,1)}, bf16[64,2048]{1,0:T(8,128)(2,1)S(1)}, u32[]{:S(2)}, u32[]{:S(2)}) collective-permute-start(bf16[64,2048]{1,0:T(8,128)(2,1)} %get-tuple-element.106), channel_id=1, source_target_pairs={{0,1},{1,2},{2,3},{3,4},{4,5},{5,6},{6,7},{7,8},{8,9},{9,10},{10,1... | collective-permute-start | bytes 786440 | tf_op jit(solution)/shard_map/ppermute | solution.py:468
  28.5 9.7 %collective-permute-start.5 = (bf16[8,80,128]{2,1,0:T(8,128)(2,1)S(1)}, bf16[8,80,128]{2,1,0:T(8,128)(2,1)S(1)}, u32[]{:S(2)}, u32[]{:S(2)}) collective-permute-start(bf16[8,80,128]{2,1,0:T(8,128)(2,1)S(1)} %get-tuple-element.69.refs_0_), channel_id=1, source_target_pairs={{0,12},{4,0},{8,4},{12,8},{1,13},{5,1},{9,5},{13,9},{2,14},{6,2},{... | collective-permute-start | bytes 491528 | tf_op jit(solution)/shard_map/ppermute | solution.py:532
  28.8 11.0 %collective-permute-start.4 = (bf16[8,80,128]{2,1,0:T(8,128)(2,1)S(1)}, bf16[8,80,128]{2,1,0:T(8,128)(2,1)S(1)}, u32[]{:S(2)}, u32[]{:S(2)}) collective-permute-start(bf16[8,80,128]{2,1,0:T(8,128)(2,1)S(1)} %get-tuple-element.69.refs_0_), channel_id=1, source_target_pairs={{0,8},{4,12},{8,0},{12,4},{1,9},{5,13},{9,1},{13,5},{2,10},{6,14},... | collective-permute-start | bytes 491528 | tf_op jit(solution)/shard_map/ppermute | solution.py:532
  30.9 12.4 %collective-permute-start.3 = (bf16[8,80,128]{2,1,0:T(8,128)(2,1)S(1)}, bf16[8,80,128]{2,1,0:T(8,128)(2,1)S(1)}, u32[]{:S(2)}, u32[]{:S(2)}) collective-permute-start(bf16[8,80,128]{2,1,0:T(8,128)(2,1)S(1)} %get-tuple-element.69.refs_0_), channel_id=1, source_target_pairs={{0,4},{4,8},{8,12},{12,0},{1,5},{5,9},{9,13},{13,1},{2,6},{6,10},{... | collective-permute-start | bytes 491528 | tf_op jit(solution)/shard_map/ppermute | solution.py:532
  32.6 19.0 %all-to-all-start.2 = ((bf16[64,64,128]{2,1,0:T(8,128)(2,1)}), bf16[64,64,128]{2,1,0:T(8,128)(2,1)S(1)}, u32[]{:S(2)}, u32[]{:S(2)}) async-start(bf16[64,64,128]{2,1,0:T(8,128)(2,1)} %pack_1a.1), calls=%async_computation.2 | async-start | bytes 2097152 | tf_op jit(solution)/shard_map/all_to_all | solution.py:474
  38.2 13.2 %copy-start.22 = (bf16[64,2048]{1,0:T(8,128)(2,1)}, bf16[64,2048]{1,0:T(8,128)(2,1)S(1)}, u32[]{:S(2)}) copy-start(bf16[64,2048]{1,0:T(8,128)(2,1)S(1)} %collective-permute-done.7.below) | copy-start | bytes 786436
  38.2 13.2 %copy-start.24 = (bf16[64,2048]{1,0:T(8,128)(2,1)}, bf16[64,2048]{1,0:T(8,128)(2,1)S(1)}, u32[]{:S(2)}) copy-start(bf16[64,2048]{1,0:T(8,128)(2,1)S(1)} %collective-permute-done.6.above) | copy-start | bytes 786436
  44.0 14.1 %collective-permute-start.10 = (bf16[8,144,128]{2,1,0:T(8,128)(2,1)S(1)}, bf16[8,144,128]{2,1,0:T(8,128)(2,1)S(1)}, u32[]{:S(2)}, u32[]{:S(2)}) collective-permute-start(bf16[8,144,128]{2,1,0:T(8,128)(2,1)S(1)} %wire_0.1.refs_0_), channel_id=1, source_target_pairs={{0,12},{4,0},{8,4},{12,8},{1,13},{5,1},{9,5},{13,9},{2,14},{6,2},{... | collective-permute-start | bytes 884744 | tf_op jit(solution)/shard_map/ppermute | solution.py:532
  46.5 19.1 %collective-permute-start.9 = (bf16[8,144,128]{2,1,0:T(8,128)(2,1)S(1)}, bf16[8,144,128]{2,1,0:T(8,128)(2,1)S(1)}, u32[]{:S(2)}, u32[]{:S(2)}) collective-permute-start(bf16[8,144,128]{2,1,0:T(8,128)(2,1)S(1)} %wire_0.1.refs_0_), channel_id=1, source_target_pairs={{0,8},{4,12},{8,0},{12,4},{1,9},{5,13},{9,1},{13,5},{2,10},{6,14},... | collective-permute-start | bytes 884744 | tf_op jit(solution)/shard_map/ppermute | solution.py:532
  47.3 24.6 %collective-permute-start.8 = (bf16[8,144,128]{2,1,0:T(8,128)(2,1)S(1)}, bf16[8,144,128]{2,1,0:T(8,128)(2,1)S(1)}, u32[]{:S(2)}, u32[]{:S(2)}) collective-permute-start(bf16[8,144,128]{2,1,0:T(8,128)(2,1)S(1)} %wire_0.1.refs_0_), channel_id=1, source_target_pairs={{0,4},{4,8},{8,12},{12,0},{1,5},{5,9},{9,13},{13,1},{2,6},{6,10},{... | collective-permute-start | bytes 884744 | tf_op jit(solution)/shard_map/ppermute | solution.py:532
  52.7 21.7 %all-to-all-start.3 = ((bf16[64,80,128]{2,1,0:T(8,128)(2,1)}), bf16[64,80,128]{2,1,0:T(8,128)(2,1)S(1)}, u32[]{:S(2)}, u32[]{:S(2)}) async-start(bf16[64,80,128]{2,1,0:T(8,128)(2,1)} %pack_1b.1), calls=%async_computation.3 | async-start | bytes 2621440 | tf_op jit(solution)/shard_map/all_to_all | solution.py:474
  74.4 33.8 %all-to-all-start.1 = ((bf16[64,144,128]{2,1,0:T(8,128)(2,1)}), bf16[64,144,128]{2,1,0:T(8,128)(2,1)}, u32[]{:S(2)}, u32[]{:S(2)}) async-start(bf16[64,144,128]{2,1,0:T(8,128)(2,1)} %copy-done.16), calls=%async_computation.1 | async-start | bytes 4718592 | tf_op jit(solution)/shard_map/all_to_all | solution.py:474
  79.8 41.4 %copy-start.26 = (s32[32]{0:T(128)}, s32[32]{0:T(128)S(1)}, u32[]{:S(2)}) copy-start(s32[32]{0:T(128)S(1)} %reshape.245.listed) | copy-start | bytes 388
  89.4 31.8 %collective-permute-start.14 = (bf16[64,2048]{1,0:T(8,128)(2,1)}, bf16[64,2048]{1,0:T(8,128)(2,1)S(1)}, u32[]{:S(2)}, u32[]{:S(2)}) collective-permute-start(bf16[64,2048]{1,0:T(8,128)(2,1)} %get-tuple-element.101), channel_id=1, source_target_pairs={{1,0},{2,1},{3,2},{4,3},{5,4},{6,5},{7,6},{8,7},{9,8},{10,9},{11,1... | collective-permute-start | bytes 786440 | tf_op jit(solution)/shard_map/ppermute | solution.py:469
  91.7 29.6 %collective-permute-start.13 = (bf16[64,2048]{1,0:T(8,128)(2,1)}, bf16[64,2048]{1,0:T(8,128)(2,1)}, u32[]{:S(2)}, u32[]{:S(2)}) collective-permute-start(bf16[64,2048]{1,0:T(8,128)(2,1)} %get-tuple-element.102), channel_id=1, source_target_pairs={{0,1},{1,2},{2,3},{3,4},{4,5},{5,6},{6,7},{7,8},{8,9},{9,10},{10,1... | collective-permute-start | bytes 786440 | tf_op jit(solution)/shard_map/ppermute | solution.py:468
  109.2 12.1 %copy-start.20 = (f32[2,64,2048]{2,1,0:T(8,128)S(1)}, f32[2,64,2048]{2,1,0:T(8,128)}, u32[]{:S(2)}) copy-start(f32[2,64,2048]{2,1,0:T(8,128)} %copy-done.19) | copy-start | bytes 3145732
  109.2 12.1 %copy-start.29 = (s32[32]{0:T(128)S(1)}, s32[32]{0:T(128)}, u32[]{:S(2)}) copy-start(s32[32]{0:T(128)} %copy-done.28) | copy-start | bytes 388
  112.7 12.1 %copy-start.7 = (bf16[2,64,2048]{2,1,0:T(8,128)(2,1)}, bf16[2,64,2048]{2,1,0:T(8,128)(2,1)S(1)}, u32[]{:S(2)}) copy-start(bf16[2,64,2048]{2,1,0:T(8,128)(2,1)S(1)} %conv_0.1.hidden.middle) | copy-start | bytes 1572868
  112.8 14.3 %collective-permute-start.12 = (bf16[64,2048]{1,0:T(8,128)(2,1)S(1)}, bf16[64,2048]{1,0:T(8,128)(2,1)S(1)}, u32[]{:S(2)}, u32[]{:S(2)}) collective-permute-start(bf16[64,2048]{1,0:T(8,128)(2,1)S(1)} %get-tuple-element.103), channel_id=1, source_target_pairs={{1,0},{2,1},{3,2},{4,3},{5,4},{6,5},{7,6},{8,7},{9,8},{10,9},{11,1... | collective-permute-start | bytes 786440 | tf_op jit(solution)/shard_map/ppermute | solution.py:469
  116.6 10.4 %collective-permute-start.11 = (bf16[64,2048]{1,0:T(8,128)(2,1)S(1)}, bf16[64,2048]{1,0:T(8,128)(2,1)S(1)}, u32[]{:S(2)}, u32[]{:S(2)}) collective-permute-start(bf16[64,2048]{1,0:T(8,128)(2,1)S(1)} %get-tuple-element.104), channel_id=1, source_target_pairs={{0,1},{1,2},{2,3},{3,4},{4,5},{5,6},{6,7},{7,8},{8,9},{9,10},{10,1... | collective-permute-start | bytes 786440 | tf_op jit(solution)/shard_map/ppermute | solution.py:468
  128.5 59.9 %all-to-all-start.5 = ((bf16[32,288,128]{2,1,0:T(8,128)(2,1)}), bf16[32,288,128]{2,1,0:T(8,128)(2,1)S(1)}, u32[]{:S(2)}, u32[]{:S(2)}) async-start(bf16[32,288,128]{2,1,0:T(8,128)(2,1)} %copy-done.15), calls=%async_computation.5 | async-start | bytes 4718592 | tf_op jit(solution)/shard_map/all_to_all | solution.py:474
  139.9 48.5 %collective-permute-start.16 = (bf16[64,2048]{1,0:T(8,128)(2,1)S(1)}, bf16[64,2048]{1,0:T(8,128)(2,1)S(1)}, u32[]{:S(2)}, u32[]{:S(2)}) collective-permute-start(bf16[64,2048]{1,0:T(8,128)(2,1)S(1)} %get-tuple-element.99), channel_id=1, source_target_pairs={{1,0},{2,1},{3,2},{4,3},{5,4},{6,5},{7,6},{8,7},{9,8},{10,9},{11,1... | collective-permute-start | bytes 786440 | tf_op jit(solution)/shard_map/ppermute | solution.py:469
  142.2 46.2 %collective-permute-start.15 = (bf16[64,2048]{1,0:T(8,128)(2,1)S(1)}, bf16[64,2048]{1,0:T(8,128)(2,1)S(1)}, u32[]{:S(2)}, u32[]{:S(2)}) collective-permute-start(bf16[64,2048]{1,0:T(8,128)(2,1)S(1)} %get-tuple-element.100), channel_id=1, source_target_pairs={{0,1},{1,2},{2,3},{3,4},{4,5},{5,6},{6,7},{7,8},{8,9},{9,10},{10,1... | collective-permute-start | bytes 786440 | tf_op jit(solution)/shard_map/ppermute | solution.py:468
  189.8 57.5 %all-to-all-start.4 = ((bf16[32,288,128]{2,1,0:T(8,128)(2,1)}), bf16[32,288,128]{2,1,0:T(8,128)(2,1)S(1)}, u32[]{:S(2)}, u32[]{:S(2)}) async-start(bf16[32,288,128]{2,1,0:T(8,128)(2,1)} %get-tuple-element.85), calls=%async_computation.4 | async-start | bytes 4718592 | tf_op jit(solution)/shard_map/all_to_all | solution.py:474
  (33 other events, 87.1 us)

commit v4 on v3

--- a/solution.py
+++ b/solution.py
@@ -538,7 +538,7 @@
     bank_a = gathered(wire_a)
     *bank_a, wire_b = after(bank_a, wire_b)
     bank_b = gathered(wire_b)
-    *bank_b, above, below, wire_zero = after((*bank_b, above, below), wire_zero)
+    bank_b[-1], above, below, wire_zero = after((bank_b[-1], above, below), wire_zero)
     bank_zero = gathered(wire_zero)
     kernel_one = [fetched(bank_a, "pack_1a"), fetched(bank_b, "pack_1b")]
     kernel_zero = [fetched(bank_zero, "pack_0")]

time: 252 us -> 251 us (level)
  waiting for transfers between devices: 105 us -> 109 us
  starting transfers between devices: 68.9 us -> 65.4 us
    ppermute x9, waiting for transfers between devices: 18.3 us -> 21 us  [gathered(): return [mine] + [lax.ppermute(mine, 'far', turn) for turn in turns]]
    unnamed x89 -> x85, local copies, waits for them, and re-layouts: 24.2 us -> 22.6 us
  transfers between devices with their start and end apart: 23 -> 23, of which waited for: 9 -> 7; matrix products, arithmetic and copies ran while one was open for 5% -> 5% of each run, Pallas kernels for 16% -> 16%
where the time goes in v4:
time: 251 us; the launch traced here: 249 us
  waiting for transfers between devices  109 us (43%)
  starting transfers between devices  65.4 us (26%)
  Pallas kernels  43.8 us (17%)
  local copies, waits for them, and re-layouts  29.2 us (12%)
    all_to_all x6, waiting for transfers between devices, exchange(): return lax.all_to_all(value, axes, split_axis=0, concat_axis=0, tiled=True)  52.4 us
    ppermute x4, waiting for transfers between devices, from_neighbours(): below = lax.ppermute(lower, GY, [(i + 1, i) for i in range(count - 1)])  35.4 us
    all_to_all x6, starting transfers between devices, exchange(): return lax.all_to_all(value, axes, split_axis=0, concat_axis=0, tiled=True)  28.5 us
    unnamed x85, local copies, waits for them, and re-layouts  22.6 us
    ppermute x9, waiting for transfers between devices, gathered(): return [mine] + [lax.ppermute(mine, 'far', turn) for turn in turns]  21 us
    ppermute x4, starting transfers between devices, from_neighbours(): above = lax.ppermute(upper, GY, [(i, i + 1) for i in range(count - 1)])  17.4 us
    ppermute x4, starting transfers between devices, from_neighbours(): below = lax.ppermute(lower, GY, [(i + 1, i) for i in range(count - 1)])  10.6 us
    pallas_call x2, Pallas kernels, spread_of(): pl.pallas_call(spread_kernel, out_shape=(jax.ShapeDtypeStruct(upstream.sh...  10 us
  transfers between devices with their start and end apart: 23, of which 7 were waited for; matrix products, arithmetic and copies ran while one was open for 5% of the time, Pallas kernels for 16%

profile of v4, /device:TPU:13, one launch (start us, length us, event | category | flops | bytes accessed | tf_op | source)
XLA Modules:
  0.0 249.4 jit_solution(6224953580384771466)
XLA Ops:
  3.3 2.3 collective-permute-start.1
  5.6 2.2 collective-permute-start
  10.8 5.4 %all-to-all-start = ((s32[32,1,8]{2,1,0:T(1,128)}), s32[32,1,8]{2,1,0:T(1,128)S(1)}, u32[]{:S(2)}, u32[]{:S(2)}) async-start(s32[32,1,8]{2,1,0:T(1,128)} %copy.44), calls=%async_computation | async-start | bytes 32768 | tf_op jit(solution)/shard_map/all_to_all | solution.py:474
  19.1 2.3 collective-permute-start.5
  21.3 4.2 %collective-permute-start.4 = (bf16[64,2048]{1,0:T(8,128)(2,1)}, bf16[64,2048]{1,0:T(8,128)(2,1)S(1)}, u32[]{:S(2)}, u32[]{:S(2)}) collective-permute-start(bf16[64,2048]{1,0:T(8,128)(2,1)} %get-tuple-element.100), channel_id=1, source_target_pairs={{0,1},{1,2},{2,3},{3,4},{4,5},{5,6},{6,7},{7,8},{8,9},{9,10},{10,1... | collective-permute-start | bytes 786440 | tf_op jit(solution)/shard_map/ppermute | solution.py:468
  32.6 4.6 %all-to-all-start.2 = ((bf16[64,64,128]{2,1,0:T(8,128)(2,1)}), bf16[64,64,128]{2,1,0:T(8,128)(2,1)S(1)}, u32[]{:S(2)}, u32[]{:S(2)}) async-start(bf16[64,64,128]{2,1,0:T(8,128)(2,1)} %pack_1a.1), calls=%async_computation.2 | async-start | bytes 2097152 | tf_op jit(solution)/shard_map/all_to_all | solution.py:474
  37.3 6.7 %collective-permute-done.3.refs_3_ = bf16[8,80,128]{2,1,0:T(8,128)(2,1)S(1)} collective-permute-done((bf16[8,80,128]{2,1,0:T(8,128)(2,1)S(1)}, bf16[8,80,128]{2,1,0:T(8,128)(2,1)S(1)}, u32[]{:S(2)}, u32[]{:S(2)}) %collective-permute-start.3) | collective-permute-done | bytes 163872 | tf_op jit(solution)/shard_map/ppermute | solution.py:532
  47.3 2.1 pack_1b.1
  51.8 4.5 %all-to-all-start.3 = ((bf16[64,80,128]{2,1,0:T(8,128)(2,1)}), bf16[64,80,128]{2,1,0:T(8,128)(2,1)S(1)}, u32[]{:S(2)}, u32[]{:S(2)}) async-start(bf16[64,80,128]{2,1,0:T(8,128)(2,1)} %pack_1b.1), calls=%async_computation.3 | async-start | bytes 2621440 | tf_op jit(solution)/shard_map/all_to_all | solution.py:474
  56.3 10.1 %collective-permute-done.8.refs_3_ = bf16[8,144,128]{2,1,0:T(8,128)(2,1)S(1)} collective-permute-done((bf16[8,144,128]{2,1,0:T(8,128)(2,1)S(1)}, bf16[8,144,128]{2,1,0:T(8,128)(2,1)S(1)}, u32[]{:S(2)}, u32[]{:S(2)}) %collective-permute-start.8) | collective-permute-done | bytes 294944 | tf_op jit(solution)/shard_map/ppermute | solution.py:532
  66.4 4.2 %collective-permute-done.6.refs_1_ = bf16[8,144,128]{2,1,0:T(8,128)(2,1)S(1)} collective-permute-done((bf16[8,144,128]{2,1,0:T(8,128)(2,1)S(1)}, bf16[8,144,128]{2,1,0:T(8,128)(2,1)S(1)}, u32[]{:S(2)}, u32[]{:S(2)}) %collective-permute-start.6) | collective-permute-done | bytes 294944 | tf_op jit(solution)/shard_map/ppermute | solution.py:532
  72.8 5.5 %all-to-all-start.1 = ((bf16[64,144,128]{2,1,0:T(8,128)(2,1)}), bf16[64,144,128]{2,1,0:T(8,128)(2,1)}, u32[]{:S(2)}, u32[]{:S(2)}) async-start(bf16[64,144,128]{2,1,0:T(8,128)(2,1)} %copy-done.16), calls=%async_computation.1 | async-start | bytes 4718592 | tf_op jit(solution)/shard_map/all_to_all | solution.py:474
  82.4 3.8 %spread_1.1 = (f32[2,64,2048]{2,1,0:T(8,128)S(1)}, bf16[2,64,2048]{2,1,0:T(8,128)(2,1)S(1)}) custom-call(s32[32]{0:T(128)S(1)} %get-tuple-element.102.position, s32[32]{0:T(128)S(1)} %reshape.245.listed, s32[2,2048]{1,0:T(2,128)S(1)} %copy-done.21, bf16[2,64,2048]{2,1,0:T(8,128)(2,1)S(1)} %bitcast.60, bf16[2,32,64,128]{3,2,1,0:T(8,128)(2,1)S(1)} %bitcast.56, ...), custom_call_target="tpu_custom_call" | custom-call | flops 603979776 | bytes 5000000 | tf_op jit(solution)/shard_map/spread_1/pallas_call | solution.py:446
  88.0 2.3 collective-permute-start.14
  90.3 4.2 %collective-permute-start.13 = (bf16[64,2048]{1,0:T(8,128)(2,1)}, bf16[64,2048]{1,0:T(8,128)(2,1)}, u32[]{:S(2)}, u32[]{:S(2)}) collective-permute-start(bf16[64,2048]{1,0:T(8,128)(2,1)} %get-tuple-element.96), channel_id=1, source_target_pairs={{0,1},{1,2},{2,3},{3,4},{4,5},{5,6},{6,7},{7,8},{8,9},{9,10},{10,1... | collective-permute-start | bytes 786440 | tf_op jit(solution)/shard_map/ppermute | solution.py:468
  94.5 12.3 %all-to-all-done.1 = bf16[64,144,128]{2,1,0:T(8,128)(2,1)} async-done(((bf16[64,144,128]{2,1,0:T(8,128)(2,1)}), bf16[64,144,128]{2,1,0:T(8,128)(2,1)}, u32[]{:S(2)}, u32[]{:S(2)}) %all-to-all-start.1) | async-done | bytes 2359328 | tf_op jit(solution)/shard_map/all_to_all | solution.py:474
  107.8 3.5 %conv_0.1.hidden.middle = bf16[2,64,2048]{2,1,0:T(8,128)(2,1)S(1)} custom-call(s32[32]{0:T(128)S(1)} %get-tuple-element.102.position, s32[32]{0:T(128)S(1)} %reshape.245.listed, s32[2,2048]{1,0:T(2,128)S(1)} %copy-done.21, bf16[2,64,2048]{2,1,0:T(8,128)(2,1)S(1)} %bitcast.59, bf16[3,4,64,2048]{3,2,1,0:T(8,128)(2,1)S(1)} %shift_0.1.shifts, ...), custom_call_target="tpu_custom_call" | custom-call | flops 603979776 | bytes 5000000 | tf_op jit(solution)/shard_map/conv_0/pallas_call | solution.py:299
  111.4 3.8 %collective-permute-start.10 = (bf16[64,2048]{1,0:T(8,128)(2,1)S(1)}, bf16[64,2048]{1,0:T(8,128)(2,1)S(1)}, u32[]{:S(2)}, u32[]{:S(2)}) collective-permute-start(bf16[64,2048]{1,0:T(8,128)(2,1)S(1)} %get-tuple-element.97), channel_id=1, source_target_pairs={{1,0},{2,1},{3,2},{4,3},{5,4},{6,5},{7,6},{8,7},{9,8},{10,9},{11,1... | collective-permute-start | bytes 786440 | tf_op jit(solution)/shard_map/ppermute | solution.py:469
  115.2 4.9 %collective-permute-start.9 = (bf16[64,2048]{1,0:T(8,128)(2,1)S(1)}, bf16[64,2048]{1,0:T(8,128)(2,1)S(1)}, u32[]{:S(2)}, u32[]{:S(2)}) collective-permute-start(bf16[64,2048]{1,0:T(8,128)(2,1)S(1)} %get-tuple-element.98), channel_id=1, source_target_pairs={{0,1},{1,2},{2,3},{3,4},{4,5},{5,6},{6,7},{7,8},{8,9},{9,10},{10,1... | collective-permute-start | bytes 786440 | tf_op jit(solution)/shard_map/ppermute | solution.py:468
  120.2 3.6 %carried_partial_0.1 = (bf16[2,64,2048]{2,1,0:T(8,128)(2,1)S(1)}, bf16[32,288,128]{2,1,0:T(8,128)(2,1)S(1)}) custom-call(s32[32]{0:T(128)S(1)} %copy-done.29, s32[32]{0:T(128)S(1)} %reshape.245.listed, s32[2,2048]{1,0:T(2,128)S(1)} %copy-done.21, bf16[2,64,2048]{2,1,0:T(8,128)(2,1)S(1)} %bitcast.62, bf16[2,64,2048]{2,1,0:T(8,128)(2,1)S(1)} %conv_0.1.hidden.middle, ...), custom_call_target="tpu_custom_call" | custom-call | flops 603979776 | bytes 7000000 | tf_op jit(solution)/shard_map/carried_partial_0/pallas_call | solution.py:388
  127.4 4.0 %all-to-all-start.5 = ((bf16[32,288,128]{2,1,0:T(8,128)(2,1)}), bf16[32,288,128]{2,1,0:T(8,128)(2,1)S(1)}, u32[]{:S(2)}, u32[]{:S(2)}) async-start(bf16[32,288,128]{2,1,0:T(8,128)(2,1)} %copy-done.15), calls=%async_computation.5 | async-start | bytes 4718592 | tf_op jit(solution)/shard_map/all_to_all | solution.py:474
  131.3 6.3 %spread_0.1 = (f32[2,64,2048]{2,1,0:T(8,128)}, bf16[2,64,2048]{2,1,0:T(8,128)(2,1)}) custom-call(s32[32]{0:T(128)} %copy-done.27, s32[32]{0:T(128)} %copy-done.26, s32[2,2048]{1,0:T(2,128)} %regions.11, bf16[2,64,2048]{2,1,0:T(8,128)(2,1)} %copy-done.17, bf16[2,32,144,128]{3,2,1,0:T(8,128)(2,1)} %bitcast.10.rest_0_), custom_call_target="tpu_custom_call" | custom-call | flops 603979776 | bytes 5000000 | tf_op jit(solution)/shard_map/spread_0/pallas_call | solution.py:446
  138.7 2.3 collective-permute-start.16
  140.9 4.2 %collective-permute-start.15 = (bf16[64,2048]{1,0:T(8,128)(2,1)S(1)}, bf16[64,2048]{1,0:T(8,128)(2,1)S(1)}, u32[]{:S(2)}, u32[]{:S(2)}) collective-permute-start(bf16[64,2048]{1,0:T(8,128)(2,1)S(1)} %get-tuple-element.94), channel_id=1, source_target_pairs={{0,1},{1,2},{2,3},{3,4},{4,5},{5,6},{6,7},{7,8},{8,9},{9,10},{10,1... | collective-permute-start | bytes 786440 | tf_op jit(solution)/shard_map/ppermute | solution.py:468
  145.1 6.6 %partial_1.1 = (bf16[32,288,128]{2,1,0:T(8,128)(2,1)}, bf16[3,4,64,2048]{3,2,1,0:T(8,128)(2,1)}) custom-call(s32[32]{0:T(128)} %copy-done.28, s32[32]{0:T(128)} %copy-done.26, s32[2,2048]{1,0:T(2,128)} %regions.11, bf16[2,64,2048]{2,1,0:T(8,128)(2,1)} %bitcast.61, bf16[64,2048]{1,0:T(8,128)(2,1)} %copy-done.39, bf16[2,64,2048]{2,1,0:T(8,128)(2,1)} %copy-done.7, ...), custom_call_target="tpu_custom_call" | custom-call | flops 603979776 | bytes 8000000 | tf_op jit(solution)/shard_map/partial_1/pallas_call | solution.py:345
  151.8 35.4 %collective-permute-done.16 = bf16[64,2048]{1,0:T(8,128)(2,1)S(1)} collective-permute-done((bf16[64,2048]{1,0:T(8,128)(2,1)S(1)}, bf16[64,2048]{1,0:T(8,128)(2,1)S(1)}, u32[]{:S(2)}, u32[]{:S(2)}) %collective-permute-start.16) | collective-permute-done | bytes 262176 | tf_op jit(solution)/shard_map/ppermute | solution.py:469
  188.6 4.4 %all-to-all-start.4 = ((bf16[32,288,128]{2,1,0:T(8,128)(2,1)}), bf16[32,288,128]{2,1,0:T(8,128)(2,1)S(1)}, u32[]{:S(2)}, u32[]{:S(2)}) async-start(bf16[32,288,128]{2,1,0:T(8,128)(2,1)} %get-tuple-element.79), calls=%async_computation.4 | async-start | bytes 4718592 | tf_op jit(solution)/shard_map/all_to_all | solution.py:474
  193.9 5.4 %conv_1.1 = bf16[2,64,2048]{2,1,0:T(8,128)(2,1)} custom-call(s32[32]{0:T(128)} %copy-done.27, s32[32]{0:T(128)} %copy-done.26, s32[2,2048]{1,0:T(2,128)} %regions.11, bf16[2,64,2048]{2,1,0:T(8,128)(2,1)} %copy-done.7, bf16[3,4,64,2048]{3,2,1,0:T(8,128)(2,1)} %get-tuple-element.72.shifts, bf16[2,32,64,128]{3,2,1,0:T(8,128)(2,1)} %bitcast.55, ...), custom_call_target="tpu_custom_call" | custom-call | flops 603979776 | bytes 5000000 | tf_op jit(solution)/shard_map/conv_1/pallas_call | solution.py:299
  199.4 2.5 copy.48
  203.8 3.4 %total_0.1.rest_0_ = f32[2,8,36864]{2,1,0:T(8,128)} custom-call(s32[32]{0:T(128)S(1)} %reshape.254.requested, bf16[32,288,128]{2,1,0:T(8,128)(2,1)S(1)} %copy-done.4), custom_call_target="tpu_custom_call" | custom-call | flops 1000000 | bytes 3538944 | tf_op jit(solution)/shard_map/total_0/pallas_call | solution.py:172
  207.2 38.9 %all-to-all-done.4.parts = bf16[32,288,128]{2,1,0:T(8,128)(2,1)S(1)} async-done(((bf16[32,288,128]{2,1,0:T(8,128)(2,1)}), bf16[32,288,128]{2,1,0:T(8,128)(2,1)S(1)}, u32[]{:S(2)}, u32[]{:S(2)}) %all-to-all-start.4) | async-done | bytes 2359328 | tf_op jit(solution)/shard_map/all_to_all | solution.py:474
  246.1 3.4 %total_1.1 = f32[2,8,36864]{2,1,0:T(8,128)} custom-call(s32[32]{0:T(128)S(1)} %reshape.254.requested, bf16[32,288,128]{2,1,0:T(8,128)(2,1)S(1)} %all-to-all-done.4.parts, f32[2,8,36864]{2,1,0:T(8,128)} %total_0.1.rest_0_), custom_call_target="tpu_custom_call", output_to_operand_aliasing={{}: (2, {})} | custom-call | flops 1000000 | bytes 3538944 | tf_op jit(solution)/shard_map/total_1/pallas_call | solution.py:172
  (149 shorter events, 39.0 us)
Async XLA Ops:
  1.9 23.8 %copy-start.12 = (bf16[2,8,36864]{2,1,0:T(8,128)(2,1)S(1)}, bf16[2,8,36864]{2,1,0:T(8,128)(2,1)}, u32[]{:S(2)}) copy-start(bf16[2,8,36864]{2,1,0:T(8,128)(2,1)} %banks.3) | copy-start | bytes 3538948
  3.1 25.4 %collective-permute-start.2 = (bf16[8,64,128]{2,1,0:T(8,128)(2,1)S(1)}, bf16[8,64,128]{2,1,0:T(8,128)(2,1)S(1)}, u32[]{:S(2)}, u32[]{:S(2)}) collective-permute-start(bf16[8,64,128]{2,1,0:T(8,128)(2,1)S(1)} %get-tuple-element.62.refs_0_), channel_id=1, source_target_pairs={{0,12},{4,0},{8,4},{12,8},{1,13},{5,1},{9,5},{13,9},{2,14},{6,2},{... | collective-permute-start | bytes 393224 | tf_op jit(solution)/shard_map/ppermute | solution.py:532
  3.3 25.2 %collective-permute-start.1 = (bf16[8,64,128]{2,1,0:T(8,128)(2,1)S(1)}, bf16[8,64,128]{2,1,0:T(8,128)(2,1)S(1)}, u32[]{:S(2)}, u32[]{:S(2)}) collective-permute-start(bf16[8,64,128]{2,1,0:T(8,128)(2,1)S(1)} %get-tuple-element.62.refs_0_), channel_id=1, source_target_pairs={{0,8},{4,12},{8,0},{12,4},{1,9},{5,13},{9,1},{13,5},{2,10},{6,14},... | collective-permute-start | bytes 393224 | tf_op jit(solution)/shard_map/ppermute | solution.py:532
  5.6 22.9 %collective-permute-start = (bf16[8,64,128]{2,1,0:T(8,128)(2,1)S(1)}, bf16[8,64,128]{2,1,0:T(8,128)(2,1)S(1)}, u32[]{:S(2)}, u32[]{:S(2)}) collective-permute-start(bf16[8,64,128]{2,1,0:T(8,128)(2,1)S(1)} %get-tuple-element.62.refs_0_), channel_id=1, source_target_pairs={{0,4},{4,8},{8,12},{12,0},{1,5},{5,9},{9,13},{13,1},{2,6},{6,10},{... | collective-permute-start | bytes 393224 | tf_op jit(solution)/shard_map/ppermute | solution.py:532
  9.7 23.0 %copy-start.28 = (s32[32]{0:T(128)}, s32[32]{0:T(128)S(1)}, u32[]{:S(2)}) copy-start(s32[32]{0:T(128)S(1)} %get-tuple-element.101.position) | copy-start | bytes 388
  9.7 97.1 %copy-start.27 = (s32[32]{0:T(128)}, s32[32]{0:T(128)S(1)}, u32[]{:S(2)}) copy-start(s32[32]{0:T(128)S(1)} %get-tuple-element.102.position) | copy-start | bytes 388
  10.8 16.2 %all-to-all-start = ((s32[32,1,8]{2,1,0:T(1,128)}), s32[32,1,8]{2,1,0:T(1,128)S(1)}, u32[]{:S(2)}, u32[]{:S(2)}) async-start(s32[32,1,8]{2,1,0:T(1,128)} %copy.44), calls=%async_computation | async-start | bytes 32768 | tf_op jit(solution)/shard_map/all_to_all | solution.py:474
  19.1 18.2 %collective-permute-start.5 = (bf16[64,2048]{1,0:T(8,128)(2,1)}, bf16[64,2048]{1,0:T(8,128)(2,1)S(1)}, u32[]{:S(2)}, u32[]{:S(2)}) collective-permute-start(bf16[64,2048]{1,0:T(8,128)(2,1)} %get-tuple-element.99), channel_id=1, source_target_pairs={{1,0},{2,1},{3,2},{4,3},{5,4},{6,5},{7,6},{8,7},{9,8},{10,9},{11,1... | collective-permute-start | bytes 786440 | tf_op jit(solution)/shard_map/ppermute | solution.py:469
  21.3 16.0 %collective-permute-start.4 = (bf16[64,2048]{1,0:T(8,128)(2,1)}, bf16[64,2048]{1,0:T(8,128)(2,1)S(1)}, u32[]{:S(2)}, u32[]{:S(2)}) collective-permute-start(bf16[64,2048]{1,0:T(8,128)(2,1)} %get-tuple-element.100), channel_id=1, source_target_pairs={{0,1},{1,2},{2,3},{3,4},{4,5},{5,6},{6,7},{7,8},{8,9},{9,10},{10,1... | collective-permute-start | bytes 786440 | tf_op jit(solution)/shard_map/ppermute | solution.py:468
  28.5 17.9 %collective-permute-start.12 = (bf16[8,80,128]{2,1,0:T(8,128)(2,1)S(1)}, bf16[8,80,128]{2,1,0:T(8,128)(2,1)S(1)}, u32[]{:S(2)}, u32[]{:S(2)}) collective-permute-start(bf16[8,80,128]{2,1,0:T(8,128)(2,1)S(1)} %get-tuple-element.56.refs_0_), channel_id=1, source_target_pairs={{0,8},{4,12},{8,0},{12,4},{1,9},{5,13},{9,1},{13,5},{2,10},{6,14},... | collective-permute-start | bytes 491528 | tf_op jit(solution)/shard_map/ppermute | solution.py:532
  28.6 17.8 %collective-permute-start.11 = (bf16[8,80,128]{2,1,0:T(8,128)(2,1)S(1)}, bf16[8,80,128]{2,1,0:T(8,128)(2,1)}, u32[]{:S(2)}, u32[]{:S(2)}) collective-permute-start(bf16[8,80,128]{2,1,0:T(8,128)(2,1)S(1)} %get-tuple-element.56.refs_0_), channel_id=1, source_target_pairs={{0,4},{4,8},{8,12},{12,0},{1,5},{5,9},{9,13},{13,1},{2,6},{6,10},{... | collective-permute-start | bytes 491528 | tf_op jit(solution)/shard_map/ppermute | solution.py:532
  30.0 14.0 %collective-permute-start.3 = (bf16[8,80,128]{2,1,0:T(8,128)(2,1)S(1)}, bf16[8,80,128]{2,1,0:T(8,128)(2,1)S(1)}, u32[]{:S(2)}, u32[]{:S(2)}) collective-permute-start(bf16[8,80,128]{2,1,0:T(8,128)(2,1)S(1)} %get-tuple-element.56.refs_0_), channel_id=1, source_target_pairs={{0,12},{4,0},{8,4},{12,8},{1,13},{5,1},{9,5},{13,9},{2,14},{6,2},{... | collective-permute-start | bytes 491528 | tf_op jit(solution)/shard_map/ppermute | solution.py:532
  32.6 18.1 %all-to-all-start.2 = ((bf16[64,64,128]{2,1,0:T(8,128)(2,1)}), bf16[64,64,128]{2,1,0:T(8,128)(2,1)S(1)}, u32[]{:S(2)}, u32[]{:S(2)}) async-start(bf16[64,64,128]{2,1,0:T(8,128)(2,1)} %pack_1a.1), calls=%async_computation.2 | async-start | bytes 2097152 | tf_op jit(solution)/shard_map/all_to_all | solution.py:474
  37.3 12.2 %copy-start.22 = (bf16[64,2048]{1,0:T(8,128)(2,1)}, bf16[64,2048]{1,0:T(8,128)(2,1)S(1)}, u32[]{:S(2)}) copy-start(bf16[64,2048]{1,0:T(8,128)(2,1)S(1)} %collective-permute-done.5.below) | copy-start | bytes 786436
  44.7 21.7 %collective-permute-start.8 = (bf16[8,144,128]{2,1,0:T(8,128)(2,1)S(1)}, bf16[8,144,128]{2,1,0:T(8,128)(2,1)S(1)}, u32[]{:S(2)}, u32[]{:S(2)}) collective-permute-start(bf16[8,144,128]{2,1,0:T(8,128)(2,1)S(1)} %wire_0.1.refs_0_), channel_id=1, source_target_pairs={{0,12},{4,0},{8,4},{12,8},{1,13},{5,1},{9,5},{13,9},{2,14},{6,2},{... | collective-permute-start | bytes 884744 | tf_op jit(solution)/shard_map/ppermute | solution.py:532
  44.7 21.7 %collective-permute-start.7 = (bf16[8,144,128]{2,1,0:T(8,128)(2,1)S(1)}, bf16[8,144,128]{2,1,0:T(8,128)(2,1)S(1)}, u32[]{:S(2)}, u32[]{:S(2)}) collective-permute-start(bf16[8,144,128]{2,1,0:T(8,128)(2,1)S(1)} %wire_0.1.refs_0_), channel_id=1, source_target_pairs={{0,8},{4,12},{8,0},{12,4},{1,9},{5,13},{9,1},{13,5},{2,10},{6,14},... | collective-permute-start | bytes 884744 | tf_op jit(solution)/shard_map/ppermute | solution.py:532
  45.2 25.4 %collective-permute-start.6 = (bf16[8,144,128]{2,1,0:T(8,128)(2,1)S(1)}, bf16[8,144,128]{2,1,0:T(8,128)(2,1)S(1)}, u32[]{:S(2)}, u32[]{:S(2)}) collective-permute-start(bf16[8,144,128]{2,1,0:T(8,128)(2,1)S(1)} %wire_0.1.refs_0_), channel_id=1, source_target_pairs={{0,4},{4,8},{8,12},{12,0},{1,5},{5,9},{9,13},{13,1},{2,6},{6,10},{... | collective-permute-start | bytes 884744 | tf_op jit(solution)/shard_map/ppermute | solution.py:532
  51.8 21.0 %all-to-all-start.3 = ((bf16[64,80,128]{2,1,0:T(8,128)(2,1)}), bf16[64,80,128]{2,1,0:T(8,128)(2,1)S(1)}, u32[]{:S(2)}, u32[]{:S(2)}) async-start(bf16[64,80,128]{2,1,0:T(8,128)(2,1)} %pack_1b.1), calls=%async_computation.3 | async-start | bytes 2621440 | tf_op jit(solution)/shard_map/all_to_all | solution.py:474
  72.8 33.9 %all-to-all-start.1 = ((bf16[64,144,128]{2,1,0:T(8,128)(2,1)}), bf16[64,144,128]{2,1,0:T(8,128)(2,1)}, u32[]{:S(2)}, u32[]{:S(2)}) async-start(bf16[64,144,128]{2,1,0:T(8,128)(2,1)} %copy-done.16), calls=%async_computation.1 | async-start | bytes 4718592 | tf_op jit(solution)/shard_map/all_to_all | solution.py:474
  78.4 41.7 %copy-start.26 = (s32[32]{0:T(128)}, s32[32]{0:T(128)S(1)}, u32[]{:S(2)}) copy-start(s32[32]{0:T(128)S(1)} %reshape.245.listed) | copy-start | bytes 388
  88.0 32.1 %collective-permute-start.14 = (bf16[64,2048]{1,0:T(8,128)(2,1)}, bf16[64,2048]{1,0:T(8,128)(2,1)S(1)}, u32[]{:S(2)}, u32[]{:S(2)}) collective-permute-start(bf16[64,2048]{1,0:T(8,128)(2,1)} %get-tuple-element.95), channel_id=1, source_target_pairs={{1,0},{2,1},{3,2},{4,3},{5,4},{6,5},{7,6},{8,7},{9,8},{10,9},{11,1... | collective-permute-start | bytes 786440 | tf_op jit(solution)/shard_map/ppermute | solution.py:469
  90.3 29.8 %collective-permute-start.13 = (bf16[64,2048]{1,0:T(8,128)(2,1)}, bf16[64,2048]{1,0:T(8,128)(2,1)}, u32[]{:S(2)}, u32[]{:S(2)}) collective-permute-start(bf16[64,2048]{1,0:T(8,128)(2,1)} %get-tuple-element.96), channel_id=1, source_target_pairs={{0,1},{1,2},{2,3},{3,4},{4,5},{5,6},{6,7},{7,8},{8,9},{9,10},{10,1... | collective-permute-start | bytes 786440 | tf_op jit(solution)/shard_map/ppermute | solution.py:468
  107.8 12.4 %copy-start.14 = (bf16[64,2,2048]{2,0,1:T(8,128)(2,1)S(1)}, bf16[64,2,2048]{2,0,1:T(8,128)(2,1)}, u32[]{:S(2)}) copy-start(bf16[64,2,2048]{2,0,1:T(8,128)(2,1)} %copy-done.13) | copy-start | bytes 1572868
  107.8 12.4 %copy-start.20 = (f32[2,64,2048]{2,1,0:T(8,128)S(1)}, f32[2,64,2048]{2,1,0:T(8,128)}, u32[]{:S(2)}) copy-start(f32[2,64,2048]{2,1,0:T(8,128)} %copy-done.19) | copy-start | bytes 3145732
  107.8 12.4 %copy-start.29 = (s32[32]{0:T(128)S(1)}, s32[32]{0:T(128)}, u32[]{:S(2)}) copy-start(s32[32]{0:T(128)} %copy-done.28) | copy-start | bytes 388
  111.3 12.4 %copy-start.7 = (bf16[2,64,2048]{2,1,0:T(8,128)(2,1)}, bf16[2,64,2048]{2,1,0:T(8,128)(2,1)S(1)}, u32[]{:S(2)}) copy-start(bf16[2,64,2048]{2,1,0:T(8,128)(2,1)S(1)} %conv_0.1.hidden.middle) | copy-start | bytes 1572868
  111.4 14.5 %collective-permute-start.10 = (bf16[64,2048]{1,0:T(8,128)(2,1)S(1)}, bf16[64,2048]{1,0:T(8,128)(2,1)S(1)}, u32[]{:S(2)}, u32[]{:S(2)}) collective-permute-start(bf16[64,2048]{1,0:T(8,128)(2,1)S(1)} %get-tuple-element.97), channel_id=1, source_target_pairs={{1,0},{2,1},{3,2},{4,3},{5,4},{6,5},{7,6},{8,7},{9,8},{10,9},{11,1... | collective-permute-start | bytes 786440 | tf_op jit(solution)/shard_map/ppermute | solution.py:469
  115.2 10.7 %collective-permute-start.9 = (bf16[64,2048]{1,0:T(8,128)(2,1)S(1)}, bf16[64,2048]{1,0:T(8,128)(2,1)S(1)}, u32[]{:S(2)}, u32[]{:S(2)}) collective-permute-start(bf16[64,2048]{1,0:T(8,128)(2,1)S(1)} %get-tuple-element.98), channel_id=1, source_target_pairs={{0,1},{1,2},{2,3},{3,4},{4,5},{5,6},{6,7},{7,8},{8,9},{9,10},{10,1... | collective-permute-start | bytes 786440 | tf_op jit(solution)/shard_map/ppermute | solution.py:468
  127.4 59.8 %all-to-all-start.5 = ((bf16[32,288,128]{2,1,0:T(8,128)(2,1)}), bf16[32,288,128]{2,1,0:T(8,128)(2,1)S(1)}, u32[]{:S(2)}, u32[]{:S(2)}) async-start(bf16[32,288,128]{2,1,0:T(8,128)(2,1)} %copy-done.15), calls=%async_computation.5 | async-start | bytes 4718592 | tf_op jit(solution)/shard_map/all_to_all | solution.py:474
  138.7 48.5 %collective-permute-start.16 = (bf16[64,2048]{1,0:T(8,128)(2,1)S(1)}, bf16[64,2048]{1,0:T(8,128)(2,1)S(1)}, u32[]{:S(2)}, u32[]{:S(2)}) collective-permute-start(bf16[64,2048]{1,0:T(8,128)(2,1)S(1)} %get-tuple-element.93), channel_id=1, source_target_pairs={{1,0},{2,1},{3,2},{4,3},{5,4},{6,5},{7,6},{8,7},{9,8},{10,9},{11,1... | collective-permute-start | bytes 786440 | tf_op jit(solution)/shard_map/ppermute | solution.py:469
  140.9 46.2 %collective-permute-start.15 = (bf16[64,2048]{1,0:T(8,128)(2,1)S(1)}, bf16[64,2048]{1,0:T(8,128)(2,1)S(1)}, u32[]{:S(2)}, u32[]{:S(2)}) collective-permute-start(bf16[64,2048]{1,0:T(8,128)(2,1)S(1)} %get-tuple-element.94), channel_id=1, source_target_pairs={{0,1},{1,2},{2,3},{3,4},{4,5},{5,6},{6,7},{7,8},{8,9},{9,10},{10,1... | collective-permute-start | bytes 786440 | tf_op jit(solution)/shard_map/ppermute | solution.py:468
  188.6 57.5 %all-to-all-start.4 = ((bf16[32,288,128]{2,1,0:T(8,128)(2,1)}), bf16[32,288,128]{2,1,0:T(8,128)(2,1)S(1)}, u32[]{:S(2)}, u32[]{:S(2)}) async-start(bf16[32,288,128]{2,1,0:T(8,128)(2,1)} %get-tuple-element.79), calls=%async_computation.4 | async-start | bytes 4718592 | tf_op jit(solution)/shard_map/all_to_all | solution.py:474
  (31 other events, 85.8 us)

commit v5 on v4

--- a/solution.py
+++ b/solution.py
@@ -136,7 +136,7 @@
     out, total, natural = rest[-3:]
     total[...] = jnp.zeros_like(total)
 
-    @pl.loop(0, parts.shape[0], unroll=4)
+    @pl.loop(0, parts.shape[0], unroll=8)
     def _(place):
         row = jnp.where(requested[place] < 0, per_dev, requested[place])
         total[pl.ds(pl.multiple_of(row * rows, 8), rows), :] += parts[place].astype(F32)
@@ -281,7 +281,7 @@
     pieces, out = rest[:-1], rest[-1]
     tile_rows, channels, columns = middle.shape
 
-    @pl.loop(0, columns // LANES, unroll=4)
+    @pl.loop(0, columns // LANES, unroll=8)
     def _(band):
         cells = unfolded(shifts, band, tile_rows)
         wide, last = band_weights(pieces, pieces[0].shape[0], position, band)
@@ -332,7 +332,7 @@
     tile_rows, channels, columns = upstream.shape
     fill_shifts(above, middle, below, shifts)
 
-    @pl.loop(0, columns // LANES, unroll=4)
+    @pl.loop(0, columns // LANES, unroll=8)
     def _(band):
         cells = unfolded(shifts, band, tile_rows)
         mask = first_mask(regions, listed, band, channels, tile_rows)
@@ -361,7 +361,7 @@
 ):
     tile_rows, channels, columns = hidden.shape
 
-    @pl.loop(0, columns // LANES, unroll=4)
+    @pl.loop(0, columns // LANES, unroll=8)
     def _(band):
         cells = unfolded(shifts, band, tile_rows)
         mask = first_mask(regions, listed, band, channels, tile_rows)
@@ -404,7 +404,7 @@
     tile_rows, channels, columns = upstream.shape
     total[...] = jnp.zeros_like(total)
 
-    @pl.loop(0, columns // LANES, unroll=4)
+    @pl.loop(0, columns // LANES, unroll=8)
     def _(band):
         wide, last = band_weights(pieces, pieces[0].shape[0], position, band)
         mask = first_mask(regions, listed, band, channels, tile_rows)
@@ -559,7 +559,7 @@
     partial_one, shifts_one = partial_of(*where, upstream, *around, places, groups)
     from_above, from_below, partial_one = after((from_above, from_below), partial_one)
     sent_one = exchange(partial_one, GY)
-    refined = conv(*fetch, hidden, shifts_one, kernel_one, "conv_1", 56)
+    refined = conv(*fetch, hidden, shifts_one, kernel_one, "conv_1")
     back = inner_zero.at[0].add(from_above.astype(F32)).at[last].add(from_below.astype(F32))
     input_grad = (carried.astype(F32) + jnp.where(cells > 0, back, 0.0)).astype(BF16)
     half = total_of(requested, sent_zero, banks, 0, groups)

time: 251 us -> 250 us (level)
    pallas_call x2, Pallas kernels: 8.99 us -> 5.27 us  [conv(): pl.pallas_call(conv_kernel, out_shape=jax.ShapeDtypeStruct(middle.shape,...]
    unnamed x85 -> x95, local copies, waits for them, and re-layouts: 22.6 us -> 22 us
  transfers between devices with their start and end apart: 23 -> 23, of which waited for: 7 -> 7; matrix products, arithmetic and copies ran while one was open for 5% -> 5% of each run, Pallas kernels for 16% -> 15%
where the time goes in v5:
time: 250 us; the launch traced here: 249 us
  waiting for transfers between devices  110 us (44%)
  starting transfers between devices  66.5 us (27%)
  Pallas kernels  42 us (17%)
  local copies, waits for them, and re-layouts  28.7 us (11%)
    all_to_all x6, waiting for transfers between devices, exchange(): return lax.all_to_all(value, axes, split_axis=0, concat_axis=0, tiled=True)  53.8 us
    ppermute x4, waiting for transfers between devices, from_neighbours(): below = lax.ppermute(lower, GY, [(i + 1, i) for i in range(count - 1)])  35 us
    all_to_all x6, starting transfers between devices, exchange(): return lax.all_to_all(value, axes, split_axis=0, concat_axis=0, tiled=True)  29.4 us
    unnamed x95, local copies, waits for them, and re-layouts  22 us
    ppermute x9, waiting for transfers between devices, gathered(): return [mine] + [lax.ppermute(mine, 'far', turn) for turn in turns]  21 us
    ppermute x4, starting transfers between devices, from_neighbours(): above = lax.ppermute(upper, GY, [(i, i + 1) for i in range(count - 1)])  18 us
    pallas_call x2, Pallas kernels, spread_of(): pl.pallas_call(spread_kernel, out_shape=(jax.ShapeDtypeStruct(upstream.sh...  10.5 us
    ppermute x4, starting transfers between devices, from_neighbours(): below = lax.ppermute(lower, GY, [(i + 1, i) for i in range(count - 1)])  10.3 us
  transfers between devices with their start and end apart: 23, of which 7 were waited for; matrix products, arithmetic and copies ran while one was open for 5% of the time, Pallas kernels for 15%

profile of v5, /device:TPU:13, one launch (start us, length us, event | category | flops | bytes accessed | tf_op | source)
XLA Modules:
  0.0 249.2 jit_solution(887725698213841746)
XLA Ops:
  3.3 2.3 collective-permute-start.1
  5.6 2.2 collective-permute-start
  10.8 5.4 %all-to-all-start = ((s32[32,1,8]{2,1,0:T(1,128)}), s32[32,1,8]{2,1,0:T(1,128)S(1)}, u32[]{:S(2)}, u32[]{:S(2)}) async-start(s32[32,1,8]{2,1,0:T(1,128)} %copy.44), calls=%async_computation | async-start | bytes 32768 | tf_op jit(solution)/shard_map/all_to_all | solution.py:474
  19.1 2.3 collective-permute-start.5
  21.4 4.2 %collective-permute-start.4 = (bf16[64,2048]{1,0:T(8,128)(2,1)}, bf16[64,2048]{1,0:T(8,128)(2,1)S(1)}, u32[]{:S(2)}, u32[]{:S(2)}) collective-permute-start(bf16[64,2048]{1,0:T(8,128)(2,1)} %get-tuple-element.100), channel_id=1, source_target_pairs={{0,1},{1,2},{2,3},{3,4},{4,5},{5,6},{6,7},{7,8},{8,9},{9,10},{10,1... | collective-permute-start | bytes 786440 | tf_op jit(solution)/shard_map/ppermute | solution.py:468
  32.7 4.6 %all-to-all-start.2 = ((bf16[64,64,128]{2,1,0:T(8,128)(2,1)}), bf16[64,64,128]{2,1,0:T(8,128)(2,1)S(1)}, u32[]{:S(2)}, u32[]{:S(2)}) async-start(bf16[64,64,128]{2,1,0:T(8,128)(2,1)} %pack_1a.1), calls=%async_computation.2 | async-start | bytes 2097152 | tf_op jit(solution)/shard_map/all_to_all | solution.py:474
  37.3 6.7 %collective-permute-done.3.refs_3_ = bf16[8,80,128]{2,1,0:T(8,128)(2,1)S(1)} collective-permute-done((bf16[8,80,128]{2,1,0:T(8,128)(2,1)S(1)}, bf16[8,80,128]{2,1,0:T(8,128)(2,1)S(1)}, u32[]{:S(2)}, u32[]{:S(2)}) %collective-permute-start.3) | collective-permute-done | bytes 163872 | tf_op jit(solution)/shard_map/ppermute | solution.py:532
  47.3 2.1 pack_1b.1
  51.8 4.5 %all-to-all-start.3 = ((bf16[64,80,128]{2,1,0:T(8,128)(2,1)}), bf16[64,80,128]{2,1,0:T(8,128)(2,1)S(1)}, u32[]{:S(2)}, u32[]{:S(2)}) async-start(bf16[64,80,128]{2,1,0:T(8,128)(2,1)} %pack_1b.1), calls=%async_computation.3 | async-start | bytes 2621440 | tf_op jit(solution)/shard_map/all_to_all | solution.py:474
  56.3 10.1 %collective-permute-done.8.refs_3_ = bf16[8,144,128]{2,1,0:T(8,128)(2,1)S(1)} collective-permute-done((bf16[8,144,128]{2,1,0:T(8,128)(2,1)S(1)}, bf16[8,144,128]{2,1,0:T(8,128)(2,1)S(1)}, u32[]{:S(2)}, u32[]{:S(2)}) %collective-permute-start.8) | collective-permute-done | bytes 294944 | tf_op jit(solution)/shard_map/ppermute | solution.py:532
  66.4 4.2 %collective-permute-done.6.refs_1_ = bf16[8,144,128]{2,1,0:T(8,128)(2,1)S(1)} collective-permute-done((bf16[8,144,128]{2,1,0:T(8,128)(2,1)S(1)}, bf16[8,144,128]{2,1,0:T(8,128)(2,1)S(1)}, u32[]{:S(2)}, u32[]{:S(2)}) %collective-permute-start.6) | collective-permute-done | bytes 294944 | tf_op jit(solution)/shard_map/ppermute | solution.py:532
  72.8 5.5 %all-to-all-start.1 = ((bf16[64,144,128]{2,1,0:T(8,128)(2,1)}), bf16[64,144,128]{2,1,0:T(8,128)(2,1)}, u32[]{:S(2)}, u32[]{:S(2)}) async-start(bf16[64,144,128]{2,1,0:T(8,128)(2,1)} %copy-done.18), calls=%async_computation.1 | async-start | bytes 4718592 | tf_op jit(solution)/shard_map/all_to_all | solution.py:474
  82.5 4.0 %spread_1.1 = (f32[2,64,2048]{2,1,0:T(8,128)S(1)}, bf16[2,64,2048]{2,1,0:T(8,128)(2,1)S(1)}) custom-call(s32[32]{0:T(128)S(1)} %get-tuple-element.102.position, s32[32]{0:T(128)S(1)} %reshape.245.listed, s32[2,2048]{1,0:T(2,128)S(1)} %copy-done.23, bf16[2,64,2048]{2,1,0:T(8,128)(2,1)S(1)} %bitcast.60, bf16[2,32,64,128]{3,2,1,0:T(8,128)(2,1)S(1)} %bitcast.55, ...), custom_call_target="tpu_custom_call" | custom-call | flops 603979776 | bytes 5000000 | tf_op jit(solution)/shard_map/spread_1/pallas_call | solution.py:446
  88.3 2.3 collective-permute-start.14
  90.5 4.2 %collective-permute-start.13 = (bf16[64,2048]{1,0:T(8,128)(2,1)}, bf16[64,2048]{1,0:T(8,128)(2,1)}, u32[]{:S(2)}, u32[]{:S(2)}) collective-permute-start(bf16[64,2048]{1,0:T(8,128)(2,1)} %get-tuple-element.96), channel_id=1, source_target_pairs={{0,1},{1,2},{2,3},{3,4},{4,5},{5,6},{6,7},{7,8},{8,9},{9,10},{10,1... | collective-permute-start | bytes 786440 | tf_op jit(solution)/shard_map/ppermute | solution.py:468
  94.8 12.0 %all-to-all-done.1 = bf16[64,144,128]{2,1,0:T(8,128)(2,1)} async-done(((bf16[64,144,128]{2,1,0:T(8,128)(2,1)}), bf16[64,144,128]{2,1,0:T(8,128)(2,1)}, u32[]{:S(2)}, u32[]{:S(2)}) %all-to-all-start.1) | async-done | bytes 2359328 | tf_op jit(solution)/shard_map/all_to_all | solution.py:474
  107.9 3.2 %conv_0.1.hidden.middle = bf16[2,64,2048]{2,1,0:T(8,128)(2,1)S(1)} custom-call(s32[32]{0:T(128)S(1)} %get-tuple-element.102.position, s32[32]{0:T(128)S(1)} %reshape.245.listed, s32[2,2048]{1,0:T(2,128)S(1)} %copy-done.23, bf16[2,64,2048]{2,1,0:T(8,128)(2,1)S(1)} %bitcast.59, bf16[3,4,64,2048]{3,2,1,0:T(8,128)(2,1)S(1)} %shift_0.1.shifts, ...), custom_call_target="tpu_custom_call" | custom-call | flops 603979776 | bytes 5000000 | tf_op jit(solution)/shard_map/conv_0/pallas_call | solution.py:299
  111.2 3.8 %collective-permute-start.10 = (bf16[64,2048]{1,0:T(8,128)(2,1)S(1)}, bf16[64,2048]{1,0:T(8,128)(2,1)S(1)}, u32[]{:S(2)}, u32[]{:S(2)}) collective-permute-start(bf16[64,2048]{1,0:T(8,128)(2,1)S(1)} %get-tuple-element.97), channel_id=1, source_target_pairs={{1,0},{2,1},{3,2},{4,3},{5,4},{6,5},{7,6},{8,7},{9,8},{10,9},{11,1... | collective-permute-start | bytes 786440 | tf_op jit(solution)/shard_map/ppermute | solution.py:469
  115.0 4.9 %collective-permute-start.9 = (bf16[64,2048]{1,0:T(8,128)(2,1)S(1)}, bf16[64,2048]{1,0:T(8,128)(2,1)S(1)}, u32[]{:S(2)}, u32[]{:S(2)}) collective-permute-start(bf16[64,2048]{1,0:T(8,128)(2,1)S(1)} %get-tuple-element.98), channel_id=1, source_target_pairs={{0,1},{1,2},{2,3},{3,4},{4,5},{5,6},{6,7},{7,8},{8,9},{9,10},{10,1... | collective-permute-start | bytes 786440 | tf_op jit(solution)/shard_map/ppermute | solution.py:468
  119.9 3.2 %carried_partial_0.1 = (bf16[2,64,2048]{2,1,0:T(8,128)(2,1)S(1)}, bf16[32,288,128]{2,1,0:T(8,128)(2,1)S(1)}) custom-call(s32[32]{0:T(128)S(1)} %copy-done.34, s32[32]{0:T(128)S(1)} %reshape.245.listed, s32[2,2048]{1,0:T(2,128)S(1)} %copy-done.23, bf16[2,64,2048]{2,1,0:T(8,128)(2,1)S(1)} %bitcast.62, bf16[2,64,2048]{2,1,0:T(8,128)(2,1)S(1)} %conv_0.1.hidden.middle, ...), custom_call_target="tpu_custom_call" | custom-call | flops 603979776 | bytes 7000000 | tf_op jit(solution)/shard_map/carried_partial_0/pallas_call | solution.py:388
  126.8 4.3 %all-to-all-start.5 = ((bf16[32,288,128]{2,1,0:T(8,128)(2,1)}), bf16[32,288,128]{2,1,0:T(8,128)(2,1)}, u32[]{:S(2)}, u32[]{:S(2)}) async-start(bf16[32,288,128]{2,1,0:T(8,128)(2,1)} %copy-done.17), calls=%async_computation.5 | async-start | bytes 4718592 | tf_op jit(solution)/shard_map/all_to_all | solution.py:474
  131.1 6.5 %spread_0.1 = (f32[2,64,2048]{2,1,0:T(8,128)}, bf16[2,64,2048]{2,1,0:T(8,128)(2,1)}) custom-call(s32[32]{0:T(128)} %copy-done.31, s32[32]{0:T(128)} %copy-done.29, s32[2,2048]{1,0:T(2,128)} %regions.11, bf16[2,64,2048]{2,1,0:T(8,128)(2,1)} %copy-done.19, bf16[2,32,144,128]{3,2,1,0:T(8,128)(2,1)} %bitcast.10.rest_0_), custom_call_target="tpu_custom_call" | custom-call | flops 603979776 | bytes 5000000 | tf_op jit(solution)/shard_map/spread_0/pallas_call | solution.py:446
  138.7 1.9 collective-permute-start.16
  140.6 4.7 %collective-permute-start.15 = (bf16[64,2048]{1,0:T(8,128)(2,1)S(1)}, bf16[64,2048]{1,0:T(8,128)(2,1)S(1)}, u32[]{:S(2)}, u32[]{:S(2)}) collective-permute-start(bf16[64,2048]{1,0:T(8,128)(2,1)S(1)} %get-tuple-element.94), channel_id=1, source_target_pairs={{0,1},{1,2},{2,3},{3,4},{4,5},{5,6},{6,7},{7,8},{8,9},{9,10},{10,1... | collective-permute-start | bytes 786440 | tf_op jit(solution)/shard_map/ppermute | solution.py:468
  145.3 6.3 %partial_1.1 = (bf16[32,288,128]{2,1,0:T(8,128)(2,1)}, bf16[3,4,64,2048]{3,2,1,0:T(8,128)(2,1)}) custom-call(s32[32]{0:T(128)} %copy-done.33, s32[32]{0:T(128)} %copy-done.29, s32[2,2048]{1,0:T(2,128)} %regions.11, bf16[2,64,2048]{2,1,0:T(8,128)(2,1)} %bitcast.61, bf16[64,2048]{1,0:T(8,128)(2,1)} %copy-done.44, bf16[2,64,2048]{2,1,0:T(8,128)(2,1)} %copy-done.7, ...), custom_call_target="tpu_custom_call" | custom-call | flops 603979776 | bytes 8000000 | tf_op jit(solution)/shard_map/partial_1/pallas_call | solution.py:345
  151.6 35.0 %collective-permute-done.16 = bf16[64,2048]{1,0:T(8,128)(2,1)S(1)} collective-permute-done((bf16[64,2048]{1,0:T(8,128)(2,1)S(1)}, bf16[64,2048]{1,0:T(8,128)(2,1)S(1)}, u32[]{:S(2)}, u32[]{:S(2)}) %collective-permute-start.16) | collective-permute-done | bytes 262176 | tf_op jit(solution)/shard_map/ppermute | solution.py:469
  186.6 4.9 %all-to-all-start.4 = ((bf16[32,288,128]{2,1,0:T(8,128)(2,1)}), bf16[32,288,128]{2,1,0:T(8,128)(2,1)}, u32[]{:S(2)}, u32[]{:S(2)}) async-start(bf16[32,288,128]{2,1,0:T(8,128)(2,1)} %get-tuple-element.79), calls=%async_computation.4 | async-start | bytes 4718592 | tf_op jit(solution)/shard_map/all_to_all | solution.py:474
  192.5 1.9 copy-done.16
  194.4 2.0 conv_1.1
  199.7 4.5 %total_0.1.rest_0_ = f32[2,8,36864]{2,1,0:T(8,128)} custom-call(s32[32]{0:T(128)S(1)} %reshape.254.requested, bf16[32,288,128]{2,1,0:T(8,128)(2,1)} %all-to-all-done.5.parts), custom_call_target="tpu_custom_call" | custom-call | flops 1000000 | bytes 3538944 | tf_op jit(solution)/shard_map/total_0/pallas_call | solution.py:172
  204.2 40.5 %all-to-all-done.4.parts = bf16[32,288,128]{2,1,0:T(8,128)(2,1)} async-done(((bf16[32,288,128]{2,1,0:T(8,128)(2,1)}), bf16[32,288,128]{2,1,0:T(8,128)(2,1)}, u32[]{:S(2)}, u32[]{:S(2)}) %all-to-all-start.4) | async-done | bytes 2359328 | tf_op jit(solution)/shard_map/all_to_all | solution.py:474
  244.7 4.5 %total_1.1 = f32[2,8,36864]{2,1,0:T(8,128)} custom-call(s32[32]{0:T(128)S(1)} %reshape.254.requested, bf16[32,288,128]{2,1,0:T(8,128)(2,1)} %all-to-all-done.4.parts, f32[2,8,36864]{2,1,0:T(8,128)} %total_0.1.rest_0_), custom_call_target="tpu_custom_call", output_to_operand_aliasing={{}: (2, {})} | custom-call | flops 1000000 | bytes 3538944 | tf_op jit(solution)/shard_map/total_1/pallas_call | solution.py:172
  (159 shorter events, 39.0 us)
Async XLA Ops:
  1.9 23.8 %copy-start.13 = (bf16[2,8,36864]{2,1,0:T(8,128)(2,1)S(1)}, bf16[2,8,36864]{2,1,0:T(8,128)(2,1)}, u32[]{:S(2)}) copy-start(bf16[2,8,36864]{2,1,0:T(8,128)(2,1)} %banks.3) | copy-start | bytes 3538948
  3.1 25.4 %collective-permute-start.2 = (bf16[8,64,128]{2,1,0:T(8,128)(2,1)S(1)}, bf16[8,64,128]{2,1,0:T(8,128)(2,1)S(1)}, u32[]{:S(2)}, u32[]{:S(2)}) collective-permute-start(bf16[8,64,128]{2,1,0:T(8,128)(2,1)S(1)} %get-tuple-element.62.refs_0_), channel_id=1, source_target_pairs={{0,12},{4,0},{8,4},{12,8},{1,13},{5,1},{9,5},{13,9},{2,14},{6,2},{... | collective-permute-start | bytes 393224 | tf_op jit(solution)/shard_map/ppermute | solution.py:532
  3.3 25.2 %collective-permute-start.1 = (bf16[8,64,128]{2,1,0:T(8,128)(2,1)S(1)}, bf16[8,64,128]{2,1,0:T(8,128)(2,1)S(1)}, u32[]{:S(2)}, u32[]{:S(2)}) collective-permute-start(bf16[8,64,128]{2,1,0:T(8,128)(2,1)S(1)} %get-tuple-element.62.refs_0_), channel_id=1, source_target_pairs={{0,8},{4,12},{8,0},{12,4},{1,9},{5,13},{9,1},{13,5},{2,10},{6,14},... | collective-permute-start | bytes 393224 | tf_op jit(solution)/shard_map/ppermute | solution.py:532
  5.6 22.9 %collective-permute-start = (bf16[8,64,128]{2,1,0:T(8,128)(2,1)S(1)}, bf16[8,64,128]{2,1,0:T(8,128)(2,1)S(1)}, u32[]{:S(2)}, u32[]{:S(2)}) collective-permute-start(bf16[8,64,128]{2,1,0:T(8,128)(2,1)S(1)} %get-tuple-element.62.refs_0_), channel_id=1, source_target_pairs={{0,4},{4,8},{8,12},{12,0},{1,5},{5,9},{9,13},{13,1},{2,6},{6,10},{... | collective-permute-start | bytes 393224 | tf_op jit(solution)/shard_map/ppermute | solution.py:532
  9.7 23.0 %copy-start.33 = (s32[32]{0:T(128)}, s32[32]{0:T(128)S(1)}, u32[]{:S(2)}) copy-start(s32[32]{0:T(128)S(1)} %get-tuple-element.101.position) | copy-start | bytes 388
  9.7 97.1 %copy-start.31 = (s32[32]{0:T(128)}, s32[32]{0:T(128)S(1)}, u32[]{:S(2)}) copy-start(s32[32]{0:T(128)S(1)} %get-tuple-element.102.position) | copy-start | bytes 388
  10.8 16.2 %all-to-all-start = ((s32[32,1,8]{2,1,0:T(1,128)}), s32[32,1,8]{2,1,0:T(1,128)S(1)}, u32[]{:S(2)}, u32[]{:S(2)}) async-start(s32[32,1,8]{2,1,0:T(1,128)} %copy.44), calls=%async_computation | async-start | bytes 32768 | tf_op jit(solution)/shard_map/all_to_all | solution.py:474
  19.1 18.2 %collective-permute-start.5 = (bf16[64,2048]{1,0:T(8,128)(2,1)}, bf16[64,2048]{1,0:T(8,128)(2,1)S(1)}, u32[]{:S(2)}, u32[]{:S(2)}) collective-permute-start(bf16[64,2048]{1,0:T(8,128)(2,1)} %get-tuple-element.99), channel_id=1, source_target_pairs={{1,0},{2,1},{3,2},{4,3},{5,4},{6,5},{7,6},{8,7},{9,8},{10,9},{11,1... | collective-permute-start | bytes 786440 | tf_op jit(solution)/shard_map/ppermute | solution.py:469
  21.4 16.0 %collective-permute-start.4 = (bf16[64,2048]{1,0:T(8,128)(2,1)}, bf16[64,2048]{1,0:T(8,128)(2,1)S(1)}, u32[]{:S(2)}, u32[]{:S(2)}) collective-permute-start(bf16[64,2048]{1,0:T(8,128)(2,1)} %get-tuple-element.100), channel_id=1, source_target_pairs={{0,1},{1,2},{2,3},{3,4},{4,5},{5,6},{6,7},{7,8},{8,9},{9,10},{10,1... | collective-permute-start | bytes 786440 | tf_op jit(solution)/shard_map/ppermute | solution.py:468
  28.5 17.9 %collective-permute-start.12 = (bf16[8,80,128]{2,1,0:T(8,128)(2,1)S(1)}, bf16[8,80,128]{2,1,0:T(8,128)(2,1)S(1)}, u32[]{:S(2)}, u32[]{:S(2)}) collective-permute-start(bf16[8,80,128]{2,1,0:T(8,128)(2,1)S(1)} %get-tuple-element.56.refs_0_), channel_id=1, source_target_pairs={{0,8},{4,12},{8,0},{12,4},{1,9},{5,13},{9,1},{13,5},{2,10},{6,14},... | collective-permute-start | bytes 491528 | tf_op jit(solution)/shard_map/ppermute | solution.py:532
  28.6 17.8 %collective-permute-start.11 = (bf16[8,80,128]{2,1,0:T(8,128)(2,1)S(1)}, bf16[8,80,128]{2,1,0:T(8,128)(2,1)}, u32[]{:S(2)}, u32[]{:S(2)}) collective-permute-start(bf16[8,80,128]{2,1,0:T(8,128)(2,1)S(1)} %get-tuple-element.56.refs_0_), channel_id=1, source_target_pairs={{0,4},{4,8},{8,12},{12,0},{1,5},{5,9},{9,13},{13,1},{2,6},{6,10},{... | collective-permute-start | bytes 491528 | tf_op jit(solution)/shard_map/ppermute | solution.py:532
  30.1 14.0 %collective-permute-start.3 = (bf16[8,80,128]{2,1,0:T(8,128)(2,1)S(1)}, bf16[8,80,128]{2,1,0:T(8,128)(2,1)S(1)}, u32[]{:S(2)}, u32[]{:S(2)}) collective-permute-start(bf16[8,80,128]{2,1,0:T(8,128)(2,1)S(1)} %get-tuple-element.56.refs_0_), channel_id=1, source_target_pairs={{0,12},{4,0},{8,4},{12,8},{1,13},{5,1},{9,5},{13,9},{2,14},{6,2},{... | collective-permute-start | bytes 491528 | tf_op jit(solution)/shard_map/ppermute | solution.py:532
  32.7 18.1 %all-to-all-start.2 = ((bf16[64,64,128]{2,1,0:T(8,128)(2,1)}), bf16[64,64,128]{2,1,0:T(8,128)(2,1)S(1)}, u32[]{:S(2)}, u32[]{:S(2)}) async-start(bf16[64,64,128]{2,1,0:T(8,128)(2,1)} %pack_1a.1), calls=%async_computation.2 | async-start | bytes 2097152 | tf_op jit(solution)/shard_map/all_to_all | solution.py:474
  37.3 12.2 %copy-start.25 = (bf16[64,2048]{1,0:T(8,128)(2,1)}, bf16[64,2048]{1,0:T(8,128)(2,1)S(1)}, u32[]{:S(2)}) copy-start(bf16[64,2048]{1,0:T(8,128)(2,1)S(1)} %collective-permute-done.5.below) | copy-start | bytes 786436
  37.3 12.2 %copy-start.27 = (bf16[64,2048]{1,0:T(8,128)(2,1)}, bf16[64,2048]{1,0:T(8,128)(2,1)S(1)}, u32[]{:S(2)}) copy-start(bf16[64,2048]{1,0:T(8,128)(2,1)S(1)} %collective-permute-done.4.above) | copy-start | bytes 786436
  44.8 21.7 %collective-permute-start.8 = (bf16[8,144,128]{2,1,0:T(8,128)(2,1)S(1)}, bf16[8,144,128]{2,1,0:T(8,128)(2,1)S(1)}, u32[]{:S(2)}, u32[]{:S(2)}) collective-permute-start(bf16[8,144,128]{2,1,0:T(8,128)(2,1)S(1)} %wire_0.1.refs_0_), channel_id=1, source_target_pairs={{0,12},{4,0},{8,4},{12,8},{1,13},{5,1},{9,5},{13,9},{2,14},{6,2},{... | collective-permute-start | bytes 884744 | tf_op jit(solution)/shard_map/ppermute | solution.py:532
  44.8 21.7 %collective-permute-start.7 = (bf16[8,144,128]{2,1,0:T(8,128)(2,1)S(1)}, bf16[8,144,128]{2,1,0:T(8,128)(2,1)S(1)}, u32[]{:S(2)}, u32[]{:S(2)}) collective-permute-start(bf16[8,144,128]{2,1,0:T(8,128)(2,1)S(1)} %wire_0.1.refs_0_), channel_id=1, source_target_pairs={{0,8},{4,12},{8,0},{12,4},{1,9},{5,13},{9,1},{13,5},{2,10},{6,14},... | collective-permute-start | bytes 884744 | tf_op jit(solution)/shard_map/ppermute | solution.py:532
  45.2 25.4 %collective-permute-start.6 = (bf16[8,144,128]{2,1,0:T(8,128)(2,1)S(1)}, bf16[8,144,128]{2,1,0:T(8,128)(2,1)S(1)}, u32[]{:S(2)}, u32[]{:S(2)}) collective-permute-start(bf16[8,144,128]{2,1,0:T(8,128)(2,1)S(1)} %wire_0.1.refs_0_), channel_id=1, source_target_pairs={{0,4},{4,8},{8,12},{12,0},{1,5},{5,9},{9,13},{13,1},{2,6},{6,10},{... | collective-permute-start | bytes 884744 | tf_op jit(solution)/shard_map/ppermute | solution.py:532
  51.8 21.0 %all-to-all-start.3 = ((bf16[64,80,128]{2,1,0:T(8,128)(2,1)}), bf16[64,80,128]{2,1,0:T(8,128)(2,1)S(1)}, u32[]{:S(2)}, u32[]{:S(2)}) async-start(bf16[64,80,128]{2,1,0:T(8,128)(2,1)} %pack_1b.1), calls=%async_computation.3 | async-start | bytes 2621440 | tf_op jit(solution)/shard_map/all_to_all | solution.py:474
  72.8 34.0 %all-to-all-start.1 = ((bf16[64,144,128]{2,1,0:T(8,128)(2,1)}), bf16[64,144,128]{2,1,0:T(8,128)(2,1)}, u32[]{:S(2)}, u32[]{:S(2)}) async-start(bf16[64,144,128]{2,1,0:T(8,128)(2,1)} %copy-done.18), calls=%async_computation.1 | async-start | bytes 4718592 | tf_op jit(solution)/shard_map/all_to_all | solution.py:474
  78.5 41.4 %copy-start.29 = (s32[32]{0:T(128)}, s32[32]{0:T(128)S(1)}, u32[]{:S(2)}) copy-start(s32[32]{0:T(128)S(1)} %reshape.245.listed) | copy-start | bytes 388
  88.3 31.6 %collective-permute-start.14 = (bf16[64,2048]{1,0:T(8,128)(2,1)}, bf16[64,2048]{1,0:T(8,128)(2,1)S(1)}, u32[]{:S(2)}, u32[]{:S(2)}) collective-permute-start(bf16[64,2048]{1,0:T(8,128)(2,1)} %get-tuple-element.95), channel_id=1, source_target_pairs={{1,0},{2,1},{3,2},{4,3},{5,4},{6,5},{7,6},{8,7},{9,8},{10,9},{11,1... | collective-permute-start | bytes 786440 | tf_op jit(solution)/shard_map/ppermute | solution.py:469
  90.5 29.3 %collective-permute-start.13 = (bf16[64,2048]{1,0:T(8,128)(2,1)}, bf16[64,2048]{1,0:T(8,128)(2,1)}, u32[]{:S(2)}, u32[]{:S(2)}) collective-permute-start(bf16[64,2048]{1,0:T(8,128)(2,1)} %get-tuple-element.96), channel_id=1, source_target_pairs={{0,1},{1,2},{2,3},{3,4},{4,5},{5,6},{6,7},{7,8},{8,9},{9,10},{10,1... | collective-permute-start | bytes 786440 | tf_op jit(solution)/shard_map/ppermute | solution.py:468
  107.8 12.1 %copy-start.15 = (bf16[64,2,2048]{2,0,1:T(8,128)(2,1)S(1)}, bf16[64,2,2048]{2,0,1:T(8,128)(2,1)}, u32[]{:S(2)}) copy-start(bf16[64,2,2048]{2,0,1:T(8,128)(2,1)} %copy-done.14) | copy-start | bytes 1572868
  107.8 12.1 %copy-start.22 = (f32[2,64,2048]{2,1,0:T(8,128)S(1)}, f32[2,64,2048]{2,1,0:T(8,128)}, u32[]{:S(2)}) copy-start(f32[2,64,2048]{2,1,0:T(8,128)} %copy-done.21) | copy-start | bytes 3145732
  107.8 12.1 %copy-start.34 = (s32[32]{0:T(128)S(1)}, s32[32]{0:T(128)}, u32[]{:S(2)}) copy-start(s32[32]{0:T(128)} %copy-done.33) | copy-start | bytes 388
  111.2 14.2 %collective-permute-start.10 = (bf16[64,2048]{1,0:T(8,128)(2,1)S(1)}, bf16[64,2048]{1,0:T(8,128)(2,1)S(1)}, u32[]{:S(2)}, u32[]{:S(2)}) collective-permute-start(bf16[64,2048]{1,0:T(8,128)(2,1)S(1)} %get-tuple-element.97), channel_id=1, source_target_pairs={{1,0},{2,1},{3,2},{4,3},{5,4},{6,5},{7,6},{8,7},{9,8},{10,9},{11,1... | collective-permute-start | bytes 786440 | tf_op jit(solution)/shard_map/ppermute | solution.py:469
  115.0 10.3 %collective-permute-start.9 = (bf16[64,2048]{1,0:T(8,128)(2,1)S(1)}, bf16[64,2048]{1,0:T(8,128)(2,1)S(1)}, u32[]{:S(2)}, u32[]{:S(2)}) collective-permute-start(bf16[64,2048]{1,0:T(8,128)(2,1)S(1)} %get-tuple-element.98), channel_id=1, source_target_pairs={{0,1},{1,2},{2,3},{3,4},{4,5},{5,6},{6,7},{7,8},{8,9},{9,10},{10,1... | collective-permute-start | bytes 786440 | tf_op jit(solution)/shard_map/ppermute | solution.py:468
  126.8 59.9 %all-to-all-start.5 = ((bf16[32,288,128]{2,1,0:T(8,128)(2,1)}), bf16[32,288,128]{2,1,0:T(8,128)(2,1)}, u32[]{:S(2)}, u32[]{:S(2)}) async-start(bf16[32,288,128]{2,1,0:T(8,128)(2,1)} %copy-done.17), calls=%async_computation.5 | async-start | bytes 4718592 | tf_op jit(solution)/shard_map/all_to_all | solution.py:474
  138.7 47.9 %collective-permute-start.16 = (bf16[64,2048]{1,0:T(8,128)(2,1)S(1)}, bf16[64,2048]{1,0:T(8,128)(2,1)S(1)}, u32[]{:S(2)}, u32[]{:S(2)}) collective-permute-start(bf16[64,2048]{1,0:T(8,128)(2,1)S(1)} %get-tuple-element.93), channel_id=1, source_target_pairs={{1,0},{2,1},{3,2},{4,3},{5,4},{6,5},{7,6},{8,7},{9,8},{10,9},{11,1... | collective-permute-start | bytes 786440 | tf_op jit(solution)/shard_map/ppermute | solution.py:469
  140.6 46.0 %collective-permute-start.15 = (bf16[64,2048]{1,0:T(8,128)(2,1)S(1)}, bf16[64,2048]{1,0:T(8,128)(2,1)S(1)}, u32[]{:S(2)}, u32[]{:S(2)}) collective-permute-start(bf16[64,2048]{1,0:T(8,128)(2,1)S(1)} %get-tuple-element.94), channel_id=1, source_target_pairs={{0,1},{1,2},{2,3},{3,4},{4,5},{5,6},{6,7},{7,8},{8,9},{9,10},{10,1... | collective-permute-start | bytes 786440 | tf_op jit(solution)/shard_map/ppermute | solution.py:468
  186.6 58.1 %all-to-all-start.4 = ((bf16[32,288,128]{2,1,0:T(8,128)(2,1)}), bf16[32,288,128]{2,1,0:T(8,128)(2,1)}, u32[]{:S(2)}, u32[]{:S(2)}) async-start(bf16[32,288,128]{2,1,0:T(8,128)(2,1)} %get-tuple-element.79), calls=%async_computation.4 | async-start | bytes 4718592 | tf_op jit(solution)/shard_map/all_to_all | solution.py:474
  (36 other events, 113.1 us)

commit v6 on v5

--- a/solution.py
+++ b/solution.py
@@ -141,7 +141,7 @@
         row = jnp.where(requested[place] < 0, per_dev, requested[place])
         total[pl.ds(pl.multiple_of(row * rows, 8), rows), :] += parts[place].astype(F32)
 
-    @pl.loop(0, per_dev, unroll=2)
+    @pl.loop(0, per_dev, unroll=4)
     def _(row):
         base = row * rows
 

time: 250 us -> 250 us (level)
  no operation moved by 1% of the time
where the time goes in v6:
time: 250 us; the launch traced here: 249 us
  waiting for transfers between devices  110 us (44%)
  starting transfers between devices  66.5 us (27%)
  Pallas kernels  41.7 us (17%)
  local copies, waits for them, and re-layouts  28.7 us (11%)
    all_to_all x6, waiting for transfers between devices, exchange(): return lax.all_to_all(value, axes, split_axis=0, concat_axis=0, tiled=True)  53.9 us
    ppermute x4, waiting for transfers between devices, from_neighbours(): below = lax.ppermute(lower, GY, [(i + 1, i) for i in range(count - 1)])  35 us
    all_to_all x6, starting transfers between devices, exchange(): return lax.all_to_all(value, axes, split_axis=0, concat_axis=0, tiled=True)  29.4 us
    unnamed x95, local copies, waits for them, and re-layouts  22 us
    ppermute x9, waiting for transfers between devices, gathered(): return [mine] + [lax.ppermute(mine, 'far', turn) for turn in turns]  21 us
    ppermute x4, starting transfers between devices, from_neighbours(): above = lax.ppermute(upper, GY, [(i, i + 1) for i in range(count - 1)])  18 us
    pallas_call x2, Pallas kernels, spread_of(): pl.pallas_call(spread_kernel, out_shape=(jax.ShapeDtypeStruct(upstream.sh...  10.5 us
    ppermute x4, starting transfers between devices, from_neighbours(): below = lax.ppermute(lower, GY, [(i + 1, i) for i in range(count - 1)])  10.3 us
  transfers between devices with their start and end apart: 23, of which 7 were waited for; matrix products, arithmetic and copies ran while one was open for 5% of the time, Pallas kernels for 15%

profile of v6, /device:TPU:13, one launch (start us, length us, event | category | flops | bytes accessed | tf_op | source)
XLA Modules:
  0.0 249.1 jit_solution(8390041115543531151)
XLA Ops:
  3.3 2.3 collective-permute-start.1
  5.6 2.2 collective-permute-start
  10.8 5.4 %all-to-all-start = ((s32[32,1,8]{2,1,0:T(1,128)}), s32[32,1,8]{2,1,0:T(1,128)S(1)}, u32[]{:S(2)}, u32[]{:S(2)}) async-start(s32[32,1,8]{2,1,0:T(1,128)} %copy.44), calls=%async_computation | async-start | bytes 32768 | tf_op jit(solution)/shard_map/all_to_all | solution.py:474
  19.1 2.3 collective-permute-start.5
  21.4 4.2 %collective-permute-start.4 = (bf16[64,2048]{1,0:T(8,128)(2,1)}, bf16[64,2048]{1,0:T(8,128)(2,1)S(1)}, u32[]{:S(2)}, u32[]{:S(2)}) collective-permute-start(bf16[64,2048]{1,0:T(8,128)(2,1)} %get-tuple-element.100), channel_id=1, source_target_pairs={{0,1},{1,2},{2,3},{3,4},{4,5},{5,6},{6,7},{7,8},{8,9},{9,10},{10,1... | collective-permute-start | bytes 786440 | tf_op jit(solution)/shard_map/ppermute | solution.py:468
  32.7 4.6 %all-to-all-start.2 = ((bf16[64,64,128]{2,1,0:T(8,128)(2,1)}), bf16[64,64,128]{2,1,0:T(8,128)(2,1)S(1)}, u32[]{:S(2)}, u32[]{:S(2)}) async-start(bf16[64,64,128]{2,1,0:T(8,128)(2,1)} %pack_1a.1), calls=%async_computation.2 | async-start | bytes 2097152 | tf_op jit(solution)/shard_map/all_to_all | solution.py:474
  37.3 6.7 %collective-permute-done.3.refs_3_ = bf16[8,80,128]{2,1,0:T(8,128)(2,1)S(1)} collective-permute-done((bf16[8,80,128]{2,1,0:T(8,128)(2,1)S(1)}, bf16[8,80,128]{2,1,0:T(8,128)(2,1)S(1)}, u32[]{:S(2)}, u32[]{:S(2)}) %collective-permute-start.3) | collective-permute-done | bytes 163872 | tf_op jit(solution)/shard_map/ppermute | solution.py:532
  47.3 2.1 pack_1b.1
  51.8 4.5 %all-to-all-start.3 = ((bf16[64,80,128]{2,1,0:T(8,128)(2,1)}), bf16[64,80,128]{2,1,0:T(8,128)(2,1)S(1)}, u32[]{:S(2)}, u32[]{:S(2)}) async-start(bf16[64,80,128]{2,1,0:T(8,128)(2,1)} %pack_1b.1), calls=%async_computation.3 | async-start | bytes 2621440 | tf_op jit(solution)/shard_map/all_to_all | solution.py:474
  56.3 10.1 %collective-permute-done.8.refs_3_ = bf16[8,144,128]{2,1,0:T(8,128)(2,1)S(1)} collective-permute-done((bf16[8,144,128]{2,1,0:T(8,128)(2,1)S(1)}, bf16[8,144,128]{2,1,0:T(8,128)(2,1)S(1)}, u32[]{:S(2)}, u32[]{:S(2)}) %collective-permute-start.8) | collective-permute-done | bytes 294944 | tf_op jit(solution)/shard_map/ppermute | solution.py:532
  66.4 4.2 %collective-permute-done.6.refs_1_ = bf16[8,144,128]{2,1,0:T(8,128)(2,1)S(1)} collective-permute-done((bf16[8,144,128]{2,1,0:T(8,128)(2,1)S(1)}, bf16[8,144,128]{2,1,0:T(8,128)(2,1)S(1)}, u32[]{:S(2)}, u32[]{:S(2)}) %collective-permute-start.6) | collective-permute-done | bytes 294944 | tf_op jit(solution)/shard_map/ppermute | solution.py:532
  72.8 5.5 %all-to-all-start.1 = ((bf16[64,144,128]{2,1,0:T(8,128)(2,1)}), bf16[64,144,128]{2,1,0:T(8,128)(2,1)}, u32[]{:S(2)}, u32[]{:S(2)}) async-start(bf16[64,144,128]{2,1,0:T(8,128)(2,1)} %copy-done.18), calls=%async_computation.1 | async-start | bytes 4718592 | tf_op jit(solution)/shard_map/all_to_all | solution.py:474
  82.5 4.0 %spread_1.1 = (f32[2,64,2048]{2,1,0:T(8,128)S(1)}, bf16[2,64,2048]{2,1,0:T(8,128)(2,1)S(1)}) custom-call(s32[32]{0:T(128)S(1)} %get-tuple-element.102.position, s32[32]{0:T(128)S(1)} %reshape.245.listed, s32[2,2048]{1,0:T(2,128)S(1)} %copy-done.23, bf16[2,64,2048]{2,1,0:T(8,128)(2,1)S(1)} %bitcast.60, bf16[2,32,64,128]{3,2,1,0:T(8,128)(2,1)S(1)} %bitcast.55, ...), custom_call_target="tpu_custom_call" | custom-call | flops 603979776 | bytes 5000000 | tf_op jit(solution)/shard_map/spread_1/pallas_call | solution.py:446
  88.3 2.3 collective-permute-start.14
  90.6 4.2 %collective-permute-start.13 = (bf16[64,2048]{1,0:T(8,128)(2,1)}, bf16[64,2048]{1,0:T(8,128)(2,1)}, u32[]{:S(2)}, u32[]{:S(2)}) collective-permute-start(bf16[64,2048]{1,0:T(8,128)(2,1)} %get-tuple-element.96), channel_id=1, source_target_pairs={{0,1},{1,2},{2,3},{3,4},{4,5},{5,6},{6,7},{7,8},{8,9},{9,10},{10,1... | collective-permute-start | bytes 786440 | tf_op jit(solution)/shard_map/ppermute | solution.py:468
  94.8 12.0 %all-to-all-done.1 = bf16[64,144,128]{2,1,0:T(8,128)(2,1)} async-done(((bf16[64,144,128]{2,1,0:T(8,128)(2,1)}), bf16[64,144,128]{2,1,0:T(8,128)(2,1)}, u32[]{:S(2)}, u32[]{:S(2)}) %all-to-all-start.1) | async-done | bytes 2359328 | tf_op jit(solution)/shard_map/all_to_all | solution.py:474
  107.9 3.2 %conv_0.1.hidden.middle = bf16[2,64,2048]{2,1,0:T(8,128)(2,1)S(1)} custom-call(s32[32]{0:T(128)S(1)} %get-tuple-element.102.position, s32[32]{0:T(128)S(1)} %reshape.245.listed, s32[2,2048]{1,0:T(2,128)S(1)} %copy-done.23, bf16[2,64,2048]{2,1,0:T(8,128)(2,1)S(1)} %bitcast.59, bf16[3,4,64,2048]{3,2,1,0:T(8,128)(2,1)S(1)} %shift_0.1.shifts, ...), custom_call_target="tpu_custom_call" | custom-call | flops 603979776 | bytes 5000000 | tf_op jit(solution)/shard_map/conv_0/pallas_call | solution.py:299
  111.2 3.8 %collective-permute-start.10 = (bf16[64,2048]{1,0:T(8,128)(2,1)S(1)}, bf16[64,2048]{1,0:T(8,128)(2,1)S(1)}, u32[]{:S(2)}, u32[]{:S(2)}) collective-permute-start(bf16[64,2048]{1,0:T(8,128)(2,1)S(1)} %get-tuple-element.97), channel_id=1, source_target_pairs={{1,0},{2,1},{3,2},{4,3},{5,4},{6,5},{7,6},{8,7},{9,8},{10,9},{11,1... | collective-permute-start | bytes 786440 | tf_op jit(solution)/shard_map/ppermute | solution.py:469
  115.0 4.9 %collective-permute-start.9 = (bf16[64,2048]{1,0:T(8,128)(2,1)S(1)}, bf16[64,2048]{1,0:T(8,128)(2,1)S(1)}, u32[]{:S(2)}, u32[]{:S(2)}) collective-permute-start(bf16[64,2048]{1,0:T(8,128)(2,1)S(1)} %get-tuple-element.98), channel_id=1, source_target_pairs={{0,1},{1,2},{2,3},{3,4},{4,5},{5,6},{6,7},{7,8},{8,9},{9,10},{10,1... | collective-permute-start | bytes 786440 | tf_op jit(solution)/shard_map/ppermute | solution.py:468
  119.9 3.2 %carried_partial_0.1 = (bf16[2,64,2048]{2,1,0:T(8,128)(2,1)S(1)}, bf16[32,288,128]{2,1,0:T(8,128)(2,1)S(1)}) custom-call(s32[32]{0:T(128)S(1)} %copy-done.34, s32[32]{0:T(128)S(1)} %reshape.245.listed, s32[2,2048]{1,0:T(2,128)S(1)} %copy-done.23, bf16[2,64,2048]{2,1,0:T(8,128)(2,1)S(1)} %bitcast.62, bf16[2,64,2048]{2,1,0:T(8,128)(2,1)S(1)} %conv_0.1.hidden.middle, ...), custom_call_target="tpu_custom_call" | custom-call | flops 603979776 | bytes 7000000 | tf_op jit(solution)/shard_map/carried_partial_0/pallas_call | solution.py:388
  126.8 4.3 %all-to-all-start.5 = ((bf16[32,288,128]{2,1,0:T(8,128)(2,1)}), bf16[32,288,128]{2,1,0:T(8,128)(2,1)}, u32[]{:S(2)}, u32[]{:S(2)}) async-start(bf16[32,288,128]{2,1,0:T(8,128)(2,1)} %copy-done.17), calls=%async_computation.5 | async-start | bytes 4718592 | tf_op jit(solution)/shard_map/all_to_all | solution.py:474
  131.1 6.5 %spread_0.1 = (f32[2,64,2048]{2,1,0:T(8,128)}, bf16[2,64,2048]{2,1,0:T(8,128)(2,1)}) custom-call(s32[32]{0:T(128)} %copy-done.31, s32[32]{0:T(128)} %copy-done.29, s32[2,2048]{1,0:T(2,128)} %regions.11, bf16[2,64,2048]{2,1,0:T(8,128)(2,1)} %copy-done.19, bf16[2,32,144,128]{3,2,1,0:T(8,128)(2,1)} %bitcast.10.rest_0_), custom_call_target="tpu_custom_call" | custom-call | flops 603979776 | bytes 5000000 | tf_op jit(solution)/shard_map/spread_0/pallas_call | solution.py:446
  138.7 1.9 collective-permute-start.16
  140.6 4.7 %collective-permute-start.15 = (bf16[64,2048]{1,0:T(8,128)(2,1)S(1)}, bf16[64,2048]{1,0:T(8,128)(2,1)S(1)}, u32[]{:S(2)}, u32[]{:S(2)}) collective-permute-start(bf16[64,2048]{1,0:T(8,128)(2,1)S(1)} %get-tuple-element.94), channel_id=1, source_target_pairs={{0,1},{1,2},{2,3},{3,4},{4,5},{5,6},{6,7},{7,8},{8,9},{9,10},{10,1... | collective-permute-start | bytes 786440 | tf_op jit(solution)/shard_map/ppermute | solution.py:468
  145.3 6.3 %partial_1.1 = (bf16[32,288,128]{2,1,0:T(8,128)(2,1)}, bf16[3,4,64,2048]{3,2,1,0:T(8,128)(2,1)}) custom-call(s32[32]{0:T(128)} %copy-done.33, s32[32]{0:T(128)} %copy-done.29, s32[2,2048]{1,0:T(2,128)} %regions.11, bf16[2,64,2048]{2,1,0:T(8,128)(2,1)} %bitcast.61, bf16[64,2048]{1,0:T(8,128)(2,1)} %copy-done.44, bf16[2,64,2048]{2,1,0:T(8,128)(2,1)} %copy-done.7, ...), custom_call_target="tpu_custom_call" | custom-call | flops 603979776 | bytes 8000000 | tf_op jit(solution)/shard_map/partial_1/pallas_call | solution.py:345
  151.6 35.0 %collective-permute-done.16 = bf16[64,2048]{1,0:T(8,128)(2,1)S(1)} collective-permute-done((bf16[64,2048]{1,0:T(8,128)(2,1)S(1)}, bf16[64,2048]{1,0:T(8,128)(2,1)S(1)}, u32[]{:S(2)}, u32[]{:S(2)}) %collective-permute-start.16) | collective-permute-done | bytes 262176 | tf_op jit(solution)/shard_map/ppermute | solution.py:469
  186.6 4.9 %all-to-all-start.4 = ((bf16[32,288,128]{2,1,0:T(8,128)(2,1)}), bf16[32,288,128]{2,1,0:T(8,128)(2,1)}, u32[]{:S(2)}, u32[]{:S(2)}) async-start(bf16[32,288,128]{2,1,0:T(8,128)(2,1)} %get-tuple-element.79), calls=%async_computation.4 | async-start | bytes 4718592 | tf_op jit(solution)/shard_map/all_to_all | solution.py:474
  192.5 1.9 copy-done.16
  194.4 2.0 conv_1.1
  199.7 4.3 %total_0.1.rest_0_ = f32[2,8,36864]{2,1,0:T(8,128)} custom-call(s32[32]{0:T(128)S(1)} %reshape.254.requested, bf16[32,288,128]{2,1,0:T(8,128)(2,1)} %all-to-all-done.5.parts), custom_call_target="tpu_custom_call" | custom-call | flops 1000000 | bytes 3538944 | tf_op jit(solution)/shard_map/total_0/pallas_call | solution.py:172
  204.1 40.6 %all-to-all-done.4.parts = bf16[32,288,128]{2,1,0:T(8,128)(2,1)} async-done(((bf16[32,288,128]{2,1,0:T(8,128)(2,1)}), bf16[32,288,128]{2,1,0:T(8,128)(2,1)}, u32[]{:S(2)}, u32[]{:S(2)}) %all-to-all-start.4) | async-done | bytes 2359328 | tf_op jit(solution)/shard_map/all_to_all | solution.py:474
  244.7 4.3 %total_1.1 = f32[2,8,36864]{2,1,0:T(8,128)} custom-call(s32[32]{0:T(128)S(1)} %reshape.254.requested, bf16[32,288,128]{2,1,0:T(8,128)(2,1)} %all-to-all-done.4.parts, f32[2,8,36864]{2,1,0:T(8,128)} %total_0.1.rest_0_), custom_call_target="tpu_custom_call", output_to_operand_aliasing={{}: (2, {})} | custom-call | flops 1000000 | bytes 3538944 | tf_op jit(solution)/shard_map/total_1/pallas_call | solution.py:172
  (159 shorter events, 39.0 us)
Async XLA Ops:
  1.9 23.8 %copy-start.13 = (bf16[2,8,36864]{2,1,0:T(8,128)(2,1)S(1)}, bf16[2,8,36864]{2,1,0:T(8,128)(2,1)}, u32[]{:S(2)}) copy-start(bf16[2,8,36864]{2,1,0:T(8,128)(2,1)} %banks.3) | copy-start | bytes 3538948
  3.1 25.4 %collective-permute-start.2 = (bf16[8,64,128]{2,1,0:T(8,128)(2,1)S(1)}, bf16[8,64,128]{2,1,0:T(8,128)(2,1)S(1)}, u32[]{:S(2)}, u32[]{:S(2)}) collective-permute-start(bf16[8,64,128]{2,1,0:T(8,128)(2,1)S(1)} %get-tuple-element.62.refs_0_), channel_id=1, source_target_pairs={{0,12},{4,0},{8,4},{12,8},{1,13},{5,1},{9,5},{13,9},{2,14},{6,2},{... | collective-permute-start | bytes 393224 | tf_op jit(solution)/shard_map/ppermute | solution.py:532
  3.3 25.2 %collective-permute-start.1 = (bf16[8,64,128]{2,1,0:T(8,128)(2,1)S(1)}, bf16[8,64,128]{2,1,0:T(8,128)(2,1)S(1)}, u32[]{:S(2)}, u32[]{:S(2)}) collective-permute-start(bf16[8,64,128]{2,1,0:T(8,128)(2,1)S(1)} %get-tuple-element.62.refs_0_), channel_id=1, source_target_pairs={{0,8},{4,12},{8,0},{12,4},{1,9},{5,13},{9,1},{13,5},{2,10},{6,14},... | collective-permute-start | bytes 393224 | tf_op jit(solution)/shard_map/ppermute | solution.py:532
  5.6 22.9 %collective-permute-start = (bf16[8,64,128]{2,1,0:T(8,128)(2,1)S(1)}, bf16[8,64,128]{2,1,0:T(8,128)(2,1)S(1)}, u32[]{:S(2)}, u32[]{:S(2)}) collective-permute-start(bf16[8,64,128]{2,1,0:T(8,128)(2,1)S(1)} %get-tuple-element.62.refs_0_), channel_id=1, source_target_pairs={{0,4},{4,8},{8,12},{12,0},{1,5},{5,9},{9,13},{13,1},{2,6},{6,10},{... | collective-permute-start | bytes 393224 | tf_op jit(solution)/shard_map/ppermute | solution.py:532
  9.7 23.0 %copy-start.33 = (s32[32]{0:T(128)}, s32[32]{0:T(128)S(1)}, u32[]{:S(2)}) copy-start(s32[32]{0:T(128)S(1)} %get-tuple-element.101.position) | copy-start | bytes 388
  9.7 97.1 %copy-start.31 = (s32[32]{0:T(128)}, s32[32]{0:T(128)S(1)}, u32[]{:S(2)}) copy-start(s32[32]{0:T(128)S(1)} %get-tuple-element.102.position) | copy-start | bytes 388
  10.8 16.2 %all-to-all-start = ((s32[32,1,8]{2,1,0:T(1,128)}), s32[32,1,8]{2,1,0:T(1,128)S(1)}, u32[]{:S(2)}, u32[]{:S(2)}) async-start(s32[32,1,8]{2,1,0:T(1,128)} %copy.44), calls=%async_computation | async-start | bytes 32768 | tf_op jit(solution)/shard_map/all_to_all | solution.py:474
  19.1 18.2 %collective-permute-start.5 = (bf16[64,2048]{1,0:T(8,128)(2,1)}, bf16[64,2048]{1,0:T(8,128)(2,1)S(1)}, u32[]{:S(2)}, u32[]{:S(2)}) collective-permute-start(bf16[64,2048]{1,0:T(8,128)(2,1)} %get-tuple-element.99), channel_id=1, source_target_pairs={{1,0},{2,1},{3,2},{4,3},{5,4},{6,5},{7,6},{8,7},{9,8},{10,9},{11,1... | collective-permute-start | bytes 786440 | tf_op jit(solution)/shard_map/ppermute | solution.py:469
  21.4 16.0 %collective-permute-start.4 = (bf16[64,2048]{1,0:T(8,128)(2,1)}, bf16[64,2048]{1,0:T(8,128)(2,1)S(1)}, u32[]{:S(2)}, u32[]{:S(2)}) collective-permute-start(bf16[64,2048]{1,0:T(8,128)(2,1)} %get-tuple-element.100), channel_id=1, source_target_pairs={{0,1},{1,2},{2,3},{3,4},{4,5},{5,6},{6,7},{7,8},{8,9},{9,10},{10,1... | collective-permute-start | bytes 786440 | tf_op jit(solution)/shard_map/ppermute | solution.py:468
  28.5 17.9 %collective-permute-start.12 = (bf16[8,80,128]{2,1,0:T(8,128)(2,1)S(1)}, bf16[8,80,128]{2,1,0:T(8,128)(2,1)S(1)}, u32[]{:S(2)}, u32[]{:S(2)}) collective-permute-start(bf16[8,80,128]{2,1,0:T(8,128)(2,1)S(1)} %get-tuple-element.56.refs_0_), channel_id=1, source_target_pairs={{0,8},{4,12},{8,0},{12,4},{1,9},{5,13},{9,1},{13,5},{2,10},{6,14},... | collective-permute-start | bytes 491528 | tf_op jit(solution)/shard_map/ppermute | solution.py:532
  28.6 17.8 %collective-permute-start.11 = (bf16[8,80,128]{2,1,0:T(8,128)(2,1)S(1)}, bf16[8,80,128]{2,1,0:T(8,128)(2,1)}, u32[]{:S(2)}, u32[]{:S(2)}) collective-permute-start(bf16[8,80,128]{2,1,0:T(8,128)(2,1)S(1)} %get-tuple-element.56.refs_0_), channel_id=1, source_target_pairs={{0,4},{4,8},{8,12},{12,0},{1,5},{5,9},{9,13},{13,1},{2,6},{6,10},{... | collective-permute-start | bytes 491528 | tf_op jit(solution)/shard_map/ppermute | solution.py:532
  30.1 14.0 %collective-permute-start.3 = (bf16[8,80,128]{2,1,0:T(8,128)(2,1)S(1)}, bf16[8,80,128]{2,1,0:T(8,128)(2,1)S(1)}, u32[]{:S(2)}, u32[]{:S(2)}) collective-permute-start(bf16[8,80,128]{2,1,0:T(8,128)(2,1)S(1)} %get-tuple-element.56.refs_0_), channel_id=1, source_target_pairs={{0,12},{4,0},{8,4},{12,8},{1,13},{5,1},{9,5},{13,9},{2,14},{6,2},{... | collective-permute-start | bytes 491528 | tf_op jit(solution)/shard_map/ppermute | solution.py:532
  32.7 18.1 %all-to-all-start.2 = ((bf16[64,64,128]{2,1,0:T(8,128)(2,1)}), bf16[64,64,128]{2,1,0:T(8,128)(2,1)S(1)}, u32[]{:S(2)}, u32[]{:S(2)}) async-start(bf16[64,64,128]{2,1,0:T(8,128)(2,1)} %pack_1a.1), calls=%async_computation.2 | async-start | bytes 2097152 | tf_op jit(solution)/shard_map/all_to_all | solution.py:474
  37.3 12.2 %copy-start.25 = (bf16[64,2048]{1,0:T(8,128)(2,1)}, bf16[64,2048]{1,0:T(8,128)(2,1)S(1)}, u32[]{:S(2)}) copy-start(bf16[64,2048]{1,0:T(8,128)(2,1)S(1)} %collective-permute-done.5.below) | copy-start | bytes 786436
  37.3 12.2 %copy-start.27 = (bf16[64,2048]{1,0:T(8,128)(2,1)}, bf16[64,2048]{1,0:T(8,128)(2,1)S(1)}, u32[]{:S(2)}) copy-start(bf16[64,2048]{1,0:T(8,128)(2,1)S(1)} %collective-permute-done.4.above) | copy-start | bytes 786436
  44.8 21.7 %collective-permute-start.8 = (bf16[8,144,128]{2,1,0:T(8,128)(2,1)S(1)}, bf16[8,144,128]{2,1,0:T(8,128)(2,1)S(1)}, u32[]{:S(2)}, u32[]{:S(2)}) collective-permute-start(bf16[8,144,128]{2,1,0:T(8,128)(2,1)S(1)} %wire_0.1.refs_0_), channel_id=1, source_target_pairs={{0,12},{4,0},{8,4},{12,8},{1,13},{5,1},{9,5},{13,9},{2,14},{6,2},{... | collective-permute-start | bytes 884744 | tf_op jit(solution)/shard_map/ppermute | solution.py:532
  44.8 21.7 %collective-permute-start.7 = (bf16[8,144,128]{2,1,0:T(8,128)(2,1)S(1)}, bf16[8,144,128]{2,1,0:T(8,128)(2,1)S(1)}, u32[]{:S(2)}, u32[]{:S(2)}) collective-permute-start(bf16[8,144,128]{2,1,0:T(8,128)(2,1)S(1)} %wire_0.1.refs_0_), channel_id=1, source_target_pairs={{0,8},{4,12},{8,0},{12,4},{1,9},{5,13},{9,1},{13,5},{2,10},{6,14},... | collective-permute-start | bytes 884744 | tf_op jit(solution)/shard_map/ppermute | solution.py:532
  45.2 25.4 %collective-permute-start.6 = (bf16[8,144,128]{2,1,0:T(8,128)(2,1)S(1)}, bf16[8,144,128]{2,1,0:T(8,128)(2,1)S(1)}, u32[]{:S(2)}, u32[]{:S(2)}) collective-permute-start(bf16[8,144,128]{2,1,0:T(8,128)(2,1)S(1)} %wire_0.1.refs_0_), channel_id=1, source_target_pairs={{0,4},{4,8},{8,12},{12,0},{1,5},{5,9},{9,13},{13,1},{2,6},{6,10},{... | collective-permute-start | bytes 884744 | tf_op jit(solution)/shard_map/ppermute | solution.py:532
  51.8 21.0 %all-to-all-start.3 = ((bf16[64,80,128]{2,1,0:T(8,128)(2,1)}), bf16[64,80,128]{2,1,0:T(8,128)(2,1)S(1)}, u32[]{:S(2)}, u32[]{:S(2)}) async-start(bf16[64,80,128]{2,1,0:T(8,128)(2,1)} %pack_1b.1), calls=%async_computation.3 | async-start | bytes 2621440 | tf_op jit(solution)/shard_map/all_to_all | solution.py:474
  72.8 34.0 %all-to-all-start.1 = ((bf16[64,144,128]{2,1,0:T(8,128)(2,1)}), bf16[64,144,128]{2,1,0:T(8,128)(2,1)}, u32[]{:S(2)}, u32[]{:S(2)}) async-start(bf16[64,144,128]{2,1,0:T(8,128)(2,1)} %copy-done.18), calls=%async_computation.1 | async-start | bytes 4718592 | tf_op jit(solution)/shard_map/all_to_all | solution.py:474
  78.5 41.4 %copy-start.29 = (s32[32]{0:T(128)}, s32[32]{0:T(128)S(1)}, u32[]{:S(2)}) copy-start(s32[32]{0:T(128)S(1)} %reshape.245.listed) | copy-start | bytes 388
  88.3 31.6 %collective-permute-start.14 = (bf16[64,2048]{1,0:T(8,128)(2,1)}, bf16[64,2048]{1,0:T(8,128)(2,1)S(1)}, u32[]{:S(2)}, u32[]{:S(2)}) collective-permute-start(bf16[64,2048]{1,0:T(8,128)(2,1)} %get-tuple-element.95), channel_id=1, source_target_pairs={{1,0},{2,1},{3,2},{4,3},{5,4},{6,5},{7,6},{8,7},{9,8},{10,9},{11,1... | collective-permute-start | bytes 786440 | tf_op jit(solution)/shard_map/ppermute | solution.py:469
  90.6 29.3 %collective-permute-start.13 = (bf16[64,2048]{1,0:T(8,128)(2,1)}, bf16[64,2048]{1,0:T(8,128)(2,1)}, u32[]{:S(2)}, u32[]{:S(2)}) collective-permute-start(bf16[64,2048]{1,0:T(8,128)(2,1)} %get-tuple-element.96), channel_id=1, source_target_pairs={{0,1},{1,2},{2,3},{3,4},{4,5},{5,6},{6,7},{7,8},{8,9},{9,10},{10,1... | collective-permute-start | bytes 786440 | tf_op jit(solution)/shard_map/ppermute | solution.py:468
  107.8 12.1 %copy-start.15 = (bf16[64,2,2048]{2,0,1:T(8,128)(2,1)S(1)}, bf16[64,2,2048]{2,0,1:T(8,128)(2,1)}, u32[]{:S(2)}) copy-start(bf16[64,2,2048]{2,0,1:T(8,128)(2,1)} %copy-done.14) | copy-start | bytes 1572868
  107.8 12.1 %copy-start.22 = (f32[2,64,2048]{2,1,0:T(8,128)S(1)}, f32[2,64,2048]{2,1,0:T(8,128)}, u32[]{:S(2)}) copy-start(f32[2,64,2048]{2,1,0:T(8,128)} %copy-done.21) | copy-start | bytes 3145732
  107.8 12.1 %copy-start.34 = (s32[32]{0:T(128)S(1)}, s32[32]{0:T(128)}, u32[]{:S(2)}) copy-start(s32[32]{0:T(128)} %copy-done.33) | copy-start | bytes 388
  111.2 14.2 %collective-permute-start.10 = (bf16[64,2048]{1,0:T(8,128)(2,1)S(1)}, bf16[64,2048]{1,0:T(8,128)(2,1)S(1)}, u32[]{:S(2)}, u32[]{:S(2)}) collective-permute-start(bf16[64,2048]{1,0:T(8,128)(2,1)S(1)} %get-tuple-element.97), channel_id=1, source_target_pairs={{1,0},{2,1},{3,2},{4,3},{5,4},{6,5},{7,6},{8,7},{9,8},{10,9},{11,1... | collective-permute-start | bytes 786440 | tf_op jit(solution)/shard_map/ppermute | solution.py:469
  115.0 10.3 %collective-permute-start.9 = (bf16[64,2048]{1,0:T(8,128)(2,1)S(1)}, bf16[64,2048]{1,0:T(8,128)(2,1)S(1)}, u32[]{:S(2)}, u32[]{:S(2)}) collective-permute-start(bf16[64,2048]{1,0:T(8,128)(2,1)S(1)} %get-tuple-element.98), channel_id=1, source_target_pairs={{0,1},{1,2},{2,3},{3,4},{4,5},{5,6},{6,7},{7,8},{8,9},{9,10},{10,1... | collective-permute-start | bytes 786440 | tf_op jit(solution)/shard_map/ppermute | solution.py:468
  126.8 59.9 %all-to-all-start.5 = ((bf16[32,288,128]{2,1,0:T(8,128)(2,1)}), bf16[32,288,128]{2,1,0:T(8,128)(2,1)}, u32[]{:S(2)}, u32[]{:S(2)}) async-start(bf16[32,288,128]{2,1,0:T(8,128)(2,1)} %copy-done.17), calls=%async_computation.5 | async-start | bytes 4718592 | tf_op jit(solution)/shard_map/all_to_all | solution.py:474
  138.7 47.9 %collective-permute-start.16 = (bf16[64,2048]{1,0:T(8,128)(2,1)S(1)}, bf16[64,2048]{1,0:T(8,128)(2,1)S(1)}, u32[]{:S(2)}, u32[]{:S(2)}) collective-permute-start(bf16[64,2048]{1,0:T(8,128)(2,1)S(1)} %get-tuple-element.93), channel_id=1, source_target_pairs={{1,0},{2,1},{3,2},{4,3},{5,4},{6,5},{7,6},{8,7},{9,8},{10,9},{11,1... | collective-permute-start | bytes 786440 | tf_op jit(solution)/shard_map/ppermute | solution.py:469
  140.6 46.0 %collective-permute-start.15 = (bf16[64,2048]{1,0:T(8,128)(2,1)S(1)}, bf16[64,2048]{1,0:T(8,128)(2,1)S(1)}, u32[]{:S(2)}, u32[]{:S(2)}) collective-permute-start(bf16[64,2048]{1,0:T(8,128)(2,1)S(1)} %get-tuple-element.94), channel_id=1, source_target_pairs={{0,1},{1,2},{2,3},{3,4},{4,5},{5,6},{6,7},{7,8},{8,9},{9,10},{10,1... | collective-permute-start | bytes 786440 | tf_op jit(solution)/shard_map/ppermute | solution.py:468
  186.6 58.1 %all-to-all-start.4 = ((bf16[32,288,128]{2,1,0:T(8,128)(2,1)}), bf16[32,288,128]{2,1,0:T(8,128)(2,1)}, u32[]{:S(2)}, u32[]{:S(2)}) async-start(bf16[32,288,128]{2,1,0:T(8,128)(2,1)} %get-tuple-element.79), calls=%async_computation.4 | async-start | bytes 4718592 | tf_op jit(solution)/shard_map/all_to_all | solution.py:474
  (36 other events, 113.1 us)
